TPU v7x, 32 devices: a whole 2x2x4 slice. The times are simulated.
32 devices in a mesh: gx: 8 (over z, x), gy: 4 (over y, core).
Axes of the slice: x: 2, y: 2, z: 4, core: 2. Of those that a mesh axis runs over, the one named last changes fastest.
Arguments:
- velocity: float32 [1, 2048, 2048], P(None, 'gx', 'gy'), may hold values from -6 to 6
Outputs:
- du_dx: float32 [1, 2048, 2048], P(None, 'gx', 'gy')
- du_dy: float32 [1, 2048, 2048], P(None, 'gx', 'gy')
- d2u_dx2: float32 [1, 2048, 2048], P(None, 'gx', 'gy')
- d2u_dy2: float32 [1, 2048, 2048], P(None, 'gx', 'gy')
All inputs are finite; a program needn't handle non-finite values.
Results may differ from a plain program's by a relative error of at most 0.00007.
Values sent between devices are 32-bit elements; how exact they have to be, the bound alone decides.
No kernel may reach another device: no remote copies, remote signals or barrier semaphores. Data moves between devices by JAX's collectives and lax.ppermute only.
A program may use at most 64 MiB of HBM per device.

v0:
```python
import jax
import jax.numpy as jnp
from jax import lax
from jax.sharding import PartitionSpec as P

FIRST_NEAR = 7.0 / 9.0
FIRST_FAR = 1.0 / 36.0
SECOND_NEAR = 12.0 / 11.0
SECOND_FAR = 3.0 / 44.0
COUPLINGS = (1.0 / 3.0, 2.0 / 11.0)
HIGHEST = lax.Precision.HIGHEST
window_margin = 24


def with_halo(block, sides, width):
    for axis, dim in sides:
        count = lax.axis_size(axis)
        forward = [(i, i + 1) for i in range(count - 1)]
        forward.append((count - 1, 0))
        backward = [(target, source) for source, target in forward]
        low = lax.ppermute(
            lax.slice_in_dim(block, block.shape[dim] - width, None, axis=dim), axis, forward
        )
        high = lax.ppermute(lax.slice_in_dim(block, 0, width, axis=dim), axis, backward)
        block = jnp.concatenate([low, block, high], axis=dim)
    return block


def stencils(shifted):
    minus_two, minus_one, centre, plus_one, plus_two = shifted
    first_order = FIRST_NEAR * (plus_one - minus_one) + FIRST_FAR * (plus_two - minus_two)
    second_order = SECOND_NEAR * (plus_one - 2.0 * centre + minus_one) + SECOND_FAR * (
        plus_two - 2.0 * centre + minus_two
    )
    return jnp.stack([first_order, second_order])


def window_rows(coupling, block):
    length = block + 2 * window_margin
    coupled = jnp.full((length - 1,), coupling, jnp.float32)
    zero_entry = jnp.zeros((1,), jnp.float32)
    lower = jnp.concatenate([zero_entry, coupled])
    upper = jnp.concatenate([coupled, zero_entry])
    diagonal = jnp.ones((length,), jnp.float32)
    inverse = lax.linalg.tridiagonal_solve(
        lower, diagonal, upper, jnp.eye(length, dtype=jnp.float32)
    )
    return inverse[window_margin : window_margin + block]


def window_stack(block):
    return jnp.stack([window_rows(coupling, block) for coupling in COUPLINGS])


def local(velocity):
    cells_x = velocity.shape[1]
    cells_y = velocity.shape[2]
    matrices_x = window_stack(cells_x)
    matrices_y = window_stack(cells_y)
    width = window_margin + 2
    padded = with_halo(velocity, (("gx", 1), ("gy", 2)), width)
    span_x = cells_x + 2 * window_margin
    span_y = cells_y + 2 * window_margin
    along_rows = [padded[:, k : k + span_x, width : width + cells_y] for k in range(5)]
    along_columns = [padded[:, width : width + cells_x, k : k + span_y] for k in range(5)]
    solved_x = jnp.einsum("sij,spjy->spiy", matrices_x, stencils(along_rows), precision=HIGHEST)
    solved_y = jnp.einsum("sij,spxj->spxi", matrices_y, stencils(along_columns), precision=HIGHEST)
    return (solved_x[0], solved_y[0], solved_x[1], solved_y[1])


def solution(mesh):
    placed = (P(None, "gx", "gy"),)
    return jax.shard_map(
        local,
        mesh=mesh,
        in_specs=placed,
        out_specs=(
            P(None, "gx", "gy"),
            P(None, "gx", "gy"),
            P(None, "gx", "gy"),
            P(None, "gx", "gy"),
        ),
        check_vma=False,
    )
```

profile of v0, /device:TPU:0, one launch (start us, length us, event | category | flops | bytes accessed | tf_op | source)
XLA Modules:
  0.0 1546.3 jit_solution(9537665907376650043)
XLA Ops:
  10.1 87.6 %while.132 = (s32[]{:T(128)}, f32[]{:T(128)}, f32[560]{0:T(1024)S(1)}, f32[17,32]{1,0:T(8,128)S(1)}, f32[17,32,560]{2,1,0:T(8,128)S(1)}, /*index=5*/f32[17,32,56...) while((s32[]{:T(128)}, f32[]{:T(128)}, ...), condition=%wide.region_9.10_spmd, body=%wide.region_8.9_spmd.sunk | while | flops 53889 | bytes 742173 | solution.py:45
  112.1 435.2 %while.133 = (s32[]{:T(128)}, f32[560]{0:T(1024)S(1)}, f32[17,32,560]{2,1,0:T(8,128)}, f32[17,32,560]{2,1,0:T(8,128)}, f32[17,32]{1,0:T(8,128)S(1)}, /*index=5*/...) while((s32[]{:T(128)}, f32[560]{0:T(1024)S(1)}, ...), condition=%wide.region_11.12_spmd, body=%wide.region_10.11_spmd.sunk | while | flops 35874 | bytes 730777 | solution.py:45
  547.5 87.6 %while.134 = (s32[]{:T(128)}, f32[]{:T(128)}, f32[560]{0:T(1024)S(1)}, f32[17,32]{1,0:T(8,128)S(1)}, f32[17,32,560]{2,1,0:T(8,128)S(1)}, /*index=5*/f32[17,32,56...) while((s32[]{:T(128)}, f32[]{:T(128)}, ...), condition=%wide.region_13.14_spmd, body=%wide.region_12.13_spmd.sunk | while | flops 53889 | bytes 742173 | solution.py:45
  646.8 419.2 %while.135 = (s32[]{:T(128)}, f32[560]{0:T(1024)S(1)}, f32[17,32,560]{2,1,0:T(8,128)S(1)}, f32[17,32,560]{2,1,0:T(8,128)}, f32[17,32]{1,0:T(8,128)S(1)}, /*index...) while((s32[]{:T(128)}, f32[560]{0:T(1024)S(1)}, ...), condition=%wide.region_15.16_spmd, body=%wide.region_14.15_spmd.sunk | while | flops 35874 | bytes 741017 | solution.py:45
  1066.2 24.0 %while.128 = (s32[]{:T(128)}, f32[]{:T(128)}, f32[304]{0:T(512)S(1)}, f32[9,32]{1,0:T(8,128)S(1)}, f32[9,32,304]{2,1,0:T(8,128)S(1)}, /*index=5*/f32[9,32,304]{2...) while((s32[]{:T(128)}, f32[]{:T(128)}, ...), condition=%wide.region_1.2_spmd, body=%wide.region_0.1_spmd.sunk | while | flops 29313 | bytes 413469 | solution.py:45
  1092.6 207.5 %while.129 = (s32[]{:T(128)}, f32[304]{0:T(512)S(1)}, f32[9,32,304]{2,1,0:T(8,128)}, f32[9,32,304]{2,1,0:T(8,128)S(1)}, f32[9,32]{1,0:T(8,128)S(1)}, /*index=5*/...) while((s32[]{:T(128)}, f32[304]{0:T(512)S(1)}, ...), condition=%wide.region_3.4_spmd, body=%wide.region_2.3_spmd.sunk | while | flops 19490 | bytes 402073 | solution.py:45
  1094.3 20.2 %multiply_subtract_fusion.256 = (f32[304]{0:T(512)S(1)}, f32[304]{0:T(512)S(1)}, f32[304]{0:T(512)S(1)}, f32[304]{0:T(512)S(1)}, f32[304]{0:T(512)S(1)}, /*index...) fusion(f32[304]{0:T(512)S(1)} %get-tuple-element.2359, ...), kind=kLoop, calls=%fused_computation.131.clone.1 | loop fusion | flops 19456 | bytes 79168 | tf_op jit(solution)/shard_map/while/body/eval_jaxpr/sub | solution.py:45
  1117.3 20.2 %multiply_subtract_fusion.256 = (f32[304]{0:T(512)S(1)}, f32[304]{0:T(512)S(1)}, f32[304]{0:T(512)S(1)}, f32[304]{0:T(512)S(1)}, f32[304]{0:T(512)S(1)}, /*index...) fusion(f32[304]{0:T(512)S(1)} %get-tuple-element.2359, ...), kind=kLoop, calls=%fused_computation.131.clone.1 | loop fusion | flops 19456 | bytes 79168 | tf_op jit(solution)/shard_map/while/body/eval_jaxpr/sub | solution.py:45
  1140.4 20.2 %multiply_subtract_fusion.256 = (f32[304]{0:T(512)S(1)}, f32[304]{0:T(512)S(1)}, f32[304]{0:T(512)S(1)}, f32[304]{0:T(512)S(1)}, f32[304]{0:T(512)S(1)}, /*index...) fusion(f32[304]{0:T(512)S(1)} %get-tuple-element.2359, ...), kind=kLoop, calls=%fused_computation.131.clone.1 | loop fusion | flops 19456 | bytes 79168 | tf_op jit(solution)/shard_map/while/body/eval_jaxpr/sub | solution.py:45
  1163.5 20.2 %multiply_subtract_fusion.256 = (f32[304]{0:T(512)S(1)}, f32[304]{0:T(512)S(1)}, f32[304]{0:T(512)S(1)}, f32[304]{0:T(512)S(1)}, f32[304]{0:T(512)S(1)}, /*index...) fusion(f32[304]{0:T(512)S(1)} %get-tuple-element.2359, ...), kind=kLoop, calls=%fused_computation.131.clone.1 | loop fusion | flops 19456 | bytes 79168 | tf_op jit(solution)/shard_map/while/body/eval_jaxpr/sub | solution.py:45
  1186.5 20.2 %multiply_subtract_fusion.256 = (f32[304]{0:T(512)S(1)}, f32[304]{0:T(512)S(1)}, f32[304]{0:T(512)S(1)}, f32[304]{0:T(512)S(1)}, f32[304]{0:T(512)S(1)}, /*index...) fusion(f32[304]{0:T(512)S(1)} %get-tuple-element.2359, ...), kind=kLoop, calls=%fused_computation.131.clone.1 | loop fusion | flops 19456 | bytes 79168 | tf_op jit(solution)/shard_map/while/body/eval_jaxpr/sub | solution.py:45
  1209.6 20.2 %multiply_subtract_fusion.256 = (f32[304]{0:T(512)S(1)}, f32[304]{0:T(512)S(1)}, f32[304]{0:T(512)S(1)}, f32[304]{0:T(512)S(1)}, f32[304]{0:T(512)S(1)}, /*index...) fusion(f32[304]{0:T(512)S(1)} %get-tuple-element.2359, ...), kind=kLoop, calls=%fused_computation.131.clone.1 | loop fusion | flops 19456 | bytes 79168 | tf_op jit(solution)/shard_map/while/body/eval_jaxpr/sub | solution.py:45
  1232.6 20.2 %multiply_subtract_fusion.256 = (f32[304]{0:T(512)S(1)}, f32[304]{0:T(512)S(1)}, f32[304]{0:T(512)S(1)}, f32[304]{0:T(512)S(1)}, f32[304]{0:T(512)S(1)}, /*index...) fusion(f32[304]{0:T(512)S(1)} %get-tuple-element.2359, ...), kind=kLoop, calls=%fused_computation.131.clone.1 | loop fusion | flops 19456 | bytes 79168 | tf_op jit(solution)/shard_map/while/body/eval_jaxpr/sub | solution.py:45
  1255.7 20.2 %multiply_subtract_fusion.256 = (f32[304]{0:T(512)S(1)}, f32[304]{0:T(512)S(1)}, f32[304]{0:T(512)S(1)}, f32[304]{0:T(512)S(1)}, f32[304]{0:T(512)S(1)}, /*index...) fusion(f32[304]{0:T(512)S(1)} %get-tuple-element.2359, ...), kind=kLoop, calls=%fused_computation.131.clone.1 | loop fusion | flops 19456 | bytes 79168 | tf_op jit(solution)/shard_map/while/body/eval_jaxpr/sub | solution.py:45
  1278.7 20.2 %multiply_subtract_fusion.256 = (f32[304]{0:T(512)S(1)}, f32[304]{0:T(512)S(1)}, f32[304]{0:T(512)S(1)}, f32[304]{0:T(512)S(1)}, f32[304]{0:T(512)S(1)}, /*index...) fusion(f32[304]{0:T(512)S(1)} %get-tuple-element.2359, ...), kind=kLoop, calls=%fused_computation.131.clone.1 | loop fusion | flops 19456 | bytes 79168 | tf_op jit(solution)/shard_map/while/body/eval_jaxpr/sub | solution.py:45
  1300.1 24.0 %while.130 = (s32[]{:T(128)}, f32[]{:T(128)}, f32[304]{0:T(512)S(1)}, f32[9,32]{1,0:T(8,128)S(1)}, f32[9,32,304]{2,1,0:T(8,128)S(1)}, /*index=5*/f32[9,32,304]{2...) while((s32[]{:T(128)}, f32[]{:T(128)}, ...), condition=%wide.region_5.6_spmd, body=%wide.region_4.5_spmd.sunk | while | flops 29313 | bytes 413469 | solution.py:45
  1325.6 202.4 %while.131 = (s32[]{:T(128)}, f32[304]{0:T(512)S(1)}, f32[9,32,304]{2,1,0:T(8,128)S(1)}, f32[9,32,304]{2,1,0:T(8,128)S(1)}, f32[9,32]{1,0:T(8,128)S(1)}, /*index...) while((s32[]{:T(128)}, f32[304]{0:T(512)S(1)}, ...), condition=%wide.region_7.8_spmd, body=%wide.region_6.7_spmd.sunk | while | flops 19490 | bytes 412313 | solution.py:45
  1327.5 20.2 %multiply_subtract_fusion.257 = (f32[304]{0:T(512)S(1)}, f32[304]{0:T(512)S(1)}, f32[304]{0:T(512)S(1)}, f32[304]{0:T(512)S(1)}, f32[304]{0:T(512)S(1)}, /*index...) fusion(f32[304]{0:T(512)S(1)} %get-tuple-element.2530, ...), kind=kLoop, calls=%fused_computation.326.clone.1 | loop fusion | flops 19456 | bytes 79168 | tf_op jit(solution)/shard_map/while/body/eval_jaxpr/sub | solution.py:45
  1350.0 20.2 %multiply_subtract_fusion.257 = (f32[304]{0:T(512)S(1)}, f32[304]{0:T(512)S(1)}, f32[304]{0:T(512)S(1)}, f32[304]{0:T(512)S(1)}, f32[304]{0:T(512)S(1)}, /*index...) fusion(f32[304]{0:T(512)S(1)} %get-tuple-element.2530, ...), kind=kLoop, calls=%fused_computation.326.clone.1 | loop fusion | flops 19456 | bytes 79168 | tf_op jit(solution)/shard_map/while/body/eval_jaxpr/sub | solution.py:45
  1372.5 20.2 %multiply_subtract_fusion.257 = (f32[304]{0:T(512)S(1)}, f32[304]{0:T(512)S(1)}, f32[304]{0:T(512)S(1)}, f32[304]{0:T(512)S(1)}, f32[304]{0:T(512)S(1)}, /*index...) fusion(f32[304]{0:T(512)S(1)} %get-tuple-element.2530, ...), kind=kLoop, calls=%fused_computation.326.clone.1 | loop fusion | flops 19456 | bytes 79168 | tf_op jit(solution)/shard_map/while/body/eval_jaxpr/sub | solution.py:45
  1394.9 20.2 %multiply_subtract_fusion.257 = (f32[304]{0:T(512)S(1)}, f32[304]{0:T(512)S(1)}, f32[304]{0:T(512)S(1)}, f32[304]{0:T(512)S(1)}, f32[304]{0:T(512)S(1)}, /*index...) fusion(f32[304]{0:T(512)S(1)} %get-tuple-element.2530, ...), kind=kLoop, calls=%fused_computation.326.clone.1 | loop fusion | flops 19456 | bytes 79168 | tf_op jit(solution)/shard_map/while/body/eval_jaxpr/sub | solution.py:45
  1417.4 20.2 %multiply_subtract_fusion.257 = (f32[304]{0:T(512)S(1)}, f32[304]{0:T(512)S(1)}, f32[304]{0:T(512)S(1)}, f32[304]{0:T(512)S(1)}, f32[304]{0:T(512)S(1)}, /*index...) fusion(f32[304]{0:T(512)S(1)} %get-tuple-element.2530, ...), kind=kLoop, calls=%fused_computation.326.clone.1 | loop fusion | flops 19456 | bytes 79168 | tf_op jit(solution)/shard_map/while/body/eval_jaxpr/sub | solution.py:45
  1439.9 20.2 %multiply_subtract_fusion.257 = (f32[304]{0:T(512)S(1)}, f32[304]{0:T(512)S(1)}, f32[304]{0:T(512)S(1)}, f32[304]{0:T(512)S(1)}, f32[304]{0:T(512)S(1)}, /*index...) fusion(f32[304]{0:T(512)S(1)} %get-tuple-element.2530, ...), kind=kLoop, calls=%fused_computation.326.clone.1 | loop fusion | flops 19456 | bytes 79168 | tf_op jit(solution)/shard_map/while/body/eval_jaxpr/sub | solution.py:45
  1484.8 20.2 %multiply_subtract_fusion.257 = (f32[304]{0:T(512)S(1)}, f32[304]{0:T(512)S(1)}, f32[304]{0:T(512)S(1)}, f32[304]{0:T(512)S(1)}, f32[304]{0:T(512)S(1)}, /*index...) fusion(f32[304]{0:T(512)S(1)} %get-tuple-element.2530, ...), kind=kLoop, calls=%fused_computation.326.clone.1 | loop fusion | flops 19456 | bytes 79168 | tf_op jit(solution)/shard_map/while/body/eval_jaxpr/sub | solution.py:45
  (4322 shorter events, 1115.5 us)
Async XLA Ops:
  1.5 1531.2 %collective-permute-start = (f32[1,26,512]{2,1,0:T(8,128)S(1)}, f32[1,26,512]{2,1,0:T(8,128)S(1)}, u32[]{:S(2)}, u32[]{:S(2)}) collective-permute-start(f32[1,26,512]{2,1,0:T(8,128)S(1)} %get-tuple-element.1414), channel_id=1, source_target_pairs={{0,4},{4,8},{8,12},{12,16},{16,20},{20,24},{24,28},{28,0},{1,5},{5... | collective-permute-start | bytes 159752 | tf_op jit(solution)/shard_map/ppermute | solution.py:21
  4.5 1528.2 %collective-permute-start.1 = (f32[1,26,512]{2,1,0:T(8,128)S(1)}, f32[1,26,512]{2,1,0:T(8,128)S(1)}, u32[]{:S(2)}, u32[]{:S(2)}) collective-permute-start(f32[1,26,512]{2,1,0:T(8,128)S(1)} %get-tuple-element.1415), channel_id=1, source_target_pairs={{4,0},{8,4},{12,8},{16,12},{20,16},{24,20},{28,24},{0,28},{5,1},{9... | collective-permute-start | bytes 159752 | tf_op jit(solution)/shard_map/ppermute | solution.py:24
  7.8 91.0 %copy-start.6 = (f32[560]{0:T(1024)}, f32[560]{0:T(1024)S(1)}, u32[]{:S(2)}) copy-start(f32[560]{0:T(1024)S(1)} %get-tuple-element.843) | copy-start | bytes 6724
  7.8 91.0 %copy-start.8 = (f32[560]{0:T(1024)}, f32[560]{0:T(1024)S(1)}, u32[]{:S(2)}) copy-start(f32[560]{0:T(1024)S(1)} %get-tuple-element.844) | copy-start | bytes 6724
  7.9 91.0 %copy-start.10 = (f32[560]{0:T(1024)}, f32[560]{0:T(1024)S(1)}, u32[]{:S(2)}) copy-start(f32[560]{0:T(1024)S(1)} %get-tuple-element.845) | copy-start | bytes 6724
  7.9 91.0 %copy-start.12 = (f32[560]{0:T(1024)}, f32[560]{0:T(1024)S(1)}, u32[]{:S(2)}) copy-start(f32[560]{0:T(1024)S(1)} %get-tuple-element.846) | copy-start | bytes 6724
  7.9 91.0 %copy-start.14 = (f32[560]{0:T(1024)}, f32[560]{0:T(1024)S(1)}, u32[]{:S(2)}) copy-start(f32[560]{0:T(1024)S(1)} %get-tuple-element.847) | copy-start | bytes 6724
  7.9 91.0 %copy-start.16 = (f32[560]{0:T(1024)}, f32[560]{0:T(1024)S(1)}, u32[]{:S(2)}) copy-start(f32[560]{0:T(1024)S(1)} %get-tuple-element.848) | copy-start | bytes 6724
  7.9 91.0 %copy-start.18 = (f32[560]{0:T(1024)}, f32[560]{0:T(1024)S(1)}, u32[]{:S(2)}) copy-start(f32[560]{0:T(1024)S(1)} %get-tuple-element.849) | copy-start | bytes 6724
  7.9 91.0 %copy-start.20 = (f32[560]{0:T(1024)}, f32[560]{0:T(1024)S(1)}, u32[]{:S(2)}) copy-start(f32[560]{0:T(1024)S(1)} %get-tuple-element.850) | copy-start | bytes 6724
  7.9 91.0 %copy-start.22 = (f32[560]{0:T(1024)}, f32[560]{0:T(1024)S(1)}, u32[]{:S(2)}) copy-start(f32[560]{0:T(1024)S(1)} %get-tuple-element.851) | copy-start | bytes 6724
  7.9 91.0 %copy-start.24 = (f32[560]{0:T(1024)}, f32[560]{0:T(1024)S(1)}, u32[]{:S(2)}) copy-start(f32[560]{0:T(1024)S(1)} %get-tuple-element.852) | copy-start | bytes 6724
  7.9 91.0 %copy-start.26 = (f32[560]{0:T(1024)}, f32[560]{0:T(1024)S(1)}, u32[]{:S(2)}) copy-start(f32[560]{0:T(1024)S(1)} %get-tuple-element.853) | copy-start | bytes 6724
  7.9 91.0 %copy-start.28 = (f32[560]{0:T(1024)}, f32[560]{0:T(1024)S(1)}, u32[]{:S(2)}) copy-start(f32[560]{0:T(1024)S(1)} %get-tuple-element.854) | copy-start | bytes 6724
  8.0 91.0 %copy-start.30 = (f32[560]{0:T(1024)}, f32[560]{0:T(1024)S(1)}, u32[]{:S(2)}) copy-start(f32[560]{0:T(1024)S(1)} %get-tuple-element.855) | copy-start | bytes 6724
  547.4 89.0 %copy-start.7 = (f32[560]{0:T(1024)S(1)}, f32[560]{0:T(1024)}, u32[]{:S(2)}) copy-start(f32[560]{0:T(1024)} %copy-done.6) | copy-start | bytes 6724
  547.4 88.9 %copy-start.9 = (f32[560]{0:T(1024)S(1)}, f32[560]{0:T(1024)}, u32[]{:S(2)}) copy-start(f32[560]{0:T(1024)} %copy-done.8) | copy-start | bytes 6724
  547.4 88.9 %copy-start.11 = (f32[560]{0:T(1024)S(1)}, f32[560]{0:T(1024)}, u32[]{:S(2)}) copy-start(f32[560]{0:T(1024)} %copy-done.10) | copy-start | bytes 6724
  547.4 88.9 %copy-start.13 = (f32[560]{0:T(1024)S(1)}, f32[560]{0:T(1024)}, u32[]{:S(2)}) copy-start(f32[560]{0:T(1024)} %copy-done.12) | copy-start | bytes 6724
  547.4 88.9 %copy-start.15 = (f32[560]{0:T(1024)S(1)}, f32[560]{0:T(1024)}, u32[]{:S(2)}) copy-start(f32[560]{0:T(1024)} %copy-done.14) | copy-start | bytes 6724
  547.4 88.9 %copy-start.17 = (f32[560]{0:T(1024)S(1)}, f32[560]{0:T(1024)}, u32[]{:S(2)}) copy-start(f32[560]{0:T(1024)} %copy-done.16) | copy-start | bytes 6724
  547.4 88.9 %copy-start.19 = (f32[560]{0:T(1024)S(1)}, f32[560]{0:T(1024)}, u32[]{:S(2)}) copy-start(f32[560]{0:T(1024)} %copy-done.18) | copy-start | bytes 6724
  1533.4 6.7 collective-permute-start.2
  1533.4 6.6 collective-permute-start.3
  (27 other events, 928.1 us)
where the time goes:
time: 1570 us; the launch traced here: 1550 us
  other arithmetic  1060 us (68%)
  local copies, waits for them, and re-layouts  363 us (23%)
  loops' own time  103 us (7%)
    sub x52, other arithmetic, window_rows(): lax.linalg.tridiagonal_solve(lower, diagonal, upper, jnp.eye(length, dtyp...  1050 us
    slice x324, local copies, waits for them, and re-layouts, window_rows(): lax.linalg.tridiagonal_solve(lower, diagonal, upper, jnp.eye(length, dtyp...  276 us
    another operation x8, loops' own time, window_rows(): lax.linalg.tridiagonal_solve(lower, diagonal, upper, jnp.eye(length, dtyp...  103 us

commit v1 on v0

v1 whole, which is shorter than its diff:
```python
import math

import jax
import jax.numpy as jnp
import ml_dtypes
import numpy as np
from jax import lax
from jax.experimental import pallas as pl
from jax.experimental.pallas import tpu as pltpu
from jax.sharding import PartitionSpec as P

F32 = jnp.float32
BF16 = jnp.bfloat16

FIRST_IN, FIRST_OUT = 7.0 / 9.0 + 1.0 / 36.0, 1.0 / 36.0
SECOND_IN, SECOND_OUT = 12.0 / 11.0 + 3.0 / 44.0, 3.0 / 44.0

COUPLINGS = (1.0 / 3.0, 2.0 / 11.0)
RATIOS = tuple((math.sqrt(1.0 - 4.0 * a * a) - 1.0) / (2.0 * a) for a in COUPLINGS)
SCALES = tuple(1.0 / math.sqrt(1.0 - 4.0 * a * a) for a in COUPLINGS)

WINDOW = 256
TILE = 128
EDGE = 32
MESSAGE = 8

ANY = pl.BlockSpec(memory_space=pl.ANY)
VMEM = pl.BlockSpec(memory_space=pltpu.VMEM)


def inverse_parts():
    distance = np.abs(np.subtract.outer(np.arange(WINDOW), np.arange(WINDOW)))
    parts = []
    for ratio, scale in zip(RATIOS, SCALES):
        entries = scale * ratio ** distance.astype(np.float64)
        high = entries.astype(ml_dtypes.bfloat16)
        parts += [high, (entries - high.astype(np.float64)).astype(ml_dtypes.bfloat16)]
    return np.stack(parts)


def right_sides(cells, axis):
    length = cells.shape[axis]
    step = lambda a, k: pltpu.roll(a, k % length, axis)
    here = step(cells, -1) - cells
    before, after, far = step(here, 1), step(here, -1), step(here, 2)
    first = FIRST_IN * (here + before) + FIRST_OUT * (after + far)
    second = SECOND_IN * (here - before) + SECOND_OUT * (after - far)
    return first, second


def row_weights(rows, entry):
    at = lax.broadcasted_iota(jnp.int32, (rows, 1), 0)
    column = jnp.zeros((rows, 1), F32)
    for row in range(rows):
        if entry(row) != 0.0:
            column = jnp.where(at == row, F32(entry(row)), column)
    return column


def powers(ratio, exponent):
    size = jnp.exp(exponent.astype(F32) * math.log(-ratio))
    return jnp.where(exponent % 2 == 0, size, -size)


def message(strip, high):
    at = lax.broadcasted_iota(jnp.int32, (EDGE, 1), 0)
    known = (at >= 2) & (at < EDGE - 2)
    exponent = (EDGE - 3 - at) if high else (at - 2)
    tails = []
    for ratio, rhs in zip(RATIOS, right_sides(strip, 0)):
        weight = jnp.where(known, powers(ratio, exponent), 0.0)
        tails.append(jnp.sum(rhs * weight, axis=0, keepdims=True))
    near = pltpu.roll(strip[EDGE - 8 :], 4, 0) if high else strip[:8]
    row = lax.broadcasted_iota(jnp.int32, near.shape, 0)
    return jnp.where(row < 4, near, jnp.where(row == 4, tails[0], tails[1]))


def pack_kernel(u_ref, to_high_x, to_low_x, to_y, to_core, near_low, near_high, low_x, high_x, low_y, high_y, sems):
    rows, columns = u_ref.shape
    copies = [
        pltpu.make_async_copy(u_ref.at[:, pl.ds(0, TILE)], low_y, sems.at[0]),
        pltpu.make_async_copy(u_ref.at[:, pl.ds(columns - TILE, TILE)], high_y, sems.at[1]),
        pltpu.make_async_copy(u_ref.at[pl.ds(0, EDGE)], low_x, sems.at[2]),
        pltpu.make_async_copy(u_ref.at[pl.ds(rows - EDGE, EDGE)], high_x, sems.at[3]),
    ]
    for copy in copies:
        copy.start()
    even = lax.rem(lax.axis_index("gy"), 2) == 0
    copies[2].wait()
    to_low_x[...] = message(low_x[...], False)[: to_low_x.shape[0]]
    copies[3].wait()
    to_high_x[...] = message(high_x[...], True)
    copies[0].wait()
    low = low_y[...].T[:EDGE]
    copies[1].wait()
    high = high_y[...].T[TILE - EDGE :]
    near_low[...] = low[:8]
    near_high[...] = high[EDGE - 8 :]
    to_low, to_high = message(low, False), message(high, True)
    to_y[:, pl.ds(0, rows)] = jnp.where(even, to_low, to_high)[: to_y.shape[0]]
    to_core[...] = jnp.where(even, to_high, to_low)


def interior_kernel(u_ref, k_ref, dx, dy, dxx, dyy, strips_x, strips_y, high_x, rest_x, high_y, rest_y, solved_x, solved_y, sems):
    rows, columns = u_ref.shape

    def split(value, at, high, rest):
        upper = value.astype(BF16)
        high[at] = upper
        rest[at] = (value - upper.astype(F32)).astype(BF16)

    at = lax.broadcasted_iota(jnp.int32, (rows, 1), 0)
    known = (at >= 2) & (at < rows - 2)
    for j in range(columns // TILE):
        lanes = slice(j * TILE, (j + 1) * TILE)
        for s, rhs in enumerate(right_sides(u_ref[:, lanes], 0)):
            split(jnp.where(known, rhs, 0.0), (s, slice(None), lanes), high_x, rest_x)
    dot = lambda a, b: jnp.dot(a, b, preferred_element_type=F32)
    started = []

    def send(source, target):
        copy = pltpu.make_async_copy(source, target, sems.at[len(started)])
        copy.start()
        started.append(copy)

    outs_x, outs_y = (dx, dxx), (dy, dyy)
    span = min(columns, WINDOW)
    for j in range(columns // span):
        lanes = slice(j * span, (j + 1) * span)
        for s in range(2):
            upper, lower = k_ref[2 * s, :rows, :rows], k_ref[2 * s + 1, :rows, :rows]
            high, rest = high_x[s, :, lanes], rest_x[s, :, lanes]
            solved = dot(upper, high) + dot(upper, rest) + dot(lower, high)
            solved_x[s, :, lanes] = solved
            strips_x[s, 0, :, lanes] = solved[:EDGE]
            strips_x[s, 1, :, lanes] = solved[rows - EDGE :]
    if rows > 2 * EDGE:
        inner = pl.ds(EDGE, rows - 2 * EDGE)
        for s in range(2):
            send(solved_x.at[s, inner], outs_x[s].at[inner])

    at = lax.broadcasted_iota(jnp.int32, (1, columns), 1)
    known = (at >= 2) & (at < columns - 2)
    step = min(rows, 64)
    for i in range(rows // step):
        lines = slice(i * step, (i + 1) * step)
        for s, rhs in enumerate(right_sides(u_ref[lines, :], 1)):
            split(jnp.where(known, rhs, 0.0), (s, lines), high_y, rest_y)
    left = lax.broadcasted_iota(jnp.int32, (1, TILE), 1) < TILE // 2
    count = max((columns - WINDOW) // TILE, 0) + 1
    step = min(rows, 128)
    for i in range(rows // step):
        lines = slice(i * step, (i + 1) * step)
        for s in range(2):
            upper, lower = k_ref[2 * s, :span, :span], k_ref[2 * s + 1, :span, :span]
            windows = []
            for w in range(count):
                lanes = slice(w * TILE, w * TILE + span)
                high, rest = high_y[s, lines, lanes], rest_y[s, lines, lanes]
                windows.append(dot(high, upper) + dot(rest, upper) + dot(high, lower))
            tiles = columns // TILE
            for t in range(tiles):
                if t == 0:
                    tile = windows[0][:, :TILE]
                elif t == tiles - 1:
                    tile = windows[-1][:, span - TILE :]
                else:
                    tile = jnp.where(left, windows[t - 1][:, TILE:], windows[t][:, :TILE])
                if t == 0:
                    strips_y[s, 0, lines] = tile
                elif t == tiles - 1:
                    strips_y[s, 1, lines] = tile
                else:
                    solved_y[s, lines, (t - 1) * TILE : t * TILE] = tile
        if columns > 2 * TILE:
            for s in range(2):
                lines = pl.ds(i * step, step)
                send(solved_y.at[s, lines], outs_y[s].at[lines, pl.ds(TILE, columns - 2 * TILE)])
    for copy in started:
        copy.wait()


def side_terms(around, tails, high):
    found = []
    for s, rhs in enumerate(right_sides(around, 0)):
        ratio, scale = RATIOS[s], SCALES[s]
        pick = lambda row: rhs[row : row + 1]
        if high:
            outer, beyond, nearest, second = pick(4), pick(5), pick(3), pick(2)
        else:
            outer, beyond, nearest, second = pick(3), pick(2), pick(4), pick(5)
        total = ratio * (outer + ratio * (beyond + ratio * tails[s])) + nearest
        found.append((scale * total, scale * second))
    return found


def both_sides(from_low, from_high, own_low, own_high):
    row = lax.broadcasted_iota(jnp.int32, own_low.shape, 0)
    low = jnp.where(row < 4, from_low, pltpu.roll(own_low, 4, 0))
    high = jnp.where(row < 4, pltpu.roll(own_high, 4, 0), pltpu.roll(from_high, 4, 0))
    tails = lambda m: (m[4:5], m[5:6])
    return side_terms(low, tails(from_low), False), side_terms(high, tails(from_high), True)


def finish_kernel(from_low_x, from_high_x, from_y, from_core, near_low, near_high, own_x, strips_x, strips_y, *refs):
    dx, dy, dxx, dyy, done_x, done_y, held, sems = refs[4:]
    rows, columns = dx.shape
    started = []

    def send(source, target):
        copy = pltpu.make_async_copy(source, target, sems.at[len(started)])
        copy.start()
        started.append(copy)

    even = lax.rem(lax.axis_index("gy"), 2) == 0
    held[...] = jnp.zeros_like(held)
    held[0, : from_y.shape[0]] = from_y[:, pl.ds(0, rows)]
    held[1] = from_core[...]
    from_low = jnp.where(even, held[0], held[1])
    from_high = jnp.where(even, held[1], held[0])
    terms = both_sides(from_low, from_high, near_low[...], near_high[...])
    factors, basis = [], []
    lane = lax.broadcasted_iota(jnp.int32, (1, 4 * TILE), 1)
    row8 = lax.broadcasted_iota(jnp.int32, (8, 1), 0)
    stacked = jnp.zeros((8, rows), F32)
    table = jnp.zeros((8, 4 * TILE), F32)
    for side in range(2):
        for s in range(2):
            block = 2 * s + side
            within = lane - block * TILE
            inside = (within >= 0) & (within < TILE)
            distance = (TILE - 1 - within) if side else within
            for which in range(2):
                index = 4 * side + 2 * s + which
                power = jnp.where(inside, powers(RATIOS[s], jnp.abs(distance - which)), 0.0)
                stacked = jnp.where(row8 == index, terms[side][s][which], stacked)
                table = jnp.where(row8 == index, power, table)
    upper = lambda a: a.astype(BF16).astype(F32)
    lower = lambda a: a - upper(a)
    zero = jnp.zeros((8, 1), F32)
    lhs = jnp.concatenate([upper(stacked), lower(stacked), upper(stacked), jnp.broadcast_to(zero, stacked.shape)], axis=0)
    rhs = jnp.concatenate([upper(table), upper(table), lower(table), jnp.broadcast_to(zero, table.shape)], axis=0)
    added = lax.dot_general(
        lhs.astype(BF16), rhs.astype(BF16), (((0,), (0,)), ((), ())), preferred_element_type=F32
    )
    for s, out in enumerate((dy, dyy)):
        for side in range(2):
            block = 2 * s + side
            done_y[s, side] = strips_y[s, side] + added[:, block * TILE : (block + 1) * TILE]
            send(done_y.at[s, side], out.at[:, pl.ds(side * (columns - TILE), TILE)])

    held_x = jnp.concatenate([from_high_x[...], jnp.zeros((MESSAGE - from_high_x.shape[0], columns), F32)], axis=0)
    terms = both_sides(from_low_x[...], held_x, own_x[0], own_x[1])
    at = lax.broadcasted_iota(jnp.int32, (EDGE, 1), 0)
    for s, out in enumerate((dx, dxx)):
        for side in range(2):
            distance = (EDGE - 1 - at) if side else at
            near, second = terms[side][s]
            extra = near * powers(RATIOS[s], distance) + second * powers(RATIOS[s], jnp.abs(distance - 1))
            done_x[s, side] = strips_x[s, side] + extra
            send(done_x.at[s, side], out.at[pl.ds(side * (rows - EDGE), EDGE)])
    for copy in started:
        copy.wait()


def local(velocity):
    u = velocity[0]
    rows, columns = u.shape
    wide = max(rows, columns)
    on_chip = lambda *shape: pltpu.VMEM(shape, F32)
    gx, gy = lax.axis_size("gx"), lax.axis_size("gy")
    to_high_x, to_low_x, to_y, to_core, near_low, near_high = pl.pallas_call(
        pack_kernel,
        name="pack",
        out_shape=(
            on_chip(MESSAGE, columns),
            on_chip(MESSAGE - 2, columns),
            on_chip(MESSAGE - 1, wide),
            on_chip(MESSAGE, rows),
            on_chip(8, rows),
            on_chip(8, rows),
        ),
        in_specs=[ANY],
        out_specs=[VMEM] * 6,
        scratch_shapes=[
            on_chip(EDGE, columns),
            on_chip(EDGE, columns),
            on_chip(rows, TILE),
            on_chip(rows, TILE),
            pltpu.SemaphoreType.DMA((4,)),
        ],
    )(u)
    from_low_x = lax.ppermute(to_high_x, "gx", [(i, (i + 1) % gx) for i in range(gx)])
    across = [(i, (i - 1) % gy) if i % 2 == 0 else (i, (i + 1) % gy) for i in range(gy)]
    within = [(i, i + 1) if i % 2 == 0 else (i, i - 1) for i in range(gy)]
    from_y = lax.ppermute(to_y, "gy", across)
    from_high_x = lax.ppermute(to_low_x, "gx", [(i, (i - 1) % gx) for i in range(gx)])
    from_core = lax.ppermute(to_core, "gy", within)

    in_hbm = pltpu.HBM(u.shape, F32)
    u_near = pltpu.with_memory_space_constraint(u, pltpu.VMEM)
    inverses = pltpu.with_memory_space_constraint(jnp.asarray(inverse_parts()), pltpu.VMEM)
    dx, dy, dxx, dyy, strips_x, strips_y = pl.pallas_call(
        interior_kernel,
        name="interior",
        out_shape=(in_hbm,) * 4 + (on_chip(2, 2, EDGE, columns), on_chip(2, 2, rows, TILE)),
        in_specs=[VMEM, VMEM],
        out_specs=[ANY] * 4 + [VMEM] * 2,
        scratch_shapes=[pltpu.VMEM((2, rows, columns), BF16)] * 4
        + [
            on_chip(2, rows, columns),
            on_chip(2, rows, max(columns - 2 * TILE, TILE)),
            pltpu.SemaphoreType.DMA((16,)),
        ],
        cost_estimate=pl.CostEstimate(flops=2 * 2**28, bytes_accessed=5 * 2**19, transcendentals=0),
    )(u_near, inverses)
    own_x = jnp.stack([u[:8], u[rows - 8 :]])
    near = lambda a: pltpu.with_memory_space_constraint(a, pltpu.VMEM)
    out = jax.ShapeDtypeStruct(u.shape, F32)
    outs = pl.pallas_call(
        finish_kernel,
        name="finish",
        out_shape=(in_hbm,) * 4,
        in_specs=[VMEM] * 9 + [ANY] * 4,
        out_specs=[ANY] * 4,
        input_output_aliases={9 + k: k for k in range(4)},
        scratch_shapes=[
            on_chip(2, 2, EDGE, columns),
            on_chip(2, 2, rows, TILE),
            on_chip(2, MESSAGE, rows),
            pltpu.SemaphoreType.DMA((8,)),
        ],
    )(near(from_low_x), near(from_high_x), near(from_y), near(from_core), near(near_low), near(near_high), near(own_x), near(strips_x), near(strips_y), dx, dy, dxx, dyy)
    return tuple(o[None] for o in outs)


def solution(mesh):
    placed = P(None, "gx", "gy")
    return jax.shard_map(local, mesh=mesh, in_specs=(placed,), out_specs=(placed,) * 4, check_vma=False)
```

time: 1570 us -> 14.7 us (0.01); the launches traced: 1550 us -> 14.5 us
  other arithmetic: 1060 us -> 0.01 us
  local copies, waits for them, and re-layouts: 363 us -> 1.04 us
  loops' own time: 103 us -> 0 us
    sub x52 -> x0, other arithmetic: 1050 us -> none  [window_rows(): lax.linalg.tridiagonal_solve(lower, diagonal, upper, jnp.eye(length, dtyp...]
    slice x331 -> x1, local copies, waits for them, and re-layouts: 281 us -> 0.01 us  [local(): own_x = jnp.stack([u[:8], u[rows - 8:]])]
    another operation x8 -> x0, loops' own time: 103 us -> none  [window_rows(): lax.linalg.tridiagonal_solve(lower, diagonal, upper, jnp.eye(length, dtyp...]
    concatenate x164 -> x0, local copies, waits for them, and re-layouts: 27.7 us -> none  [window_rows(): lax.linalg.tridiagonal_solve(lower, diagonal, upper, jnp.eye(length, dtyp...]
    broadcast_in_dim x3388 -> x0, local copies, waits for them, and re-layouts: 27.3 us -> none  [window_rows(): lax.linalg.tridiagonal_solve(lower, diagonal, upper, jnp.eye(length, dtyp...]
    dynamic_update_slice x156 -> x0, local copies, waits for them, and re-layouts: 19.4 us -> none  [window_rows(): lax.linalg.tridiagonal_solve(lower, diagonal, upper, jnp.eye(length, dtyp...]
where the time goes in v1:
time: 14.7 us; the launch traced here: 14.5 us
  starting transfers between devices  7.4 us (50%)
  Pallas kernels  5.32 us (36%)
  local copies, waits for them, and re-layouts  1.04 us (7%)
  between operations  0.7 us (5%)
    ppermute x1, starting transfers between devices, local(): lax.ppermute(to_low_x, 'gx', [(i, (i - 1) % gx) for i in range(gx)])  3.12 us
    pallas_call x1, Pallas kernels, local(): pl.pallas_call(interior_kernel, name='interior', out_shape=(in_hbm,) * 4...  2.66 us
    ppermute x1, starting transfers between devices, local(): lax.ppermute(to_high_x, 'gx', [(i, (i + 1) % gx) for i in range(gx)])  2.55 us
    pallas_call x1, Pallas kernels, local(): pl.pallas_call(pack_kernel, name='pack', out_shape=(on_chip(MESSAGE, colu...  1.43 us
    pallas_call x1, Pallas kernels, local(): pl.pallas_call(finish_kernel, name='finish', out_shape=(in_hbm,) * 4, in_...  1.23 us
    ppermute x1, starting transfers between devices, local(): from_y = lax.ppermute(to_y, 'gy', across)  1.21 us
    unnamed x4, local copies, waits for them, and re-layouts  1.04 us
    ppermute x1, starting transfers between devices, local(): from_core = lax.ppermute(to_core, 'gy', within)  0.52 us
  transfers between devices with their start and end apart: 4, of which 0 were waited for; matrix products, arithmetic and copies ran while one was open for 0% of the time, Pallas kernels for 18%

profile of v1, /device:TPU:0, one launch (start us, length us, event | category | flops | bytes accessed | tf_op | source)
XLA Modules:
  0.0 14.5 jit_solution(407901839778909830)
XLA Ops:
  0.6 0.0 copy-start
  0.6 1.4 %pack.1 = (f32[8,512]{1,0:T(8,128)S(1)}, f32[6,512]{1,0:T(8,128)S(1)}, f32[7,512]{1,0:T(8,128)S(1)}, f32[8,256]{1,0:T(8,128)S(1)}, f32[8,256]{1,0:T(8,128)S(1)}, /*index=5*/f32[8,256]{1,0:T(8,128)S(1)}) custom-call(f32[256,512]{1,0:T(8,128)} %bitcast.5), custom_call_target="tpu_custom_call" | custom-call | tf_op jit(solution)/shard_map/pack/pallas_call | solution.py:272
  2.1 0.5 %collective-permute-start.3 = (f32[8,256]{1,0:T(8,128)S(1)}, f32[8,256]{1,0:T(8,128)S(1)}, u32[]{:S(2)}, u32[]{:S(2)}) collective-permute-start(f32[8,256]{1,0:T(8,128)S(1)} %get-tuple-element.23), channel_id=1, source_target_pairs={{0,1},{1,0},{2,3},{3,2},{4,5},{5,4},{6,7},{7,6},{8,9},{9,8},{10,11... | collective-permute-start | bytes 24584 | tf_op jit(solution)/shard_map/ppermute | solution.py:298
  2.6 2.6 %collective-permute-start = (f32[8,512]{1,0:T(8,128)S(1)}, f32[8,512]{1,0:T(8,128)S(1)}, u32[]{:S(2)}, u32[]{:S(2)}) collective-permute-start(f32[8,512]{1,0:T(8,128)S(1)} %get-tuple-element.20), channel_id=1, source_target_pairs={{0,4},{4,8},{8,12},{12,16},{16,20},{20,24},{24,28},{28,0},{1,5},{5... | collective-permute-start | bytes 49160 | tf_op jit(solution)/shard_map/ppermute | solution.py:293
  5.1 3.1 %collective-permute-start.1 = (f32[6,512]{1,0:T(8,128)S(1)}, f32[6,512]{1,0:T(8,128)S(1)}, u32[]{:S(2)}, u32[]{:S(2)}) collective-permute-start(f32[6,512]{1,0:T(8,128)S(1)} %get-tuple-element.21), channel_id=1, source_target_pairs={{0,28},{4,0},{8,4},{12,8},{16,12},{20,16},{24,20},{28,24},{1,29},{... | collective-permute-start | bytes 36872 | tf_op jit(solution)/shard_map/ppermute | solution.py:297
  8.3 1.2 %collective-permute-start.2 = (f32[7,512]{1,0:T(8,128)S(1)}, f32[7,512]{1,0:T(8,128)S(1)}, u32[]{:S(2)}, u32[]{:S(2)}) collective-permute-start(f32[7,512]{1,0:T(8,128)S(1)} %get-tuple-element.22), channel_id=1, source_target_pairs={{0,3},{1,2},{2,1},{3,0},{4,7},{5,6},{6,5},{7,4},{8,11},{9,10},{10,... | collective-permute-start | bytes 43016 | tf_op jit(solution)/shard_map/ppermute | solution.py:296
  9.5 0.0 copy-done
  9.5 0.0 copy-start.1
  9.5 1.0 %copy-done.1 = bf16[4,256,256]{2,1,0:T(8,128)(2,1)S(1)} copy-done((bf16[4,256,256]{2,1,0:T(8,128)(2,1)S(1)}, bf16[4,256,256]{2,1,0:T(8,128)(2,1)}, u32[]{:S(2)}) %copy-start.1) | copy-done | bytes 524312
  10.5 2.7 %interior.1 = (f32[256,512]{1,0:T(8,128)}, f32[256,512]{1,0:T(8,128)}, f32[256,512]{1,0:T(8,128)}, f32[256,512]{1,0:T(8,128)}, f32[2,2,32,512]{3,2,1,0:T(8,128)S(1)}, /*index=5*/f32[2,2,256,128]{3,2,1,0:T(8,128)S(1)}) custom-call(f32[256,512]{1,0:T(8,128)S(1)} %bitcast.6, bf16[4,256,256]{2,1,0:T(8,128)(2,1)S(1)} %copy-done.1), custom_call_target="tpu_custom_call" | custom-call | flops 536870912 | bytes 2621440 | tf_op jit(solution)/shard_map/interior/pallas_call | solution.py:303
  13.2 0.0 collective-permute-done.3.from_core
  13.2 0.0 collective-permute-done.1.from_high_x
  13.2 0.0 collective-permute-done.2.from_y
  13.2 0.0 collective-permute-done.from_low_x
  13.2 1.2 %finish.1 = (f32[256,512]{1,0:T(8,128)}, f32[256,512]{1,0:T(8,128)}, f32[256,512]{1,0:T(8,128)}, f32[256,512]{1,0:T(8,128)}) custom-call(f32[8,512]{1,0:T(8,128)S(1)} %collective-permute-done.from_low_x, f32[6,512]{1,0:T(8,128)S(1)} %collective-permute-done.1.from_high_x, ...), custom_call_target="tpu_custom_call", output_to_operand_aliasing={{0}: (9, {}), {1}: (10, {}), {2}: (11, {}), {3}: (12, {})} | custom-call | tf_op jit(solution)/shard_map/finish/pallas_call | solution.py:320
  (2 shorter events, 0.0 us)
Async XLA Ops:
  0.6 8.8 %copy-start = (f32[1,256,512]{2,1,0:T(8,128)S(1)}, f32[1,256,512]{2,1,0:T(8,128)}, u32[]{:S(2)}) copy-start(f32[1,256,512]{2,1,0:T(8,128)} %param.2) | copy-start | bytes 1572868
  2.1 11.1 %collective-permute-start.3 = (f32[8,256]{1,0:T(8,128)S(1)}, f32[8,256]{1,0:T(8,128)S(1)}, u32[]{:S(2)}, u32[]{:S(2)}) collective-permute-start(f32[8,256]{1,0:T(8,128)S(1)} %get-tuple-element.23), channel_id=1, source_target_pairs={{0,1},{1,0},{2,3},{3,2},{4,5},{5,4},{6,7},{7,6},{8,9},{9,8},{10,11... | collective-permute-start | bytes 24584 | tf_op jit(solution)/shard_map/ppermute | solution.py:298
  2.6 10.6 %collective-permute-start = (f32[8,512]{1,0:T(8,128)S(1)}, f32[8,512]{1,0:T(8,128)S(1)}, u32[]{:S(2)}, u32[]{:S(2)}) collective-permute-start(f32[8,512]{1,0:T(8,128)S(1)} %get-tuple-element.20), channel_id=1, source_target_pairs={{0,4},{4,8},{8,12},{12,16},{16,20},{20,24},{24,28},{28,0},{1,5},{5... | collective-permute-start | bytes 49160 | tf_op jit(solution)/shard_map/ppermute | solution.py:293
  5.1 8.1 %collective-permute-start.1 = (f32[6,512]{1,0:T(8,128)S(1)}, f32[6,512]{1,0:T(8,128)S(1)}, u32[]{:S(2)}, u32[]{:S(2)}) collective-permute-start(f32[6,512]{1,0:T(8,128)S(1)} %get-tuple-element.21), channel_id=1, source_target_pairs={{0,28},{4,0},{8,4},{12,8},{16,12},{20,16},{24,20},{28,24},{1,29},{... | collective-permute-start | bytes 36872 | tf_op jit(solution)/shard_map/ppermute | solution.py:297
  8.3 5.0 %collective-permute-start.2 = (f32[7,512]{1,0:T(8,128)S(1)}, f32[7,512]{1,0:T(8,128)S(1)}, u32[]{:S(2)}, u32[]{:S(2)}) collective-permute-start(f32[7,512]{1,0:T(8,128)S(1)} %get-tuple-element.22), channel_id=1, source_target_pairs={{0,3},{1,2},{2,1},{3,0},{4,7},{5,6},{6,5},{7,4},{8,11},{9,10},{10,... | collective-permute-start | bytes 43016 | tf_op jit(solution)/shard_map/ppermute | solution.py:296
  9.5 1.0 %copy-start.1 = (bf16[4,256,256]{2,1,0:T(8,128)(2,1)S(1)}, bf16[4,256,256]{2,1,0:T(8,128)(2,1)}, u32[]{:S(2)}) copy-start(bf16[4,256,256]{2,1,0:T(8,128)(2,1)} %constant.2.clone.k_ref) | copy-start | bytes 1572868

commit v2 on v1

v2 whole, which is shorter than its diff:
```python
import math

import jax
import jax.numpy as jnp
from jax import lax
from jax.experimental import pallas as pl
from jax.experimental.pallas import tpu as pltpu
from jax.sharding import PartitionSpec as P

F32 = jnp.float32
BF16 = jnp.bfloat16

FIRST_IN, FIRST_OUT = 7.0 / 9.0 + 1.0 / 36.0, 1.0 / 36.0
SECOND_IN, SECOND_OUT = 12.0 / 11.0 + 3.0 / 44.0, 3.0 / 44.0

COUPLINGS = (1.0 / 3.0, 2.0 / 11.0)
RATIOS = tuple((math.sqrt(1.0 - 4.0 * a * a) - 1.0) / (2.0 * a) for a in COUPLINGS)
SCALES = tuple(1.0 / math.sqrt(1.0 - 4.0 * a * a) for a in COUPLINGS)

WINDOW = 256
TILE = 128
EDGE = 32
REACH = 64
MESSAGE = 8

ANY = pl.BlockSpec(memory_space=pl.ANY)
VMEM = pl.BlockSpec(memory_space=pltpu.VMEM)


def right_sides(cells, axis):
    length = cells.shape[axis]
    step = lambda a, k: pltpu.roll(a, k % length, axis)
    here = step(cells, -1) - cells
    before, after, far = step(here, 1), step(here, -1), step(here, 2)
    first = FIRST_IN * (here + before) + FIRST_OUT * (after + far)
    second = SECOND_IN * (here - before) + SECOND_OUT * (after - far)
    return first, second


def powers(ratio, exponent):
    product = jnp.where(exponent < REACH, F32(1.0), F32(0.0))
    for bit in range(REACH.bit_length() - 1):
        factor = jnp.where((exponent & (1 << bit)) != 0, F32(ratio ** (1 << bit)), F32(1.0))
        product = product * factor
    return product


def tail_weights(high):
    at = lax.broadcasted_iota(jnp.int32, (EDGE, TILE), 0)
    known = (at >= 2) & (at < EDGE - 2)
    exponent = (EDGE - 3 - at) if high else (at - 2)
    return [jnp.where(known, powers(ratio, exponent), 0.0) for ratio in RATIOS]


def message(strip, high, weights):
    tails = [
        jnp.sum(rhs * weight[:, : strip.shape[1]], axis=0, keepdims=True)
        for rhs, weight in zip(right_sides(strip, 0), weights)
    ]
    near = pltpu.roll(strip[EDGE - 8 :], 4, 0) if high else strip[:8]
    row = lax.broadcasted_iota(jnp.int32, near.shape, 0)
    return jnp.where(row < 4, near, jnp.where(row == 4, tails[0], tails[1]))


def tiles_of(length):
    step = min(length, TILE)
    return [pl.ds(k * step, step) for k in range(length // step)]


def halves(value):
    upper = value.astype(BF16).astype(F32)
    return upper, value - upper


def put_inverses(k_ref):
    i = lax.broadcasted_iota(jnp.int32, (TILE, TILE), 0)
    j = lax.broadcasted_iota(jnp.int32, (TILE, TILE), 1)
    blocks = WINDOW // TILE
    for s in range(2):
        for apart in range(1 - blocks, blocks):
            upper, lower = halves(SCALES[s] * powers(RATIOS[s], jnp.abs(j - i + apart * TILE)))
            for p, part in enumerate((upper, lower)):
                for first in range(blocks):
                    if 0 <= first + apart < blocks:
                        at_i, at_j = pl.ds(first * TILE, TILE), pl.ds((first + apart) * TILE, TILE)
                        k_ref[2 * s + p, at_i, at_j] = part.astype(BF16)


def put_side_tables(table_x, table_y):
    at = lax.broadcasted_iota(jnp.int32, (EDGE, TILE), 0)
    lane = lax.broadcasted_iota(jnp.int32, (8, TILE), 1)
    row = lax.broadcasted_iota(jnp.int32, (8, TILE), 0)
    for s in range(2):
        for side in range(2):
            within = (TILE - 1 - lane) if side else lane
            lines = jnp.zeros((8, TILE), F32)
            for which in range(2):
                distance = (EDGE - 1 - at) if side else at
                table_x[s, side, which] = powers(RATIOS[s], jnp.abs(distance - which))
                lines = jnp.where(row == 4 * side + 2 * s + which, powers(RATIOS[s], jnp.abs(within - which)), lines)
            upper, lower = halves(lines)
            stack = jnp.concatenate([upper, upper, lower, jnp.zeros_like(upper)], axis=0)
            block = 2 * s + side
            table_y[:, pl.ds(block * TILE, TILE)] = stack.astype(BF16)


def pack_kernel(
    u_ref, to_high_x, to_low_x, to_y, to_core, u_near, near_low, near_high, k_ref, table_x, table_y, sems
):
    rows, columns = u_ref.shape
    across = [pl.ds(0, TILE), pl.ds(columns - TILE, TILE)]
    pieces = [(pl.ds(0, rows), lanes) for lanes in across]
    if columns > 2 * TILE:
        middle = pl.ds(TILE, columns - 2 * TILE)
        pieces += [(pl.ds(0, EDGE), middle), (pl.ds(rows - EDGE, EDGE), middle)]
        if rows > 2 * EDGE:
            pieces.append((pl.ds(EDGE, rows - 2 * EDGE), middle))
    copies = [
        pltpu.make_async_copy(u_ref.at[lines, lanes], u_near.at[lines, lanes], sems.at[k])
        for k, (lines, lanes) in enumerate(pieces)
    ]
    for copy in copies:
        copy.start()
    even = lax.rem(lax.axis_index("gy"), 2) == 0
    weights_low, weights_high = tail_weights(False), tail_weights(True)
    put_inverses(k_ref)
    put_side_tables(table_x, table_y)
    copies[0].wait()
    copies[1].wait()
    low = u_near[:, across[0]].T[:EDGE]
    high = u_near[:, across[1]].T[TILE - EDGE :]
    near_low[...] = low[:8]
    near_high[...] = high[EDGE - 8 :]
    for lanes in tiles_of(rows):
        part = slice(lanes.start, lanes.start + lanes.size)
        to_low, to_high = message(low[:, part], False, weights_low), message(high[:, part], True, weights_high)
        to_y[:, lanes] = jnp.where(even, to_low, to_high)
        to_core[:, lanes] = jnp.where(even, to_high, to_low)
    for copy in copies[2:4]:
        copy.wait()
    for lanes in tiles_of(columns):
        to_low_x[:, lanes] = message(u_near[pl.ds(0, EDGE), lanes], False, weights_low)
        to_high_x[:, lanes] = message(u_near[pl.ds(rows - EDGE, EDGE), lanes], True, weights_high)
    for copy in copies[4:]:
        copy.wait()


def put_split(value, at, high, rest):
    upper = value.astype(BF16)
    high[at] = upper
    rest[at] = (value - upper.astype(F32)).astype(BF16)


def dot(a, b):
    return jnp.dot(a, b, preferred_element_type=F32)


def solve_x(u_ref, k_ref, outs, strips, high_ref, rest_ref, solved_ref, sems):
    rows, columns = u_ref.shape
    at = lax.broadcasted_iota(jnp.int32, (rows, 1), 0)
    known = (at >= 2) & (at < rows - 2)
    for lanes in tiles_of(columns):
        for s, rhs in enumerate(right_sides(u_ref[:, lanes], 0)):
            put_split(jnp.where(known, rhs, 0.0), (s, slice(None), lanes), high_ref, rest_ref)
    span = min(columns, WINDOW)
    for s in range(2):
        for j in range(columns // span):
            lanes = slice(j * span, (j + 1) * span)
            upper, lower = k_ref[2 * s, :rows, :rows], k_ref[2 * s + 1, :rows, :rows]
            high, rest = high_ref[s, :, lanes], rest_ref[s, :, lanes]
            solved = dot(upper, high) + dot(upper, rest) + dot(lower, high)
            solved_ref[s, :, lanes] = solved
            strips[s, 0, :, lanes] = solved[:EDGE]
            strips[s, 1, :, lanes] = solved[rows - EDGE :]
    if rows > 2 * EDGE:
        inner = pl.ds(EDGE, rows - 2 * EDGE)
        copies = [pltpu.make_async_copy(solved_ref.at[s, inner], outs[s].at[inner], sems.at[s]) for s in range(2)]
        for copy in copies:
            copy.start()
        return copies
    return []


def solve_y(u_ref, k_ref, outs, strips, high_ref, rest_ref, solved_ref, sems):
    rows, columns = u_ref.shape
    at = lax.broadcasted_iota(jnp.int32, (1, columns), 1)
    known = (at >= 2) & (at < columns - 2)
    step = min(rows, 64)
    for i in range(rows // step):
        lines = slice(i * step, (i + 1) * step)
        for s, rhs in enumerate(right_sides(u_ref[lines, :], 1)):
            put_split(jnp.where(known, rhs, 0.0), (s, lines), high_ref, rest_ref)
    left = lax.broadcasted_iota(jnp.int32, (1, TILE), 1) < TILE // 2
    span = min(columns, WINDOW)
    count = max((columns - WINDOW) // TILE, 0) + 1
    tiles = columns // TILE
    step = min(rows, 128)
    copies = []
    for s in range(2):
        upper, lower = k_ref[2 * s, :span, :span], k_ref[2 * s + 1, :span, :span]
        for i in range(rows // step):
            lines = slice(i * step, (i + 1) * step)
            windows = []
            for w in range(count):
                lanes = slice(w * TILE, w * TILE + span)
                high, rest = high_ref[s, lines, lanes], rest_ref[s, lines, lanes]
                windows.append(dot(high, upper) + dot(rest, upper) + dot(high, lower))
            for t in range(tiles):
                if t == 0:
                    strips[s, 0, lines] = windows[0][:, :TILE]
                elif t == tiles - 1:
                    strips[s, 1, lines] = windows[-1][:, span - TILE :]
                else:
                    tile = jnp.where(left, windows[t - 1][:, TILE:], windows[t][:, :TILE])
                    solved_ref[s, lines, (t - 1) * TILE : t * TILE] = tile
        if tiles > 2:
            copies.append(pltpu.make_async_copy(solved_ref.at[s], outs[s].at[:, pl.ds(TILE, columns - 2 * TILE)], sems.at[s]))
            copies[-1].start()
    return copies


def solves_x_early():
    return (lax.axis_index("gx") == 0) & (lax.axis_index("gy") < 2)


def solves_y_early():
    return lax.axis_index("gx") == 0


def lead_x_kernel(u_ref, k_ref, *refs):
    dx, dxx, strips_x, *scratch = refs[4:]

    @pl.when(solves_x_early())
    def _():
        for copy in solve_x(u_ref, k_ref, (dx, dxx), strips_x, *scratch):
            copy.wait()


def lead_y_kernel(u_ref, k_ref, *refs):
    dy, dyy, strips_y, *scratch = refs[4:]

    @pl.when(solves_y_early())
    def _():
        for copy in solve_y(u_ref, k_ref, (dy, dyy), strips_y, *scratch):
            copy.wait()


def interior_kernel(u_ref, k_ref, *refs):
    dx, dxx, strips_x, dy, dyy, strips_y, *scratch = refs[6:]
    for_x, for_y = scratch[:4], scratch[4:]

    @pl.when(solves_y_early() & jnp.logical_not(solves_x_early()))
    def _():
        for copy in solve_x(u_ref, k_ref, (dx, dxx), strips_x, *for_x):
            copy.wait()

    @pl.when(jnp.logical_not(solves_y_early()))
    def _():
        copies = solve_x(u_ref, k_ref, (dx, dxx), strips_x, *for_x)
        copies += solve_y(u_ref, k_ref, (dy, dyy), strips_y, *for_y)
        for copy in copies:
            copy.wait()


def side_terms(around, tails, high):
    found = []
    for s, rhs in enumerate(right_sides(around, 0)):
        ratio, scale = RATIOS[s], SCALES[s]
        pick = lambda row: rhs[row : row + 1]
        if high:
            outer, beyond, nearest, second = pick(4), pick(5), pick(3), pick(2)
        else:
            outer, beyond, nearest, second = pick(3), pick(2), pick(4), pick(5)
        total = ratio * (outer + ratio * (beyond + ratio * tails[s])) + nearest
        found.append((scale * total, scale * second))
    return found


def both_sides(from_low, from_high, own_low, own_high):
    row = lax.broadcasted_iota(jnp.int32, own_low.shape, 0)
    low = jnp.where(row < 4, from_low, pltpu.roll(own_low, 4, 0))
    high = jnp.where(row < 4, pltpu.roll(own_high, 4, 0), pltpu.roll(from_high, 4, 0))
    tails = lambda m: (m[4:5], m[5:6])
    return side_terms(low, tails(from_low), False), side_terms(high, tails(from_high), True)


def finish_kernel(
    from_low_x, from_y, from_high_x, from_core, u_near, near_low, near_high, table_x, table_y, strips_x, strips_y, *refs
):
    dx, dxx, dy, dyy, done_x, done_y, sems = refs[4:]
    rows, columns = dx.shape
    started = []

    def send(source, target):
        copy = pltpu.make_async_copy(source, target, sems.at[len(started)])
        copy.start()
        started.append(copy)

    even = lax.rem(lax.axis_index("gy"), 2) == 0
    across, within = from_y[:, pl.ds(0, rows)], from_core[:, pl.ds(0, rows)]
    from_low = jnp.where(even, across, within)
    from_high = jnp.where(even, within, across)
    terms = both_sides(from_low, from_high, near_low[...], near_high[...])
    row = lax.broadcasted_iota(jnp.int32, (8, 1), 0)
    stacked = jnp.zeros((8, rows), F32)
    for side in range(2):
        for s in range(2):
            for which in range(2):
                stacked = jnp.where(row == 4 * side + 2 * s + which, terms[side][s][which], stacked)
    upper, lower = halves(stacked)
    factors = jnp.concatenate([upper, lower, upper, jnp.zeros_like(upper)], axis=0).astype(BF16)
    added = lax.dot_general(factors, table_y[...], (((0,), (0,)), ((), ())), preferred_element_type=F32)
    for s, out in enumerate((dy, dyy)):
        for side in range(2):
            block = 2 * s + side
            done_y[s, side] = strips_y[s, side] + added[:, block * TILE : (block + 1) * TILE]
            send(done_y.at[s, side], out.at[:, pl.ds(side * (columns - TILE), TILE)])

    terms = both_sides(from_low_x[...], from_high_x[...], u_near[pl.ds(0, 8)], u_near[pl.ds(rows - 8, 8)])
    step = min(columns, TILE)
    for s, out in enumerate((dx, dxx)):
        for side in range(2):
            near, second = terms[side][s]
            for j in range(columns // step):
                lanes = slice(j * step, (j + 1) * step)
                extra = near[:, lanes] * table_x[s, side, 0, :, :step] + second[:, lanes] * table_x[s, side, 1, :, :step]
                done_x[s, side, :, lanes] = strips_x[s, side, :, lanes] + extra
            send(done_x.at[s, side], out.at[pl.ds(side * (rows - EDGE), EDGE)])
    for copy in started:
        copy.wait()


def on_chip(*shape):
    return pltpu.VMEM(shape, F32)


def near(array):
    return pltpu.with_memory_space_constraint(array, pltpu.VMEM)


def pack(u):
    rows, columns = u.shape
    wide = max(rows, columns)
    return pl.pallas_call(
        pack_kernel,
        name="pack",
        out_shape=(
            on_chip(MESSAGE, columns),
            on_chip(MESSAGE, columns),
            on_chip(MESSAGE, wide),
            on_chip(MESSAGE, wide),
            on_chip(rows, columns),
            on_chip(8, rows),
            on_chip(8, rows),
            pltpu.VMEM((4, WINDOW, WINDOW), BF16),
            on_chip(2, 2, 2, EDGE, TILE),
            pltpu.VMEM((32, 4 * TILE), BF16),
        ),
        in_specs=[ANY],
        out_specs=[VMEM] * 10,
        scratch_shapes=[pltpu.SemaphoreType.DMA((5,))],
    )(u)


def scratch_x(rows, columns):
    return [pltpu.VMEM((2, rows, columns), BF16)] * 2 + [on_chip(2, rows, columns), pltpu.SemaphoreType.DMA((2,))]


def scratch_y(rows, columns):
    inner = max(columns - 2 * TILE, TILE)
    return [pltpu.VMEM((2, rows, columns), BF16)] * 2 + [on_chip(2, rows, inner), pltpu.SemaphoreType.DMA((2,))]


def shapes_x(rows, columns):
    return (pltpu.HBM((rows, columns), F32),) * 2 + (on_chip(2, 2, EDGE, columns),)


def shapes_y(rows, columns):
    return (pltpu.HBM((rows, columns), F32),) * 2 + (on_chip(2, 2, rows, TILE),)


def lead(kernel, name, u_near, inverses, shapes, scratch, passing):
    return pl.pallas_call(
        kernel,
        name=name,
        out_shape=tuple(on_chip(*a.shape) for a in passing) + shapes,
        in_specs=[VMEM] * 4,
        out_specs=[VMEM] * 2 + [ANY] * 2 + [VMEM],
        input_output_aliases={2: 0, 3: 1},
        scratch_shapes=scratch,
    )(near(u_near), near(inverses), *(near(a) for a in passing))


def interior(u_near, inverses, solved_x, solved_y):
    size = u_near.shape
    return pl.pallas_call(
        interior_kernel,
        name="interior",
        out_shape=shapes_x(*size) + shapes_y(*size),
        in_specs=[VMEM] * 2 + ([ANY] * 2 + [VMEM]) * 2,
        out_specs=([ANY] * 2 + [VMEM]) * 2,
        input_output_aliases={2 + k: k for k in range(6)},
        scratch_shapes=scratch_x(*size) + scratch_y(*size),
        cost_estimate=pl.CostEstimate(flops=2 * 2**28, bytes_accessed=5 * 2**19, transcendentals=0),
    )(near(u_near), near(inverses), *solved_x[:2], near(solved_x[2]), *solved_y[:2], near(solved_y[2]))


def finish(arrays, parts):
    rows, columns = parts[0].shape
    return pl.pallas_call(
        finish_kernel,
        name="finish",
        out_shape=(pltpu.HBM(parts[0].shape, F32),) * 4,
        in_specs=[VMEM] * 11 + [ANY] * 4,
        out_specs=[ANY] * 4,
        input_output_aliases={11 + k: k for k in range(4)},
        scratch_shapes=[
            on_chip(2, 2, EDGE, columns),
            on_chip(2, 2, rows, TILE),
            pltpu.SemaphoreType.DMA((8,)),
        ],
    )(*(near(a) for a in arrays), *parts)


def local(velocity):
    to_high_x, to_low_x, to_y, to_core, u_near, near_low, near_high, inverses, *tables = pack(velocity[0])
    size = u_near.shape
    to_high_x, to_y, *solved_x = lead(
        lead_x_kernel, "lead_x", u_near, inverses, shapes_x(*size), scratch_x(*size), (to_high_x, to_y)
    )
    to_low_x, to_core, *solved_y = lead(
        lead_y_kernel, "lead_y", u_near, inverses, shapes_y(*size), scratch_y(*size), (to_low_x, to_core)
    )
    gx, gy = lax.axis_size("gx"), lax.axis_size("gy")
    across = [(i, (i - 1) % gy) if i % 2 == 0 else (i, (i + 1) % gy) for i in range(gy)]
    within = [(i, i + 1) if i % 2 == 0 else (i, i - 1) for i in range(gy)]
    messages = (
        lax.ppermute(to_high_x, "gx", [(i, (i + 1) % gx) for i in range(gx)]),
        lax.ppermute(to_y, "gy", across),
        lax.ppermute(to_low_x, "gx", [(i, (i - 1) % gx) for i in range(gx)]),
        lax.ppermute(to_core, "gy", within),
    )
    dx, dxx, strips_x, dy, dyy, strips_y = interior(u_near, inverses, solved_x, solved_y)
    arrays = (*messages, u_near, near_low, near_high, *tables, strips_x, strips_y)
    dx, dxx, dy, dyy = finish(arrays, (dx, dxx, dy, dyy))
    return tuple(o[None] for o in (dx, dy, dxx, dyy))


def solution(mesh):
    placed = P(None, "gx", "gy")
    return jax.shard_map(local, mesh=mesh, in_specs=(placed,), out_specs=(placed,) * 4, check_vma=False)
```

time: 14.7 us -> 13 us (0.88)
  starting transfers between devices: 7.4 us -> 3.77 us
  waiting for transfers between devices: 0.01 us -> 1.91 us
  Pallas kernels: 5.32 us -> 6.48 us
  local copies, waits for them, and re-layouts: 1.04 us -> 0 us
    ppermute x1, starting transfers between devices: 3.12 us -> 1.49 us  [local(): lax.ppermute(to_low_x, 'gx', [(i, (i - 1) % gx) for i in range(gx)])]
    ppermute x1, starting transfers between devices: 2.55 us -> 1.09 us  [local(): lax.ppermute(to_high_x, 'gx', [(i, (i + 1) % gx) for i in range(gx)])]
    ppermute x1, waiting for transfers between devices: 0.01 us -> 1.22 us  [local(): lax.ppermute(to_low_x, 'gx', [(i, (i - 1) % gx) for i in range(gx)])]
    pallas_call x3 -> x5, Pallas kernels: 5.32 us -> 6.48 us  [the longest x2 3.91 us: lead(): pl.pallas_call(kernel, name=name, out_shape=tuple((on_chip(*a.shape) for...]
    unnamed x4 -> x0, local copies, waits for them, and re-layouts: 1.04 us -> none
    ppermute x1, waiting for transfers between devices: 0.01 us -> 0.68 us  [local(): lax.ppermute(to_high_x, 'gx', [(i, (i + 1) % gx) for i in range(gx)])]
    ppermute x2, starting transfers between devices: 1.72 us -> 1.19 us  [the longest x1 0.68 us: local(): lax.ppermute(to_y, 'gy', across)]
  transfers between devices with their start and end apart: 4 -> 4, of which waited for: 0 -> 2; matrix products, arithmetic and copies ran while one was open for 0% -> 0% of each run, Pallas kernels for 18% -> 16%
where the time goes in v2:
time: 13 us; the launch traced here: 12.8 us
  Pallas kernels  6.48 us (50%)
  starting transfers between devices  3.77 us (29%)
  waiting for transfers between devices  1.91 us (15%)
  between operations  0.67 us (5%)
    pallas_call x2, Pallas kernels, lead(): pl.pallas_call(kernel, name=name, out_shape=tuple((on_chip(*a.shape) for...  3.91 us
    ppermute x1, starting transfers between devices, local(): lax.ppermute(to_low_x, 'gx', [(i, (i - 1) % gx) for i in range(gx)])  1.49 us
    pallas_call x1, Pallas kernels, pack(): pl.pallas_call(pack_kernel, name='pack', out_shape=(on_chip(MESSAGE, colu...  1.3 us
    pallas_call x1, Pallas kernels, finish(): pl.pallas_call(finish_kernel, name='finish', out_shape=(pltpu.HBM(parts[0...  1.23 us
    ppermute x1, waiting for transfers between devices, local(): lax.ppermute(to_low_x, 'gx', [(i, (i - 1) % gx) for i in range(gx)])  1.22 us
    ppermute x1, starting transfers between devices, local(): lax.ppermute(to_high_x, 'gx', [(i, (i + 1) % gx) for i in range(gx)])  1.09 us
    ppermute x1, waiting for transfers between devices, local(): lax.ppermute(to_high_x, 'gx', [(i, (i + 1) % gx) for i in range(gx)])  0.68 us
    ppermute x1, starting transfers between devices, local(): lax.ppermute(to_y, 'gy', across)  0.68 us
  transfers between devices with their start and end apart: 4, of which 2 were waited for; matrix products, arithmetic and copies ran while one was open for 0% of the time, Pallas kernels for 16%

profile of v2, /device:TPU:0, one launch (start us, length us, event | category | flops | bytes accessed | tf_op | source)
XLA Modules:
  0.0 12.8 jit_solution(2046302378368894592)
XLA Ops:
  0.6 1.3 %pack.1 = (f32[8,512]{1,0:T(8,128)S(1)}, f32[8,512]{1,0:T(8,128)S(1)}, f32[8,512]{1,0:T(8,128)S(1)}, f32[8,512]{1,0:T(8,128)S(1)}, f32[256,512]{1,0:T(8,128)S(1)...) custom-call(f32[256,512]{1,0:T(8,128)} %bitcast.9), custom_call_target="tpu_custom_call" | custom-call | tf_op jit(solution)/shard_map/pack/pallas_call | solution.py:344
  1.9 1.9 %lead_x.1 = (f32[8,512]{1,0:T(8,128)S(1)}, f32[8,512]{1,0:T(8,128)S(1)}, f32[256,512]{1,0:T(8,128)}, f32[256,512]{1,0:T(8,128)}, f32[2,2,32,512]{3,2,1,0:T(8,128)S(1)}) custom-call(f32[256,512]{1,0:T(8,128)S(1)} %get-tuple-element.34.u_ref.u_near, bf16[4,256,256]{2,1,0:T(8,128)(2,1)S(1)} %get-tuple-element.35.k_ref, ...), custom_call_target="tpu_custom_call", output_to_operand_aliasing={{0}: (2, {}), {1}: (3, {})} | custom-call | tf_op jit(solution)/shard_map/lead_x/pallas_call | solution.py:383
  3.9 1.1 %collective-permute-start = (f32[8,512]{1,0:T(8,128)S(1)}, f32[8,512]{1,0:T(8,128)S(1)}, u32[]{:S(2)}, u32[]{:S(2)}) collective-permute-start(f32[8,512]{1,0:T(8,128)S(1)} %get-tuple-element.38), channel_id=1, source_target_pairs={{0,4},{4,8},{8,12},{12,16},{16,20},{20,24},{24,28},{28,0},{1,5},{5... | collective-permute-start | bytes 49160 | tf_op jit(solution)/shard_map/ppermute | solution.py:438
  5.0 0.7 %collective-permute-start.1 = (f32[8,512]{1,0:T(8,128)S(1)}, f32[8,512]{1,0:T(8,128)S(1)}, u32[]{:S(2)}, u32[]{:S(2)}) collective-permute-start(f32[8,512]{1,0:T(8,128)S(1)} %get-tuple-element.39), channel_id=1, source_target_pairs={{0,3},{1,2},{2,1},{3,0},{4,7},{5,6},{6,5},{7,4},{8,11},{9,10},{10,... | collective-permute-start | bytes 49160 | tf_op jit(solution)/shard_map/ppermute | solution.py:439
  5.7 2.0 %lead_y.1 = (f32[8,512]{1,0:T(8,128)S(1)}, f32[8,512]{1,0:T(8,128)S(1)}, f32[256,512]{1,0:T(8,128)}, f32[256,512]{1,0:T(8,128)}, f32[2,2,256,128]{3,2,1,0:T(8,128)S(1)}) custom-call(f32[256,512]{1,0:T(8,128)S(1)} %get-tuple-element.34.u_ref.u_near, bf16[4,256,256]{2,1,0:T(8,128)(2,1)S(1)} %get-tuple-element.35.k_ref, ...), custom_call_target="tpu_custom_call", output_to_operand_aliasing={{0}: (2, {}), {1}: (3, {})} | custom-call | tf_op jit(solution)/shard_map/lead_y/pallas_call | solution.py:383
  7.6 1.5 %collective-permute-start.2 = (f32[8,512]{1,0:T(8,128)S(1)}, f32[8,512]{1,0:T(8,128)S(1)}, u32[]{:S(2)}, u32[]{:S(2)}) collective-permute-start(f32[8,512]{1,0:T(8,128)S(1)} %get-tuple-element.42), channel_id=1, source_target_pairs={{0,28},{4,0},{8,4},{12,8},{16,12},{20,16},{24,20},{28,24},{1,29},{... | collective-permute-start | bytes 49160 | tf_op jit(solution)/shard_map/ppermute | solution.py:440
  9.1 0.5 %collective-permute-start.3 = (f32[8,512]{1,0:T(8,128)S(1)}, f32[8,512]{1,0:T(8,128)S(1)}, u32[]{:S(2)}, u32[]{:S(2)}) collective-permute-start(f32[8,512]{1,0:T(8,128)S(1)} %get-tuple-element.43), channel_id=1, source_target_pairs={{0,1},{1,0},{2,3},{3,2},{4,5},{5,4},{6,7},{7,6},{8,9},{9,8},{10,11... | collective-permute-start | bytes 49160 | tf_op jit(solution)/shard_map/ppermute | solution.py:441
  9.7 0.7 %collective-permute-done.from_low_x = f32[8,512]{1,0:T(8,128)S(1)} collective-permute-done((f32[8,512]{1,0:T(8,128)S(1)}, f32[8,512]{1,0:T(8,128)S(1)}, u32[]{:S(2)}, u32[]{:S(2)}) %collective-permute-start) | collective-permute-done | bytes 16416 | tf_op jit(solution)/shard_map/ppermute | solution.py:438
  10.4 0.0 collective-permute-done.1.from_y
  10.4 1.2 %collective-permute-done.2.from_high_x = f32[8,512]{1,0:T(8,128)S(1)} collective-permute-done((f32[8,512]{1,0:T(8,128)S(1)}, f32[8,512]{1,0:T(8,128)S(1)}, u32[]{:S(2)}, u32[]{:S(2)}) %collective-permute-start.2) | collective-permute-done | bytes 16416 | tf_op jit(solution)/shard_map/ppermute | solution.py:440
  11.6 0.0 collective-permute-done.3.from_core
  11.6 1.2 %finish.1 = (f32[256,512]{1,0:T(8,128)}, f32[256,512]{1,0:T(8,128)}, f32[256,512]{1,0:T(8,128)}, f32[256,512]{1,0:T(8,128)}) custom-call(f32[8,512]{1,0:T(8,128)S(1)} %collective-permute-done.from_low_x, f32[8,512]{1,0:T(8,128)S(1)} %collective-permute-done.1.from_y, ...), custom_call_target="tpu_custom_call", output_to_operand_aliasing={{0}: (11, {}), {1}: (12, {}), {2}: (13, {}), {3}: (14, {})} | custom-call | tf_op jit(solution)/shard_map/finish/pallas_call | solution.py:410
  (1 shorter events, 0.0 us)
Async XLA Ops:
  3.9 6.5 %collective-permute-start = (f32[8,512]{1,0:T(8,128)S(1)}, f32[8,512]{1,0:T(8,128)S(1)}, u32[]{:S(2)}, u32[]{:S(2)}) collective-permute-start(f32[8,512]{1,0:T(8,128)S(1)} %get-tuple-element.38), channel_id=1, source_target_pairs={{0,4},{4,8},{8,12},{12,16},{16,20},{20,24},{24,28},{28,0},{1,5},{5... | collective-permute-start | bytes 49160 | tf_op jit(solution)/shard_map/ppermute | solution.py:438
  5.0 5.4 %collective-permute-start.1 = (f32[8,512]{1,0:T(8,128)S(1)}, f32[8,512]{1,0:T(8,128)S(1)}, u32[]{:S(2)}, u32[]{:S(2)}) collective-permute-start(f32[8,512]{1,0:T(8,128)S(1)} %get-tuple-element.39), channel_id=1, source_target_pairs={{0,3},{1,2},{2,1},{3,0},{4,7},{5,6},{6,5},{7,4},{8,11},{9,10},{10,... | collective-permute-start | bytes 49160 | tf_op jit(solution)/shard_map/ppermute | solution.py:439
  7.6 4.0 %collective-permute-start.2 = (f32[8,512]{1,0:T(8,128)S(1)}, f32[8,512]{1,0:T(8,128)S(1)}, u32[]{:S(2)}, u32[]{:S(2)}) collective-permute-start(f32[8,512]{1,0:T(8,128)S(1)} %get-tuple-element.42), channel_id=1, source_target_pairs={{0,28},{4,0},{8,4},{12,8},{16,12},{20,16},{24,20},{28,24},{1,29},{... | collective-permute-start | bytes 49160 | tf_op jit(solution)/shard_map/ppermute | solution.py:440
  9.1 2.5 %collective-permute-start.3 = (f32[8,512]{1,0:T(8,128)S(1)}, f32[8,512]{1,0:T(8,128)S(1)}, u32[]{:S(2)}, u32[]{:S(2)}) collective-permute-start(f32[8,512]{1,0:T(8,128)S(1)} %get-tuple-element.43), channel_id=1, source_target_pairs={{0,1},{1,0},{2,3},{3,2},{4,5},{5,4},{6,7},{7,6},{8,9},{9,8},{10,11... | collective-permute-start | bytes 49160 | tf_op jit(solution)/shard_map/ppermute | solution.py:441

commit v3 on v2

--- a/solution.py
+++ b/solution.py
@@ -25,6 +25,7 @@
 
 ANY = pl.BlockSpec(memory_space=pl.ANY)
 VMEM = pl.BlockSpec(memory_space=pltpu.VMEM)
+LIMIT = pltpu.CompilerParams(vmem_limit_bytes=16 * 2**20)
 
 
 def right_sides(cells, axis):
@@ -104,8 +105,25 @@
             table_y[:, pl.ds(block * TILE, TILE)] = stack.astype(BF16)
 
 
+def low_goes_first():
+    next_chip_first = 2 * lax.axis_index("gx") < lax.axis_size("gx")
+    return next_chip_first == (lax.rem(lax.axis_index("gy"), 2) == 0)
+
+
+def trades_along_y():
+    gx, gy = lax.axis_size("gx"), lax.axis_size("gy")
+    next_chip = [(y, (y - 1) % gy if y % 2 == 0 else (y + 1) % gy) for y in range(gy)]
+    same_chip = [(y, y + 1 if y % 2 == 0 else y - 1) for y in range(gy)]
+    first, second = [], []
+    for x in range(gx):
+        orders = (next_chip, same_chip) if 2 * x < gx else (same_chip, next_chip)
+        for found, pairs in zip((first, second), orders):
+            found += [(x * gy + source, x * gy + target) for source, target in pairs]
+    return first, second
+
+
 def pack_kernel(
-    u_ref, to_high_x, to_low_x, to_y, to_core, u_near, near_low, near_high, k_ref, table_x, table_y, sems
+    u_ref, to_high_x, to_low_x, to_y_first, to_y_second, u_near, near_low, near_high, k_ref, table_x, table_y, sems
 ):
     rows, columns = u_ref.shape
     across = [pl.ds(0, TILE), pl.ds(columns - TILE, TILE)]
@@ -121,7 +139,7 @@
     ]
     for copy in copies:
         copy.start()
-    even = lax.rem(lax.axis_index("gy"), 2) == 0
+    low_first = low_goes_first()
     weights_low, weights_high = tail_weights(False), tail_weights(True)
     put_inverses(k_ref)
     put_side_tables(table_x, table_y)
@@ -134,8 +152,8 @@
     for lanes in tiles_of(rows):
         part = slice(lanes.start, lanes.start + lanes.size)
         to_low, to_high = message(low[:, part], False, weights_low), message(high[:, part], True, weights_high)
-        to_y[:, lanes] = jnp.where(even, to_low, to_high)
-        to_core[:, lanes] = jnp.where(even, to_high, to_low)
+        to_y_first[:, lanes] = jnp.where(low_first, to_low, to_high)
+        to_y_second[:, lanes] = jnp.where(low_first, to_high, to_low)
     for copy in copies[2:4]:
         copy.wait()
     for lanes in tiles_of(columns):
@@ -155,7 +173,7 @@
     return jnp.dot(a, b, preferred_element_type=F32)
 
 
-def solve_x(u_ref, k_ref, outs, strips, high_ref, rest_ref, solved_ref, sems):
+def solve_x(u_ref, k_ref, strips, solved_ref, high_ref, rest_ref):
     rows, columns = u_ref.shape
     at = lax.broadcasted_iota(jnp.int32, (rows, 1), 0)
     known = (at >= 2) & (at < rows - 2)
@@ -172,16 +190,9 @@
             solved_ref[s, :, lanes] = solved
             strips[s, 0, :, lanes] = solved[:EDGE]
             strips[s, 1, :, lanes] = solved[rows - EDGE :]
-    if rows > 2 * EDGE:
-        inner = pl.ds(EDGE, rows - 2 * EDGE)
-        copies = [pltpu.make_async_copy(solved_ref.at[s, inner], outs[s].at[inner], sems.at[s]) for s in range(2)]
-        for copy in copies:
-            copy.start()
-        return copies
-    return []
-
-
-def solve_y(u_ref, k_ref, outs, strips, high_ref, rest_ref, solved_ref, sems):
+
+
+def solve_y(u_ref, k_ref, strips, solved_ref, high_ref, rest_ref):
     rows, columns = u_ref.shape
     at = lax.broadcasted_iota(jnp.int32, (1, columns), 1)
     known = (at >= 2) & (at < columns - 2)
@@ -195,7 +206,6 @@
     count = max((columns - WINDOW) // TILE, 0) + 1
     tiles = columns // TILE
     step = min(rows, 128)
-    copies = []
     for s in range(2):
         upper, lower = k_ref[2 * s, :span, :span], k_ref[2 * s + 1, :span, :span]
         for i in range(rows // step):
@@ -213,51 +223,49 @@
                 else:
                     tile = jnp.where(left, windows[t - 1][:, TILE:], windows[t][:, :TILE])
                     solved_ref[s, lines, (t - 1) * TILE : t * TILE] = tile
-        if tiles > 2:
-            copies.append(pltpu.make_async_copy(solved_ref.at[s], outs[s].at[:, pl.ds(TILE, columns - 2 * TILE)], sems.at[s]))
-            copies[-1].start()
-    return copies
 
 
 def solves_x_early():
     return (lax.axis_index("gx") == 0) & (lax.axis_index("gy") < 2)
 
 
-def solves_y_early():
-    return lax.axis_index("gx") == 0
-
-
-def lead_x_kernel(u_ref, k_ref, *refs):
-    dx, dxx, strips_x, *scratch = refs[4:]
+def lead_kernel(u_ref, k_ref, *refs):
+    messages, passed, (strips_x, solved_x, high_ref, rest_ref) = refs[:4], refs[4:8], refs[8:]
+    for message_ref, passed_ref in zip(messages, passed):
+        passed_ref[...] = message_ref[...]
 
     @pl.when(solves_x_early())
     def _():
-        for copy in solve_x(u_ref, k_ref, (dx, dxx), strips_x, *scratch):
+        solve_x(u_ref, k_ref, strips_x, solved_x, high_ref, rest_ref)
+
+
+def interior_kernel(u_ref, k_ref, early_strips, early_solved, *refs):
+    strips_x, dx, dxx, strips_y, solved_y, high_ref, rest_ref, high_y, rest_y, solved_x, sems = refs
+    rows, columns = u_ref.shape
+
+    def inner_copies(source):
+        if rows <= 2 * EDGE:
+            return []
+        inner = pl.ds(EDGE, rows - 2 * EDGE)
+        return [pltpu.make_async_copy(source.at[s, inner], out.at[inner], sems.at[s]) for s, out in enumerate((dx, dxx))]
+
+    @pl.when(solves_x_early())
+    def _():
+        copies = inner_copies(early_solved)
+        for copy in copies:
+            copy.start()
+        strips_x[...] = early_strips[...]
+        solve_y(u_ref, k_ref, strips_y, solved_y, high_y, rest_y)
+        for copy in copies:
             copy.wait()
 
-
-def lead_y_kernel(u_ref, k_ref, *refs):
-    dy, dyy, strips_y, *scratch = refs[4:]
-
-    @pl.when(solves_y_early())
+    @pl.when(jnp.logical_not(solves_x_early()))
     def _():
-        for copy in solve_y(u_ref, k_ref, (dy, dyy), strips_y, *scratch):
-            copy.wait()
-
-
-def interior_kernel(u_ref, k_ref, *refs):
-    dx, dxx, strips_x, dy, dyy, strips_y, *scratch = refs[6:]
-    for_x, for_y = scratch[:4], scratch[4:]
-
-    @pl.when(solves_y_early() & jnp.logical_not(solves_x_early()))
-    def _():
-        for copy in solve_x(u_ref, k_ref, (dx, dxx), strips_x, *for_x):
-            copy.wait()
-
-    @pl.when(jnp.logical_not(solves_y_early()))
-    def _():
-        copies = solve_x(u_ref, k_ref, (dx, dxx), strips_x, *for_x)
-        copies += solve_y(u_ref, k_ref, (dy, dyy), strips_y, *for_y)
+        solve_x(u_ref, k_ref, strips_x, solved_x, high_ref, rest_ref)
+        copies = inner_copies(solved_x)
+        for copy in copies:
+            copy.start()
+        solve_y(u_ref, k_ref, strips_y, solved_y, high_y, rest_y)
         for copy in copies:
             copy.wait()
 
@@ -285,9 +293,9 @@
 
 
 def finish_kernel(
-    from_low_x, from_y, from_high_x, from_core, u_near, near_low, near_high, table_x, table_y, strips_x, strips_y, *refs
+    from_low_x, from_y_first, from_high_x, from_y_second, u_near, near_low, near_high, table_x, table_y, strips_x, strips_y, solved_y, *refs
 ):
-    dx, dxx, dy, dyy, done_x, done_y, sems = refs[4:]
+    dx, dxx, dy, dyy, done_x, done_y, sems = refs[2:]
     rows, columns = dx.shape
     started = []
 
@@ -296,10 +304,13 @@
         copy.start()
         started.append(copy)
 
-    even = lax.rem(lax.axis_index("gy"), 2) == 0
-    across, within = from_y[:, pl.ds(0, rows)], from_core[:, pl.ds(0, rows)]
-    from_low = jnp.where(even, across, within)
-    from_high = jnp.where(even, within, across)
+    if columns > 2 * TILE:
+        for s, out in enumerate((dy, dyy)):
+            send(solved_y.at[s], out.at[:, pl.ds(TILE, columns - 2 * TILE)])
+    low_first = low_goes_first()
+    first, second = from_y_first[:, pl.ds(0, rows)], from_y_second[:, pl.ds(0, rows)]
+    from_low = jnp.where(low_first, first, second)
+    from_high = jnp.where(low_first, second, first)
     terms = both_sides(from_low, from_high, near_low[...], near_high[...])
     row = lax.broadcasted_iota(jnp.int32, (8, 1), 0)
     stacked = jnp.zeros((8, rows), F32)
@@ -359,50 +370,46 @@
         in_specs=[ANY],
         out_specs=[VMEM] * 10,
         scratch_shapes=[pltpu.SemaphoreType.DMA((5,))],
-    )(u)
-
-
-def scratch_x(rows, columns):
-    return [pltpu.VMEM((2, rows, columns), BF16)] * 2 + [on_chip(2, rows, columns), pltpu.SemaphoreType.DMA((2,))]
-
-
-def scratch_y(rows, columns):
-    inner = max(columns - 2 * TILE, TILE)
-    return [pltpu.VMEM((2, rows, columns), BF16)] * 2 + [on_chip(2, rows, inner), pltpu.SemaphoreType.DMA((2,))]
+        compiler_params=LIMIT,
+    )(pltpu.with_memory_space_constraint(u, pltpu.HBM))
+
+
+def split_refs(rows, columns):
+    return [pltpu.VMEM((2, rows, columns), BF16)] * 2
 
 
 def shapes_x(rows, columns):
-    return (pltpu.HBM((rows, columns), F32),) * 2 + (on_chip(2, 2, EDGE, columns),)
-
-
-def shapes_y(rows, columns):
-    return (pltpu.HBM((rows, columns), F32),) * 2 + (on_chip(2, 2, rows, TILE),)
-
-
-def lead(kernel, name, u_near, inverses, shapes, scratch, passing):
+    return on_chip(2, 2, EDGE, columns), on_chip(2, rows, columns)
+
+
+def lead(u_near, inverses, messages):
+    size = u_near.shape
     return pl.pallas_call(
-        kernel,
-        name=name,
-        out_shape=tuple(on_chip(*a.shape) for a in passing) + shapes,
-        in_specs=[VMEM] * 4,
-        out_specs=[VMEM] * 2 + [ANY] * 2 + [VMEM],
-        input_output_aliases={2: 0, 3: 1},
-        scratch_shapes=scratch,
-    )(near(u_near), near(inverses), *(near(a) for a in passing))
-
-
-def interior(u_near, inverses, solved_x, solved_y):
-    size = u_near.shape
+        lead_kernel,
+        name="lead",
+        out_shape=tuple(on_chip(*a.shape) for a in messages) + shapes_x(*size),
+        in_specs=[VMEM] * 6,
+        out_specs=[VMEM] * 6,
+        scratch_shapes=split_refs(*size),
+        compiler_params=LIMIT,
+    )(near(u_near), near(inverses), *(near(a) for a in messages))
+
+
+def interior(u_near, inverses, early_strips, early_solved):
+    rows, columns = u_near.shape
+    strips_x, solved_x = shapes_x(rows, columns)
     return pl.pallas_call(
         interior_kernel,
         name="interior",
-        out_shape=shapes_x(*size) + shapes_y(*size),
-        in_specs=[VMEM] * 2 + ([ANY] * 2 + [VMEM]) * 2,
-        out_specs=([ANY] * 2 + [VMEM]) * 2,
-        input_output_aliases={2 + k: k for k in range(6)},
-        scratch_shapes=scratch_x(*size) + scratch_y(*size),
+        out_shape=(strips_x,)
+        + (pltpu.HBM(u_near.shape, F32),) * 2
+        + (on_chip(2, 2, rows, TILE), on_chip(2, rows, max(columns - 2 * TILE, TILE))),
+        in_specs=[VMEM] * 4,
+        out_specs=[VMEM] + [ANY] * 2 + [VMEM] * 2,
+        scratch_shapes=split_refs(rows, columns) * 2 + [solved_x, pltpu.SemaphoreType.DMA((2,))],
+        compiler_params=LIMIT,
         cost_estimate=pl.CostEstimate(flops=2 * 2**28, bytes_accessed=5 * 2**19, transcendentals=0),
-    )(near(u_near), near(inverses), *solved_x[:2], near(solved_x[2]), *solved_y[:2], near(solved_y[2]))
+    )(near(u_near), near(inverses), near(early_strips), near(early_solved))
 
 
 def finish(arrays, parts):
@@ -411,38 +418,34 @@
         finish_kernel,
         name="finish",
         out_shape=(pltpu.HBM(parts[0].shape, F32),) * 4,
-        in_specs=[VMEM] * 11 + [ANY] * 4,
+        in_specs=[VMEM] * 12 + [ANY] * 2,
         out_specs=[ANY] * 4,
-        input_output_aliases={11 + k: k for k in range(4)},
+        input_output_aliases={12: 0, 13: 1},
         scratch_shapes=[
             on_chip(2, 2, EDGE, columns),
             on_chip(2, 2, rows, TILE),
-            pltpu.SemaphoreType.DMA((8,)),
+            pltpu.SemaphoreType.DMA((10,)),
         ],
+        compiler_params=LIMIT,
     )(*(near(a) for a in arrays), *parts)
 
 
 def local(velocity):
-    to_high_x, to_low_x, to_y, to_core, u_near, near_low, near_high, inverses, *tables = pack(velocity[0])
-    size = u_near.shape
-    to_high_x, to_y, *solved_x = lead(
-        lead_x_kernel, "lead_x", u_near, inverses, shapes_x(*size), scratch_x(*size), (to_high_x, to_y)
+    to_high_x, to_low_x, to_y_first, to_y_second, u_near, near_low, near_high, inverses, *tables = pack(velocity[0])
+    to_high_x, to_y_first, to_low_x, to_y_second, strips_x, solved_x = lead(
+        u_near, inverses, (to_high_x, to_y_first, to_low_x, to_y_second)
     )
-    to_low_x, to_core, *solved_y = lead(
-        lead_y_kernel, "lead_y", u_near, inverses, shapes_y(*size), scratch_y(*size), (to_low_x, to_core)
-    )
-    gx, gy = lax.axis_size("gx"), lax.axis_size("gy")
-    across = [(i, (i - 1) % gy) if i % 2 == 0 else (i, (i + 1) % gy) for i in range(gy)]
-    within = [(i, i + 1) if i % 2 == 0 else (i, i - 1) for i in range(gy)]
+    gx = lax.axis_size("gx")
+    first, second = trades_along_y()
     messages = (
         lax.ppermute(to_high_x, "gx", [(i, (i + 1) % gx) for i in range(gx)]),
-        lax.ppermute(to_y, "gy", across),
+        lax.ppermute(to_y_first, ("gx", "gy"), first),
         lax.ppermute(to_low_x, "gx", [(i, (i - 1) % gx) for i in range(gx)]),
-        lax.ppermute(to_core, "gy", within),
+        lax.ppermute(to_y_second, ("gx", "gy"), second),
     )
-    dx, dxx, strips_x, dy, dyy, strips_y = interior(u_near, inverses, solved_x, solved_y)
-    arrays = (*messages, u_near, near_low, near_high, *tables, strips_x, strips_y)
-    dx, dxx, dy, dyy = finish(arrays, (dx, dxx, dy, dyy))
+    strips_x, dx, dxx, strips_y, solved_y = interior(u_near, inverses, strips_x, solved_x)
+    arrays = (*messages, u_near, near_low, near_high, *tables, strips_x, strips_y, solved_y)
+    dx, dxx, dy, dyy = finish(arrays, (dx, dxx))
     return tuple(o[None] for o in (dx, dy, dxx, dyy))
 
 

time: 13 us -> 11.4 us (0.88)
  the two profiles are of different devices: /device:TPU:0 before, /device:TPU:5 now
where the time goes in v3:
time: 11.4 us; the launch traced here: 11.2 us
  starting transfers between devices  5.45 us (48%)
  Pallas kernels  5.1 us (45%)
  between operations  0.69 us (6%)
    ppermute x1, starting transfers between devices, local(): lax.ppermute(to_low_x, 'gx', [(i, (i - 1) % gx) for i in range(gx)])  2.84 us
    pallas_call x1, Pallas kernels, interior(): pl.pallas_call(interior_kernel, name='interior', out_shape=(strips_x,) +...  2.52 us
    pallas_call x1, Pallas kernels, pack(): pl.pallas_call(pack_kernel, name='pack', out_shape=(on_chip(MESSAGE, colu...  1.3 us
    ppermute x1, starting transfers between devices, local(): lax.ppermute(to_high_x, 'gx', [(i, (i + 1) % gx) for i in range(gx)])  1.26 us
    pallas_call x1, Pallas kernels, finish(): pl.pallas_call(finish_kernel, name='finish', out_shape=(pltpu.HBM(parts[0...  1.26 us
    ppermute x1, starting transfers between devices, local(): lax.ppermute(to_y_first, ('gx', 'gy'), first)  1.07 us
    ppermute x1, starting transfers between devices, local(): lax.ppermute(to_y_second, ('gx', 'gy'), second)  0.28 us
  transfers between devices with their start and end apart: 4, of which 0 were waited for; matrix products, arithmetic and copies ran while one was open for 0% of the time, Pallas kernels for 22%

profile of v3, /device:TPU:5, one launch (start us, length us, event | category | flops | bytes accessed | tf_op | source)
XLA Modules:
  0.0 11.2 jit_solution(11346261422385808603)
XLA Ops:
  0.6 1.3 %pack.1 = (f32[8,512]{1,0:T(8,128)S(1)}, f32[8,512]{1,0:T(8,128)S(1)}, f32[8,512]{1,0:T(8,128)S(1)}, f32[8,512]{1,0:T(8,128)S(1)}, f32[256,512]{1,0:T(8,128)S(1)...) custom-call(f32[256,512]{1,0:T(8,128)} %bitcast.5), custom_call_target="tpu_custom_call" | custom-call | tf_op jit(solution)/shard_map/pack/pallas_call | solution.py:355
  2.0 1.3 %collective-permute-start = (f32[8,512]{1,0:T(8,128)S(1)}, f32[8,512]{1,0:T(8,128)S(1)}, u32[]{:S(2)}, u32[]{:S(2)}) collective-permute-start(f32[8,512]{1,0:T(8,128)S(1)} %get-tuple-element.35), channel_id=1, source_target_pairs={{0,4},{4,8},{8,12},{12,16},{16,20},{20,24},{24,28},{28,0},{1,5},{5... | collective-permute-start | bytes 49160 | tf_op jit(solution)/shard_map/ppermute | solution.py:441
  3.2 1.1 %collective-permute-start.1 = (f32[8,512]{1,0:T(8,128)S(1)}, f32[8,512]{1,0:T(8,128)S(1)}, u32[]{:S(2)}, u32[]{:S(2)}) collective-permute-start(f32[8,512]{1,0:T(8,128)S(1)} %get-tuple-element.36), channel_id=1, source_target_pairs={{0,3},{1,2},{2,1},{3,0},{4,7},{5,6},{6,5},{7,4},{8,11},{9,10},{10,... | collective-permute-start | bytes 49160 | tf_op jit(solution)/shard_map/ppermute | solution.py:442
  4.3 2.8 %collective-permute-start.2 = (f32[8,512]{1,0:T(8,128)S(1)}, f32[8,512]{1,0:T(8,128)S(1)}, u32[]{:S(2)}, u32[]{:S(2)}) collective-permute-start(f32[8,512]{1,0:T(8,128)S(1)} %get-tuple-element.37), channel_id=1, source_target_pairs={{0,28},{4,0},{8,4},{12,8},{16,12},{20,16},{24,20},{28,24},{1,29},{... | collective-permute-start | bytes 49160 | tf_op jit(solution)/shard_map/ppermute | solution.py:443
  7.1 0.3 %collective-permute-start.3 = (f32[8,512]{1,0:T(8,128)S(1)}, f32[8,512]{1,0:T(8,128)S(1)}, u32[]{:S(2)}, u32[]{:S(2)}) collective-permute-start(f32[8,512]{1,0:T(8,128)S(1)} %get-tuple-element.38), channel_id=1, source_target_pairs={{0,1},{1,0},{2,3},{3,2},{4,5},{5,4},{6,7},{7,6},{8,9},{9,8},{10,11... | collective-permute-start | bytes 49160 | tf_op jit(solution)/shard_map/ppermute | solution.py:444
  7.4 2.5 %interior.1 = (f32[2,2,32,512]{3,2,1,0:T(8,128)S(1)}, f32[256,512]{1,0:T(8,128)}, f32[256,512]{1,0:T(8,128)}, f32[2,2,256,128]{3,2,1,0:T(8,128)S(1)}, f32[2,256,256]{2,1,0:T(8,128)S(1)}) custom-call(f32[256,512]{1,0:T(8,128)S(1)} %get-tuple-element.29.u_ref.u_near, bf16[4,256,256]{2,1,0:T(8,128)(2,1)S(1)} %get-tuple-element.30.k_ref, ...), custom_call_target="tpu_custom_call" | custom-call | flops 536870912 | bytes 2621440 | tf_op jit(solution)/shard_map/interior/pallas_call | solution.py:401
  9.9 0.0 collective-permute-done.from_low_x
  10.0 0.0 collective-permute-done.1.from_y_first
  10.0 0.0 collective-permute-done.2.from_high_x
  10.0 0.0 collective-permute-done.3.from_y_second
  10.0 1.3 %finish.1 = (f32[256,512]{1,0:T(8,128)}, f32[256,512]{1,0:T(8,128)}, f32[256,512]{1,0:T(8,128)}, f32[256,512]{1,0:T(8,128)}) custom-call(f32[8,512]{1,0:T(8,128)S(1)} %collective-permute-done.from_low_x, f32[8,512]{1,0:T(8,128)S(1)} %collective-permute-done.1.from_y_first, ...), custom_call_target="tpu_custom_call", output_to_operand_aliasing={{0}: (12, {}), {1}: (13, {})} | custom-call | tf_op jit(solution)/shard_map/finish/pallas_call | solution.py:417
  (1 shorter events, 0.0 us)
Async XLA Ops:
  2.0 8.0 %collective-permute-start = (f32[8,512]{1,0:T(8,128)S(1)}, f32[8,512]{1,0:T(8,128)S(1)}, u32[]{:S(2)}, u32[]{:S(2)}) collective-permute-start(f32[8,512]{1,0:T(8,128)S(1)} %get-tuple-element.35), channel_id=1, source_target_pairs={{0,4},{4,8},{8,12},{12,16},{16,20},{20,24},{24,28},{28,0},{1,5},{5... | collective-permute-start | bytes 49160 | tf_op jit(solution)/shard_map/ppermute | solution.py:441
  3.2 6.7 %collective-permute-start.1 = (f32[8,512]{1,0:T(8,128)S(1)}, f32[8,512]{1,0:T(8,128)S(1)}, u32[]{:S(2)}, u32[]{:S(2)}) collective-permute-start(f32[8,512]{1,0:T(8,128)S(1)} %get-tuple-element.36), channel_id=1, source_target_pairs={{0,3},{1,2},{2,1},{3,0},{4,7},{5,6},{6,5},{7,4},{8,11},{9,10},{10,... | collective-permute-start | bytes 49160 | tf_op jit(solution)/shard_map/ppermute | solution.py:442
  4.3 5.7 %collective-permute-start.2 = (f32[8,512]{1,0:T(8,128)S(1)}, f32[8,512]{1,0:T(8,128)S(1)}, u32[]{:S(2)}, u32[]{:S(2)}) collective-permute-start(f32[8,512]{1,0:T(8,128)S(1)} %get-tuple-element.37), channel_id=1, source_target_pairs={{0,28},{4,0},{8,4},{12,8},{16,12},{20,16},{24,20},{28,24},{1,29},{... | collective-permute-start | bytes 49160 | tf_op jit(solution)/shard_map/ppermute | solution.py:443
  7.1 2.8 %collective-permute-start.3 = (f32[8,512]{1,0:T(8,128)S(1)}, f32[8,512]{1,0:T(8,128)S(1)}, u32[]{:S(2)}, u32[]{:S(2)}) collective-permute-start(f32[8,512]{1,0:T(8,128)S(1)} %get-tuple-element.38), channel_id=1, source_target_pairs={{0,1},{1,0},{2,3},{3,2},{4,5},{5,4},{6,7},{7,6},{8,9},{9,8},{10,11... | collective-permute-start | bytes 49160 | tf_op jit(solution)/shard_map/ppermute | solution.py:444

commit v4 on v3

v4 whole, which is shorter than its diff:
```python
import math

import jax
import jax.numpy as jnp
from jax import lax
from jax.experimental import pallas as pl
from jax.experimental.pallas import tpu as pltpu
from jax.sharding import PartitionSpec as P

F32 = jnp.float32
BF16 = jnp.bfloat16

COUPLINGS = (1.0 / 3.0, 2.0 / 11.0)
CENTRES = (7.0 / 9.0, 12.0 / 11.0 + 6.0 / 44.0)
BESIDES = (1.0 / 36.0, 3.0 / 44.0)

ROOTS = tuple(math.sqrt(1.0 - 4.0 * a * a) for a in COUPLINGS)
RATIOS = tuple((root - 1.0) / (2.0 * a) for a, root in zip(COUPLINGS, ROOTS))
SCALES = tuple((c - b / a) / root for a, b, c, root in zip(COUPLINGS, BESIDES, CENTRES, ROOTS))
PEAKS = tuple((c + 2.0 * b * r) / root - h for b, c, r, root, h in zip(BESIDES, CENTRES, RATIOS, ROOTS, SCALES))

WINDOW = 256
TILE = 128
STRIP = 32
EDGE = 24
REACH = 64
MESSAGE = 8

ANY = pl.BlockSpec(memory_space=pl.ANY)
VMEM = pl.BlockSpec(memory_space=pltpu.VMEM)
LIMIT = pltpu.CompilerParams(vmem_limit_bytes=16 * 2**20)


def differences(cells, axis):
    length = cells.shape[axis]
    here = pltpu.roll(cells, length - 1, axis) - cells
    before = pltpu.roll(here, 1, axis)
    return here + before, here - before


def powers(ratio, exponent):
    product = jnp.where(exponent < REACH, F32(1.0), F32(0.0))
    for bit in range(REACH.bit_length() - 1):
        factor = jnp.where((exponent & (1 << bit)) != 0, F32(ratio ** (1 << bit)), F32(1.0))
        product = product * factor
    return product


def tail_weights(high):
    at = lax.broadcasted_iota(jnp.int32, (STRIP, TILE), 0)
    known = (at >= 1) & (at < STRIP - 1)
    exponent = (STRIP - 2 - at) if high else (at - 1)
    return [jnp.where(known, powers(ratio, exponent), 0.0) for ratio in RATIOS]


def message(strip, high, weights):
    tails = [
        jnp.sum(part * weight[:, : strip.shape[1]], axis=0, keepdims=True)
        for part, weight in zip(differences(strip, 0), weights)
    ]
    near = pltpu.roll(strip[STRIP - 8 :], 2, 0) if high else strip[:8]
    row = lax.broadcasted_iota(jnp.int32, near.shape, 0)
    return jnp.where(row < 2, near, jnp.where(row == 2, tails[0], tails[1]))


def tiles_of(length):
    step = min(length, TILE)
    return [pl.ds(k * step, step) for k in range(length // step)]


def halves(value):
    upper = value.astype(BF16).astype(F32)
    return upper, value - upper


def put_inverses(k_ref):
    i = lax.broadcasted_iota(jnp.int32, (TILE, TILE), 0)
    j = lax.broadcasted_iota(jnp.int32, (TILE, TILE), 1)
    blocks = WINDOW // TILE
    for s in range(2):
        for apart in range(1 - blocks, blocks):
            distance = jnp.abs(j - i + apart * TILE)
            weights = SCALES[s] * powers(RATIOS[s], distance)
            if apart == 0:
                weights = jnp.where(distance == 0, F32(SCALES[s] + PEAKS[s]), weights)
            upper, lower = halves(weights)
            for p, part in enumerate((upper, lower)):
                for first in range(blocks):
                    if 0 <= first + apart < blocks:
                        at_i, at_j = pl.ds(first * TILE, TILE), pl.ds((first + apart) * TILE, TILE)
                        k_ref[2 * s + p, at_i, at_j] = part.astype(BF16)


def put_side_tables(table_x, table_y):
    at = lax.broadcasted_iota(jnp.int32, (EDGE, TILE), 0)
    lane = lax.broadcasted_iota(jnp.int32, (8, TILE), 1)
    row = lax.broadcasted_iota(jnp.int32, (8, TILE), 0)
    for s in range(2):
        for side in range(2):
            table_x[s, side] = powers(RATIOS[s], (EDGE - 1 - at) if side else at)
            within = (TILE - 1 - lane) if side else lane
            first = 4 * side + 2 * s
            lines = jnp.where(row == first, powers(RATIOS[s], within), 0.0)
            lines = jnp.where((row == first + 1) & (within == 0), 1.0, lines)
            upper, lower = halves(lines)
            stack = jnp.concatenate([upper, upper, lower, jnp.zeros_like(upper)], axis=0)
            block = 2 * s + side
            table_y[:, pl.ds(block * TILE, TILE)] = stack.astype(BF16)


def low_goes_first():
    next_chip_first = 2 * lax.axis_index("gx") < lax.axis_size("gx")
    return next_chip_first == (lax.rem(lax.axis_index("gy"), 2) == 0)


def trades_along_y():
    gx, gy = lax.axis_size("gx"), lax.axis_size("gy")
    next_chip = [(y, (y - 1) % gy if y % 2 == 0 else (y + 1) % gy) for y in range(gy)]
    same_chip = [(y, y + 1 if y % 2 == 0 else y - 1) for y in range(gy)]
    first, second = [], []
    for x in range(gx):
        orders = (next_chip, same_chip) if 2 * x < gx else (same_chip, next_chip)
        for found, pairs in zip((first, second), orders):
            found += [(x * gy + source, x * gy + target) for source, target in pairs]
    return first, second


def pack_kernel(
    u_ref, to_high_x, to_low_x, to_y_first, to_y_second, u_near, near_low, near_high, k_ref, table_x, table_y, sems
):
    rows, columns = u_ref.shape
    across = [pl.ds(0, TILE), pl.ds(columns - TILE, TILE)]
    pieces = [(pl.ds(0, rows), lanes) for lanes in across]
    order = (2, 3, 0, 1, 4)
    if columns > 2 * TILE:
        middle = pl.ds(TILE, columns - 2 * TILE)
        pieces += [(pl.ds(0, STRIP), middle), (pl.ds(rows - STRIP, STRIP), middle)]
        if rows > 2 * STRIP:
            pieces.append((pl.ds(STRIP, rows - 2 * STRIP), middle))
    copies = [
        pltpu.make_async_copy(u_ref.at[lines, lanes], u_near.at[lines, lanes], sems.at[k])
        for k, (lines, lanes) in enumerate(pieces)
    ]
    for k in order:
        if k < len(copies):
            copies[k].start()
    low_first = low_goes_first()
    weights_low, weights_high = tail_weights(False), tail_weights(True)
    put_inverses(k_ref)
    put_side_tables(table_x, table_y)
    def put_x(lanes):
        to_low_x[:, lanes] = message(u_near[pl.ds(0, STRIP), lanes], False, weights_low)
        to_high_x[:, lanes] = message(u_near[pl.ds(rows - STRIP, STRIP), lanes], True, weights_high)

    for copy in copies[2:4]:
        copy.wait()
    for lanes in tiles_of(columns)[1:-1]:
        put_x(lanes)
    low, high = [], []
    for k in range(2):
        copies[k].wait()
        put_x(across[k])
        turned = u_near[:, across[k]].T
        side = turned[TILE - STRIP :] if k else turned[:STRIP]
        (near_high if k else near_low)[...] = side[STRIP - 8 :] if k else side[:8]
        for lanes in tiles_of(rows):
            part = side[:, lanes.start : lanes.start + lanes.size]
            (high if k else low).append(message(part, k == 1, (weights_low, weights_high)[k]))
    for lanes, to_low, to_high in zip(tiles_of(rows), low, high):
        to_y_first[:, lanes] = jnp.where(low_first, to_low, to_high)
        to_y_second[:, lanes] = jnp.where(low_first, to_high, to_low)
    for copy in copies[4:]:
        copy.wait()


def only_known(rhs, axis):
    length, step = rhs.shape[axis], 8 if axis == 0 else TILE
    at = lax.broadcasted_iota(jnp.int32, [step if k == axis else 1 for k in range(2)], axis)
    first, middle, last = (
        lax.slice_in_dim(rhs, low, high, axis=axis) for low, high in ((0, step), (step, length - step), (length - step, length))
    )
    parts = [jnp.where(at >= 1, first, 0.0), middle, jnp.where(at < step - 1, last, 0.0)]
    return jnp.concatenate([p for p in parts if p.shape[axis] > 0], axis=axis)


def product(a, b):
    dot = lambda p, q: jnp.dot(p, q, preferred_element_type=F32)
    return dot(a[0], b[0]) + dot(a[1], b[0]) + dot(a[0], b[1])


def split(value):
    upper = value.astype(BF16)
    return upper, (value - upper.astype(F32)).astype(BF16)


def solve_x(u_ref, k_ref, strips, solved_ref):
    rows, columns = u_ref.shape
    span = min(columns, WINDOW)
    for j in range(columns // span):
        tiles = [differences(u_ref[:, pl.ds(j * span + t.start, t.size)], 0) for t in tiles_of(span)]
        lanes = pl.ds(j * span, span)
        for s in range(2):
            inverse = k_ref[2 * s, :rows, :rows], k_ref[2 * s + 1, :rows, :rows]
            rhs = jnp.concatenate([only_known(tile[s], 0) for tile in tiles], axis=1)
            solved = product(inverse, split(rhs))
            solved_ref[s, :, lanes] = solved
            strips[s, 0, :, lanes] = solved[:EDGE]
            strips[s, 1, :, lanes] = solved[rows - EDGE :]


def solve_y(u_ref, k_ref, strips, solved_ref):
    rows, columns = u_ref.shape
    span = min(columns, WINDOW)
    lane = lax.broadcasted_iota(jnp.int32, (1, TILE), 1)
    step = min(rows, 64)
    both = [differences(u_ref[pl.ds(i * step, step), :], 1) for i in range(rows // step)]
    for s in range(2):
        inverse = k_ref[2 * s, :span, :span], k_ref[2 * s + 1, :span, :span]
        values = jnp.concatenate([only_known(piece[s], 1) for piece in both], axis=0)
        rhs = split(values)
        count = columns // span
        stacked = [jnp.concatenate([part[:, w * span : (w + 1) * span] for w in range(count)], axis=0) for part in rhs]
        solved = product(stacked, inverse)
        tiles = [solved[w * rows : (w + 1) * rows, t.start : t.start + t.size] for w in range(count) for t in tiles_of(span)]
        per = span // TILE
        added = {}
        for w in range(1, count):
            edge = w * span
            before = tiles[w * per - 1][:, TILE - 1 :] - PEAKS[s] * values[:, edge - 1 : edge]
            after = tiles[w * per][:, :1] - PEAKS[s] * values[:, edge : edge + 1]
            added[w * per] = before * powers(RATIOS[s], lane + 1)
            added[w * per - 1] = after * powers(RATIOS[s], TILE - lane)
        for t, value in added.items():
            tiles[t] = tiles[t] + value
        strips[s, 0] = tiles[0]
        strips[s, 1] = tiles[-1]
        for t in range(1, len(tiles) - 1):
            solved_ref[s, :, pl.ds((t - 1) * TILE, TILE)] = tiles[t]


def solves_x_early():
    return (lax.axis_index("gx") == 0) & (lax.axis_index("gy") < 2)


def lead_kernel(u_ref, k_ref, *refs):
    messages, passed, (strips_x, solved_x) = refs[:4], refs[4:8], refs[8:]
    for message_ref, passed_ref in zip(messages, passed):
        passed_ref[...] = message_ref[...]

    @pl.when(solves_x_early())
    def _():
        solve_x(u_ref, k_ref, strips_x, solved_x)


def interior_kernel(u_ref, k_ref, early_strips, early_solved, *refs):
    strips_x, dx, dxx, strips_y, solved_y, solved_x, sems = refs
    rows, columns = u_ref.shape

    def inner_copies(source):
        if rows <= 2 * EDGE:
            return []
        inner = pl.ds(EDGE, rows - 2 * EDGE)
        return [pltpu.make_async_copy(source.at[s, inner], out.at[inner], sems.at[s]) for s, out in enumerate((dx, dxx))]

    @pl.when(solves_x_early())
    def _():
        copies = inner_copies(early_solved)
        for copy in copies:
            copy.start()
        strips_x[...] = early_strips[...]
        solve_y(u_ref, k_ref, strips_y, solved_y)
        for copy in copies:
            copy.wait()

    @pl.when(jnp.logical_not(solves_x_early()))
    def _():
        solve_x(u_ref, k_ref, strips_x, solved_x)
        copies = inner_copies(solved_x)
        for copy in copies:
            copy.start()
        solve_y(u_ref, k_ref, strips_y, solved_y)
        for copy in copies:
            copy.wait()


def side_terms(around, tails, high):
    found = []
    for s, part in enumerate(differences(around, 0)):
        nearest, outer = (part[1:2], part[2:3]) if high else (part[2:3], part[1:2])
        total = nearest + RATIOS[s] * (outer + RATIOS[s] * tails[s])
        found.append((SCALES[s] * total, PEAKS[s] * nearest))
    return found


def both_sides(from_low, from_high, own_low, own_high):
    row = lax.broadcasted_iota(jnp.int32, own_low.shape, 0)
    low = jnp.where(row < 2, from_low, pltpu.roll(own_low, 2, 0))
    high = jnp.where(row < 2, pltpu.roll(own_high, 2, 0), pltpu.roll(from_high, 2, 0))
    tails = lambda m: (m[2:3], m[3:4])
    return side_terms(low, tails(from_low), False), side_terms(high, tails(from_high), True)


def finish_kernel(
    from_low_x, from_y_first, from_high_x, from_y_second, u_near, near_low, near_high, table_x, table_y, strips_x, strips_y, solved_y, *refs
):
    dx, dxx, dy, dyy, done_x, done_y, sems = refs[2:]
    rows, columns = dx.shape
    started = []

    def send(source, target):
        copy = pltpu.make_async_copy(source, target, sems.at[len(started)])
        copy.start()
        started.append(copy)

    if columns > 2 * TILE:
        for s, out in enumerate((dy, dyy)):
            send(solved_y.at[s], out.at[:, pl.ds(TILE, columns - 2 * TILE)])
    step = min(columns, TILE)
    row = lax.broadcasted_iota(jnp.int32, (8, 1), 0)
    tiles = tiles_of(columns)
    own = lambda start, lanes: u_near[pl.ds(start, 8), lanes]
    for lanes in tiles:
        terms = both_sides(from_low_x[:, lanes], from_high_x[:, lanes], own(0, lanes), own(rows - 8, lanes))
        for s in range(2):
            for side in range(2):
                near, first = terms[side][s]
                extra = near * table_x[s, side, :, :step]
                first = jnp.where(row == (7 if side else 0), first, 0.0)
                if side:
                    extra = jnp.concatenate([extra[: EDGE - 8], extra[EDGE - 8 :] + first], axis=0)
                else:
                    extra = jnp.concatenate([extra[:8] + first, extra[8:]], axis=0)
                done_x[s, side, :, lanes] = strips_x[s, side, :, lanes] + extra
    for s, out in enumerate((dx, dxx)):
        for side in range(2):
            send(done_x.at[s, side], out.at[pl.ds(side * (rows - EDGE), EDGE)])

    low_first = low_goes_first()
    for lines in tiles_of(rows):
        first, second = from_y_first[:, lines], from_y_second[:, lines]
        from_low, from_high = jnp.where(low_first, first, second), jnp.where(low_first, second, first)
        terms = both_sides(from_low, from_high, near_low[:, lines], near_high[:, lines])
        stacked = jnp.zeros((8, lines.size), F32)
        for side in range(2):
            for s in range(2):
                for which in range(2):
                    stacked = jnp.where(row == 4 * side + 2 * s + which, terms[side][s][which], stacked)
        upper, lower = halves(stacked)
        factors = jnp.concatenate([upper, lower, upper, jnp.zeros_like(upper)], axis=0).astype(BF16)
        added = lax.dot_general(factors, table_y[...], (((0,), (0,)), ((), ())), preferred_element_type=F32)
        for s, out in enumerate((dy, dyy)):
            for side in range(2):
                block = 2 * s + side
                done_y[s, side, lines] = strips_y[s, side, lines] + added[:, block * TILE : (block + 1) * TILE]
                send(done_y.at[s, side, lines], out.at[lines, pl.ds(side * (columns - TILE), TILE)])
    for copy in started:
        copy.wait()


def on_chip(*shape):
    return pltpu.VMEM(shape, F32)


def near(array):
    return pltpu.with_memory_space_constraint(array, pltpu.VMEM)


def pack(u):
    rows, columns = u.shape
    wide = max(rows, columns)
    return pl.pallas_call(
        pack_kernel,
        name="pack",
        out_shape=(
            on_chip(MESSAGE, columns),
            on_chip(MESSAGE, columns),
            on_chip(MESSAGE, wide),
            on_chip(MESSAGE, wide),
            on_chip(rows, columns),
            on_chip(8, rows),
            on_chip(8, rows),
            pltpu.VMEM((4, WINDOW, WINDOW), BF16),
            on_chip(2, 2, EDGE, TILE),
            pltpu.VMEM((32, 4 * TILE), BF16),
        ),
        in_specs=[ANY],
        out_specs=[VMEM] * 10,
        scratch_shapes=[pltpu.SemaphoreType.DMA((5,))],
        compiler_params=LIMIT,
    )(pltpu.with_memory_space_constraint(u, pltpu.HBM))


def shapes_x(rows, columns):
    return on_chip(2, 2, EDGE, columns), on_chip(2, rows, columns)


def lead(u_near, inverses, messages):
    size = u_near.shape
    return pl.pallas_call(
        lead_kernel,
        name="lead",
        out_shape=tuple(on_chip(*a.shape) for a in messages) + shapes_x(*size),
        in_specs=[VMEM] * 6,
        out_specs=[VMEM] * 6,
        compiler_params=LIMIT,
    )(near(u_near), near(inverses), *(near(a) for a in messages))


def interior(u_near, inverses, early_strips, early_solved):
    rows, columns = u_near.shape
    strips_x, solved_x = shapes_x(rows, columns)
    return pl.pallas_call(
        interior_kernel,
        name="interior",
        out_shape=(strips_x,)
        + (pltpu.HBM(u_near.shape, F32),) * 2
        + (on_chip(2, 2, rows, TILE), on_chip(2, rows, max(columns - 2 * TILE, TILE))),
        in_specs=[VMEM] * 4,
        out_specs=[VMEM] + [ANY] * 2 + [VMEM] * 2,
        scratch_shapes=[solved_x, pltpu.SemaphoreType.DMA((2,))],
        compiler_params=LIMIT,
        cost_estimate=pl.CostEstimate(flops=2 * 2**28, bytes_accessed=5 * 2**19, transcendentals=0),
    )(near(u_near), near(inverses), near(early_strips), near(early_solved))


def finish(arrays, parts):
    rows, columns = parts[0].shape
    return pl.pallas_call(
        finish_kernel,
        name="finish",
        out_shape=(pltpu.HBM(parts[0].shape, F32),) * 4,
        in_specs=[VMEM] * 12 + [ANY] * 2,
        out_specs=[ANY] * 4,
        input_output_aliases={12: 0, 13: 1},
        scratch_shapes=[
            on_chip(2, 2, EDGE, columns),
            on_chip(2, 2, rows, TILE),
            pltpu.SemaphoreType.DMA((6 + 4 * len(tiles_of(rows)),)),
        ],
        compiler_params=LIMIT,
    )(*(near(a) for a in arrays), *parts)


def local(velocity):
    to_high_x, to_low_x, to_y_first, to_y_second, u_near, near_low, near_high, inverses, *tables = pack(velocity[0])
    to_high_x, to_y_first, to_low_x, to_y_second, strips_x, solved_x = lead(
        u_near, inverses, (to_high_x, to_y_first, to_low_x, to_y_second)
    )
    gx = lax.axis_size("gx")
    first, second = trades_along_y()
    messages = (
        lax.ppermute(to_high_x, "gx", [(i, (i + 1) % gx) for i in range(gx)]),
        lax.ppermute(to_y_first, ("gx", "gy"), first),
        lax.ppermute(to_low_x, "gx", [(i, (i - 1) % gx) for i in range(gx)]),
        lax.ppermute(to_y_second, ("gx", "gy"), second),
    )
    strips_x, dx, dxx, strips_y, solved_y = interior(u_near, inverses, strips_x, solved_x)
    arrays = (*messages, u_near, near_low, near_high, *tables, strips_x, strips_y, solved_y)
    dx, dxx, dy, dyy = finish(arrays, (dx, dxx))
    return tuple(o[None] for o in (dx, dy, dxx, dyy))


def solution(mesh):
    placed = P(None, "gx", "gy")
    return jax.shard_map(local, mesh=mesh, in_specs=(placed,), out_specs=(placed,) * 4, check_vma=False)
```

time: 11.4 us -> 11 us (0.965)
  the two profiles are of different devices: /device:TPU:5 before, /device:TPU:0 now
where the time goes in v4:
time: 11 us; the launch traced here: 10.8 us
  starting transfers between devices  5.7 us (52%)
  Pallas kernels  4.01 us (36%)
  between operations  0.66 us (6%)
  waiting for transfers between devices  0.45 us (4%)
    ppermute x1, starting transfers between devices, local(): lax.ppermute(to_low_x, 'gx', [(i, (i - 1) % gx) for i in range(gx)])  2.5 us
    ppermute x1, starting transfers between devices, local(): lax.ppermute(to_high_x, 'gx', [(i, (i + 1) % gx) for i in range(gx)])  2.35 us
    pallas_call x1, Pallas kernels, pack(): pl.pallas_call(pack_kernel, name='pack', out_shape=(on_chip(MESSAGE, colu...  1.21 us
    pallas_call x1, Pallas kernels, finish(): pl.pallas_call(finish_kernel, name='finish', out_shape=(pltpu.HBM(parts[0...  1.19 us
    pallas_call x1, Pallas kernels, interior(): pl.pallas_call(interior_kernel, name='interior', out_shape=(strips_x,) +...  0.95 us
    ppermute x1, starting transfers between devices, local(): lax.ppermute(to_y_first, ('gx', 'gy'), first)  0.68 us
    pallas_call x1, Pallas kernels, lead(): pl.pallas_call(lead_kernel, name='lead', out_shape=tuple((on_chip(*a.shap...  0.66 us
    ppermute x1, waiting for transfers between devices, local(): lax.ppermute(to_high_x, 'gx', [(i, (i + 1) % gx) for i in range(gx)])  0.45 us
  transfers between devices with their start and end apart: 4, of which 1 were waited for; matrix products, arithmetic and copies ran while one was open for 0% of the time, Pallas kernels for 9%

profile of v4, /device:TPU:0, one launch (start us, length us, event | category | flops | bytes accessed | tf_op | source)
XLA Modules:
  0.0 10.8 jit_solution(5134750630684439825)
XLA Ops:
  0.6 1.2 %pack.1 = (f32[8,512]{1,0:T(8,128)S(1)}, f32[8,512]{1,0:T(8,128)S(1)}, f32[8,512]{1,0:T(8,128)S(1)}, f32[8,512]{1,0:T(8,128)S(1)}, f32[256,512]{1,0:T(8,128)S(1)...) custom-call(f32[256,512]{1,0:T(8,128)} %bitcast.5), custom_call_target="tpu_custom_call" | custom-call | tf_op jit(solution)/shard_map/pack/pallas_call | solution.py:371
  1.9 0.7 %lead.1 = (f32[8,512]{1,0:T(8,128)S(1)}, f32[8,512]{1,0:T(8,128)S(1)}, f32[8,512]{1,0:T(8,128)S(1)}, f32[8,512]{1,0:T(8,128)S(1)}, f32[2,2,24,512]{3,2,1,0:T(8,128)S(1)}, /*index=5*/f32[2,256,512]{2,1,0:T(8,128)S(1)}) custom-call(f32[256,512]{1,0:T(8,128)S(1)} %get-tuple-element.29.u_ref.u_near, bf16[4,256,256]{2,1,0:T(8,128)(2,1)S(1)} %get-tuple-element.30.k_ref, ...), custom_call_target="tpu_custom_call" | custom-call | tf_op jit(solution)/shard_map/lead/pallas_call | solution.py:399
  2.5 2.4 %collective-permute-start = (f32[8,512]{1,0:T(8,128)S(1)}, f32[8,512]{1,0:T(8,128)S(1)}, u32[]{:S(2)}, u32[]{:S(2)}) collective-permute-start(f32[8,512]{1,0:T(8,128)S(1)} %get-tuple-element.35), channel_id=1, source_target_pairs={{0,4},{4,8},{8,12},{12,16},{16,20},{20,24},{24,28},{28,0},{1,5},{5... | collective-permute-start | bytes 49160 | tf_op jit(solution)/shard_map/ppermute | solution.py:452
  4.9 0.7 %collective-permute-start.1 = (f32[8,512]{1,0:T(8,128)S(1)}, f32[8,512]{1,0:T(8,128)S(1)}, u32[]{:S(2)}, u32[]{:S(2)}) collective-permute-start(f32[8,512]{1,0:T(8,128)S(1)} %get-tuple-element.36), channel_id=1, source_target_pairs={{0,3},{1,2},{2,1},{3,0},{4,7},{5,6},{6,5},{7,4},{8,11},{9,10},{10,... | collective-permute-start | bytes 49160 | tf_op jit(solution)/shard_map/ppermute | solution.py:453
  5.5 2.5 %collective-permute-start.2 = (f32[8,512]{1,0:T(8,128)S(1)}, f32[8,512]{1,0:T(8,128)S(1)}, u32[]{:S(2)}, u32[]{:S(2)}) collective-permute-start(f32[8,512]{1,0:T(8,128)S(1)} %get-tuple-element.37), channel_id=1, source_target_pairs={{0,28},{4,0},{8,4},{12,8},{16,12},{20,16},{24,20},{28,24},{1,29},{... | collective-permute-start | bytes 49160 | tf_op jit(solution)/shard_map/ppermute | solution.py:454
  8.1 0.2 %collective-permute-start.3 = (f32[8,512]{1,0:T(8,128)S(1)}, f32[8,512]{1,0:T(8,128)S(1)}, u32[]{:S(2)}, u32[]{:S(2)}) collective-permute-start(f32[8,512]{1,0:T(8,128)S(1)} %get-tuple-element.38), channel_id=1, source_target_pairs={{0,1},{1,0},{2,3},{3,2},{4,5},{5,4},{6,7},{7,6},{8,9},{9,8},{10,11... | collective-permute-start | bytes 49160 | tf_op jit(solution)/shard_map/ppermute | solution.py:455
  8.2 1.0 %interior.1 = (f32[2,2,24,512]{3,2,1,0:T(8,128)S(1)}, f32[256,512]{1,0:T(8,128)}, f32[256,512]{1,0:T(8,128)}, f32[2,2,256,128]{3,2,1,0:T(8,128)S(1)}, f32[2,256,256]{2,1,0:T(8,128)S(1)}) custom-call(f32[256,512]{1,0:T(8,128)S(1)} %get-tuple-element.29.u_ref.u_near, bf16[4,256,256]{2,1,0:T(8,128)(2,1)S(1)} %get-tuple-element.30.k_ref, ...), custom_call_target="tpu_custom_call" | custom-call | flops 536870912 | bytes 2621440 | tf_op jit(solution)/shard_map/interior/pallas_call | solution.py:412
  9.2 0.4 %collective-permute-done.from_low_x = f32[8,512]{1,0:T(8,128)S(1)} collective-permute-done((f32[8,512]{1,0:T(8,128)S(1)}, f32[8,512]{1,0:T(8,128)S(1)}, u32[]{:S(2)}, u32[]{:S(2)}) %collective-permute-start) | collective-permute-done | bytes 16416 | tf_op jit(solution)/shard_map/ppermute | solution.py:452
  9.6 0.0 collective-permute-done.1.from_y_first
  9.6 0.0 collective-permute-done.2.from_high_x
  9.6 0.0 collective-permute-done.3.from_y_second
  9.6 1.2 %finish.1 = (f32[256,512]{1,0:T(8,128)}, f32[256,512]{1,0:T(8,128)}, f32[256,512]{1,0:T(8,128)}, f32[256,512]{1,0:T(8,128)}) custom-call(f32[8,512]{1,0:T(8,128)S(1)} %collective-permute-done.from_low_x, f32[8,512]{1,0:T(8,128)S(1)} %collective-permute-done.1.from_y_first, ...), custom_call_target="tpu_custom_call", output_to_operand_aliasing={{0}: (12, {}), {1}: (13, {})} | custom-call | tf_op jit(solution)/shard_map/finish/pallas_call | solution.py:428
Async XLA Ops:
  2.5 7.1 %collective-permute-start = (f32[8,512]{1,0:T(8,128)S(1)}, f32[8,512]{1,0:T(8,128)S(1)}, u32[]{:S(2)}, u32[]{:S(2)}) collective-permute-start(f32[8,512]{1,0:T(8,128)S(1)} %get-tuple-element.35), channel_id=1, source_target_pairs={{0,4},{4,8},{8,12},{12,16},{16,20},{20,24},{24,28},{28,0},{1,5},{5... | collective-permute-start | bytes 49160 | tf_op jit(solution)/shard_map/ppermute | solution.py:452
  4.9 4.8 %collective-permute-start.1 = (f32[8,512]{1,0:T(8,128)S(1)}, f32[8,512]{1,0:T(8,128)S(1)}, u32[]{:S(2)}, u32[]{:S(2)}) collective-permute-start(f32[8,512]{1,0:T(8,128)S(1)} %get-tuple-element.36), channel_id=1, source_target_pairs={{0,3},{1,2},{2,1},{3,0},{4,7},{5,6},{6,5},{7,4},{8,11},{9,10},{10,... | collective-permute-start | bytes 49160 | tf_op jit(solution)/shard_map/ppermute | solution.py:453
  5.5 4.1 %collective-permute-start.2 = (f32[8,512]{1,0:T(8,128)S(1)}, f32[8,512]{1,0:T(8,128)S(1)}, u32[]{:S(2)}, u32[]{:S(2)}) collective-permute-start(f32[8,512]{1,0:T(8,128)S(1)} %get-tuple-element.37), channel_id=1, source_target_pairs={{0,28},{4,0},{8,4},{12,8},{16,12},{20,16},{24,20},{28,24},{1,29},{... | collective-permute-start | bytes 49160 | tf_op jit(solution)/shard_map/ppermute | solution.py:454
  8.1 1.6 %collective-permute-start.3 = (f32[8,512]{1,0:T(8,128)S(1)}, f32[8,512]{1,0:T(8,128)S(1)}, u32[]{:S(2)}, u32[]{:S(2)}) collective-permute-start(f32[8,512]{1,0:T(8,128)S(1)} %get-tuple-element.38), channel_id=1, source_target_pairs={{0,1},{1,0},{2,3},{3,2},{4,5},{5,4},{6,7},{7,6},{8,9},{9,8},{10,11... | collective-permute-start | bytes 49160 | tf_op jit(solution)/shard_map/ppermute | solution.py:455

commit v5 on v4

--- a/solution.py
+++ b/solution.py
@@ -24,7 +24,7 @@
 STRIP = 32
 EDGE = 24
 REACH = 64
-MESSAGE = 8
+MESSAGE = 4
 
 ANY = pl.BlockSpec(memory_space=pl.ANY)
 VMEM = pl.BlockSpec(memory_space=pltpu.VMEM)
@@ -60,7 +60,7 @@
     ]
     near = pltpu.roll(strip[STRIP - 8 :], 2, 0) if high else strip[:8]
     row = lax.broadcasted_iota(jnp.int32, near.shape, 0)
-    return jnp.where(row < 2, near, jnp.where(row == 2, tails[0], tails[1]))
+    return jnp.where(row < 2, near, jnp.where(row == 2, tails[0], tails[1]))[:MESSAGE]
 
 
 def tiles_of(length):
@@ -193,19 +193,29 @@
     return upper, (value - upper.astype(F32)).astype(BF16)
 
 
-def solve_x(u_ref, k_ref, strips, solved_ref):
+def solve_x(u_ref, k_ref, strips, solved_ref, copies):
     rows, columns = u_ref.shape
     span = min(columns, WINDOW)
-    for j in range(columns // span):
-        tiles = [differences(u_ref[:, pl.ds(j * span + t.start, t.size)], 0) for t in tiles_of(span)]
-        lanes = pl.ds(j * span, span)
-        for s in range(2):
-            inverse = k_ref[2 * s, :rows, :rows], k_ref[2 * s + 1, :rows, :rows]
+    for s in range(2):
+        inverse = k_ref[2 * s, :rows, :rows], k_ref[2 * s + 1, :rows, :rows]
+        for j in range(columns // span):
+            tiles = [differences(u_ref[:, pl.ds(j * span + t.start, t.size)], 0) for t in tiles_of(span)]
+            lanes = pl.ds(j * span, span)
             rhs = jnp.concatenate([only_known(tile[s], 0) for tile in tiles], axis=1)
             solved = product(inverse, split(rhs))
             solved_ref[s, :, lanes] = solved
             strips[s, 0, :, lanes] = solved[:EDGE]
             strips[s, 1, :, lanes] = solved[rows - EDGE :]
+        if s < len(copies):
+            copies[s].start()
+
+
+def inner_copies(solved_ref, outs, sems):
+    rows = solved_ref.shape[1]
+    if rows <= 2 * EDGE:
+        return []
+    inner = pl.ds(EDGE, rows - 2 * EDGE)
+    return [pltpu.make_async_copy(solved_ref.at[s, inner], out.at[inner], sems.at[s]) for s, out in enumerate(outs)]
 
 
 def solve_y(u_ref, k_ref, strips, solved_ref):
@@ -238,49 +248,59 @@
             solved_ref[s, :, pl.ds((t - 1) * TILE, TILE)] = tiles[t]
 
 
-def solves_x_early():
-    return (lax.axis_index("gx") == 0) & (lax.axis_index("gy") < 2)
-
-
-def lead_kernel(u_ref, k_ref, *refs):
-    messages, passed, (strips_x, solved_x) = refs[:4], refs[4:8], refs[8:]
+FIRST, BETWEEN, LAST = range(3)
+
+
+def solves_x():
+    ends = jnp.where(lax.axis_index("gy") < 2, FIRST, BETWEEN)
+    return jnp.where(lax.axis_index("gx") == 0, ends, LAST)
+
+
+def first_kernel(u_ref, k_ref, *refs):
+    messages, passed, (dx, strips_x, solved_x, sems) = refs[:2], refs[2:4], refs[4:]
     for message_ref, passed_ref in zip(messages, passed):
         passed_ref[...] = message_ref[...]
 
-    @pl.when(solves_x_early())
+    @pl.when(solves_x() == FIRST)
     def _():
-        solve_x(u_ref, k_ref, strips_x, solved_x)
-
-
-def interior_kernel(u_ref, k_ref, early_strips, early_solved, *refs):
-    strips_x, dx, dxx, strips_y, solved_y, solved_x, sems = refs
-    rows, columns = u_ref.shape
-
-    def inner_copies(source):
-        if rows <= 2 * EDGE:
-            return []
-        inner = pl.ds(EDGE, rows - 2 * EDGE)
-        return [pltpu.make_async_copy(source.at[s, inner], out.at[inner], sems.at[s]) for s, out in enumerate((dx, dxx))]
-
-    @pl.when(solves_x_early())
-    def _():
-        copies = inner_copies(early_solved)
-        for copy in copies:
-            copy.start()
-        strips_x[...] = early_strips[...]
-        solve_y(u_ref, k_ref, strips_y, solved_y)
+        copies = inner_copies(solved_x, (dx,), sems)
+        solve_x(u_ref, k_ref, strips_x, solved_x, copies)
         for copy in copies:
             copy.wait()
 
-    @pl.when(jnp.logical_not(solves_x_early()))
+
+def between_kernel(u_ref, k_ref, *refs):
+    messages, passed, (strips_x, solved_x) = refs[:2], refs[3:5], refs[5:]
+    for message_ref, passed_ref in zip(messages, passed):
+        passed_ref[...] = message_ref[...]
+
+    @pl.when(solves_x() == BETWEEN)
     def _():
-        solve_x(u_ref, k_ref, strips_x, solved_x)
-        copies = inner_copies(solved_x)
-        for copy in copies:
-            copy.start()
-        solve_y(u_ref, k_ref, strips_y, solved_y)
-        for copy in copies:
-            copy.wait()
+        solve_x(u_ref, k_ref, strips_x, solved_x, [])
+
+
+def interior_kernel(u_ref, k_ref, _, first_strips, first_solved, between_strips, between_solved, *refs):
+    strips_x, dx, dxx, strips_y, solved_y, solved_x, sems = refs
+    for when, strips, solved in (
+        (FIRST, first_strips, first_solved),
+        (BETWEEN, between_strips, between_solved),
+        (LAST, strips_x, solved_x),
+    ):
+
+        @pl.when(solves_x() == when)
+        def _():
+            copies = inner_copies(solved, (dx, dxx), sems)
+            if when == LAST:
+                solve_x(u_ref, k_ref, strips, solved, copies)
+            else:
+                if when == FIRST:
+                    copies = copies[1:]
+                for copy in copies:
+                    copy.start()
+                strips_x[...] = strips[...]
+            solve_y(u_ref, k_ref, strips_y, solved_y)
+            for copy in copies:
+                copy.wait()
 
 
 def side_terms(around, tails, high):
@@ -292,54 +312,41 @@
     return found
 
 
-def both_sides(from_low, from_high, own_low, own_high):
-    row = lax.broadcasted_iota(jnp.int32, own_low.shape, 0)
-    low = jnp.where(row < 2, from_low, pltpu.roll(own_low, 2, 0))
-    high = jnp.where(row < 2, pltpu.roll(own_high, 2, 0), pltpu.roll(from_high, 2, 0))
-    tails = lambda m: (m[2:3], m[3:4])
-    return side_terms(low, tails(from_low), False), side_terms(high, tails(from_high), True)
-
-
-def finish_kernel(
-    from_low_x, from_y_first, from_high_x, from_y_second, u_near, near_low, near_high, table_x, table_y, strips_x, strips_y, solved_y, *refs
+def low_terms(message, own):
+    row = lax.broadcasted_iota(jnp.int32, own.shape, 0)
+    around = jnp.where(row < 2, jnp.concatenate([message, message], axis=0), pltpu.roll(own, 2, 0))
+    return side_terms(around, (message[2:3], message[3:4]), False)
+
+
+def high_terms(message, own):
+    row = lax.broadcasted_iota(jnp.int32, own.shape, 0)
+    around = pltpu.roll(jnp.where(row < 2, jnp.concatenate([message, message], axis=0), own), 2, 0)
+    return side_terms(around, (message[2:3], message[3:4]), True)
+
+
+def add_side_x(terms, side, lanes, table_x, strips_x, put):
+    row = lax.broadcasted_iota(jnp.int32, (8, 1), 0)
+    for s in range(2):
+        near, first = terms[s]
+        extra = near * table_x[s, side, :, : lanes.size]
+        first = jnp.where(row == (7 if side else 0), first, 0.0)
+        if side:
+            extra = jnp.concatenate([extra[: EDGE - 8], extra[EDGE - 8 :] + first], axis=0)
+        else:
+            extra = jnp.concatenate([extra[:8] + first, extra[8:]], axis=0)
+        put[s, :, lanes] = strips_x[s, side, :, lanes] + extra
+
+
+def sides_kernel(
+    from_y_first, from_y_second, near_low, near_high, table_y, strips_y, done_y
 ):
-    dx, dxx, dy, dyy, done_x, done_y, sems = refs[2:]
-    rows, columns = dx.shape
-    started = []
-
-    def send(source, target):
-        copy = pltpu.make_async_copy(source, target, sems.at[len(started)])
-        copy.start()
-        started.append(copy)
-
-    if columns > 2 * TILE:
-        for s, out in enumerate((dy, dyy)):
-            send(solved_y.at[s], out.at[:, pl.ds(TILE, columns - 2 * TILE)])
-    step = min(columns, TILE)
+    rows = near_low.shape[1]
     row = lax.broadcasted_iota(jnp.int32, (8, 1), 0)
-    tiles = tiles_of(columns)
-    own = lambda start, lanes: u_near[pl.ds(start, 8), lanes]
-    for lanes in tiles:
-        terms = both_sides(from_low_x[:, lanes], from_high_x[:, lanes], own(0, lanes), own(rows - 8, lanes))
-        for s in range(2):
-            for side in range(2):
-                near, first = terms[side][s]
-                extra = near * table_x[s, side, :, :step]
-                first = jnp.where(row == (7 if side else 0), first, 0.0)
-                if side:
-                    extra = jnp.concatenate([extra[: EDGE - 8], extra[EDGE - 8 :] + first], axis=0)
-                else:
-                    extra = jnp.concatenate([extra[:8] + first, extra[8:]], axis=0)
-                done_x[s, side, :, lanes] = strips_x[s, side, :, lanes] + extra
-    for s, out in enumerate((dx, dxx)):
-        for side in range(2):
-            send(done_x.at[s, side], out.at[pl.ds(side * (rows - EDGE), EDGE)])
-
     low_first = low_goes_first()
     for lines in tiles_of(rows):
         first, second = from_y_first[:, lines], from_y_second[:, lines]
         from_low, from_high = jnp.where(low_first, first, second), jnp.where(low_first, second, first)
-        terms = both_sides(from_low, from_high, near_low[:, lines], near_high[:, lines])
+        terms = low_terms(from_low, near_low[:, lines]), high_terms(from_high, near_high[:, lines])
         stacked = jnp.zeros((8, lines.size), F32)
         for side in range(2):
             for s in range(2):
@@ -348,11 +355,34 @@
         upper, lower = halves(stacked)
         factors = jnp.concatenate([upper, lower, upper, jnp.zeros_like(upper)], axis=0).astype(BF16)
         added = lax.dot_general(factors, table_y[...], (((0,), (0,)), ((), ())), preferred_element_type=F32)
-        for s, out in enumerate((dy, dyy)):
+        for s in range(2):
             for side in range(2):
                 block = 2 * s + side
                 done_y[s, side, lines] = strips_y[s, side, lines] + added[:, block * TILE : (block + 1) * TILE]
-                send(done_y.at[s, side, lines], out.at[lines, pl.ds(side * (columns - TILE), TILE)])
+
+
+def finish_kernel(from_low_x, from_high_x, u_near, table_x, strips_x, done_y, solved_y, *refs):
+    dx, dxx, dy, dyy, done_x, sems = refs[2:]
+    rows, columns = dx.shape
+    started = []
+
+    def send(source, target):
+        copy = pltpu.make_async_copy(source, target, sems.at[len(started)])
+        copy.start()
+        started.append(copy)
+
+    for s, out in enumerate((dy, dyy)):
+        for side in range(2):
+            send(done_y.at[s, side], out.at[:, pl.ds(side * (columns - TILE), TILE)])
+    for lanes in tiles_of(columns):
+        add_side_x(low_terms(from_low_x[:, lanes], u_near[pl.ds(0, 8), lanes]), 0, lanes, table_x, strips_x, done_x.at[0])
+        add_side_x(high_terms(from_high_x[:, lanes], u_near[pl.ds(rows - 8, 8), lanes]), 1, lanes, table_x, strips_x, done_x.at[1])
+    for s, out in enumerate((dx, dxx)):
+        for side in range(2):
+            send(done_x.at[side, s], out.at[pl.ds(side * (rows - EDGE), EDGE)])
+    if columns > 2 * TILE:
+        for s, out in enumerate((dy, dyy)):
+            send(solved_y.at[s], out.at[:, pl.ds(TILE, columns - 2 * TILE)])
     for copy in started:
         copy.wait()
 
@@ -394,19 +424,19 @@
     return on_chip(2, 2, EDGE, columns), on_chip(2, rows, columns)
 
 
-def lead(u_near, inverses, messages):
-    size = u_near.shape
+def lead(kernel, name, outs, scratch, u_near, inverses, *messages):
     return pl.pallas_call(
-        lead_kernel,
-        name="lead",
-        out_shape=tuple(on_chip(*a.shape) for a in messages) + shapes_x(*size),
-        in_specs=[VMEM] * 6,
-        out_specs=[VMEM] * 6,
+        kernel,
+        name=name,
+        out_shape=tuple(on_chip(*a.shape) for a in messages[:2]) + outs,
+        in_specs=[VMEM] * (2 + len(messages)),
+        out_specs=[VMEM] * 2 + [ANY] * (len(outs) - 2) + [VMEM] * 2,
+        scratch_shapes=scratch,
         compiler_params=LIMIT,
-    )(near(u_near), near(inverses), *(near(a) for a in messages))
-
-
-def interior(u_near, inverses, early_strips, early_solved):
+    )(*(near(a) for a in (u_near, inverses, *messages)))
+
+
+def interior(u_near, inverses, dx, *early):
     rows, columns = u_near.shape
     strips_x, solved_x = shapes_x(rows, columns)
     return pl.pallas_call(
@@ -415,48 +445,65 @@
         out_shape=(strips_x,)
         + (pltpu.HBM(u_near.shape, F32),) * 2
         + (on_chip(2, 2, rows, TILE), on_chip(2, rows, max(columns - 2 * TILE, TILE))),
-        in_specs=[VMEM] * 4,
+        in_specs=[VMEM] * 2 + [ANY] + [VMEM] * 4,
         out_specs=[VMEM] + [ANY] * 2 + [VMEM] * 2,
+        input_output_aliases={2: 1},
         scratch_shapes=[solved_x, pltpu.SemaphoreType.DMA((2,))],
         compiler_params=LIMIT,
         cost_estimate=pl.CostEstimate(flops=2 * 2**28, bytes_accessed=5 * 2**19, transcendentals=0),
-    )(near(u_near), near(inverses), near(early_strips), near(early_solved))
+    )(near(u_near), near(inverses), dx, *(near(a) for a in early))
+
+
+def sides(arrays, strips_y):
+    return pl.pallas_call(
+        sides_kernel,
+        name="sides",
+        out_shape=on_chip(*strips_y.shape),
+        in_specs=[VMEM] * 6,
+        out_specs=VMEM,
+        compiler_params=LIMIT,
+    )(*(near(a) for a in (*arrays, strips_y)))
 
 
 def finish(arrays, parts):
-    rows, columns = parts[0].shape
+    columns = parts[0].shape[1]
     return pl.pallas_call(
         finish_kernel,
         name="finish",
         out_shape=(pltpu.HBM(parts[0].shape, F32),) * 4,
-        in_specs=[VMEM] * 12 + [ANY] * 2,
+        in_specs=[VMEM] * 7 + [ANY] * 2,
         out_specs=[ANY] * 4,
-        input_output_aliases={12: 0, 13: 1},
-        scratch_shapes=[
-            on_chip(2, 2, EDGE, columns),
-            on_chip(2, 2, rows, TILE),
-            pltpu.SemaphoreType.DMA((6 + 4 * len(tiles_of(rows)),)),
-        ],
+        input_output_aliases={7: 0, 8: 1},
+        scratch_shapes=[on_chip(2, 2, EDGE, columns), pltpu.SemaphoreType.DMA((10,))],
         compiler_params=LIMIT,
     )(*(near(a) for a in arrays), *parts)
 
 
 def local(velocity):
     to_high_x, to_low_x, to_y_first, to_y_second, u_near, near_low, near_high, inverses, *tables = pack(velocity[0])
-    to_high_x, to_y_first, to_low_x, to_y_second, strips_x, solved_x = lead(
-        u_near, inverses, (to_high_x, to_y_first, to_low_x, to_y_second)
+    size = u_near.shape
+    outs = shapes_x(*size)
+    to_high_x, to_y_first, dx, *early = lead(
+        first_kernel,
+        "solve_first",
+        (pltpu.HBM(size, F32),) + outs,
+        [pltpu.SemaphoreType.DMA((1,))],
+        u_near,
+        inverses,
+        to_high_x,
+        to_y_first,
     )
+    to_low_x, to_y_second, *between = lead(between_kernel, "solve_between", outs, [], u_near, inverses, to_low_x, to_y_second, early[0])
     gx = lax.axis_size("gx")
     first, second = trades_along_y()
-    messages = (
-        lax.ppermute(to_high_x, "gx", [(i, (i + 1) % gx) for i in range(gx)]),
-        lax.ppermute(to_y_first, ("gx", "gy"), first),
-        lax.ppermute(to_low_x, "gx", [(i, (i - 1) % gx) for i in range(gx)]),
-        lax.ppermute(to_y_second, ("gx", "gy"), second),
-    )
-    strips_x, dx, dxx, strips_y, solved_y = interior(u_near, inverses, strips_x, solved_x)
-    arrays = (*messages, u_near, near_low, near_high, *tables, strips_x, strips_y, solved_y)
-    dx, dxx, dy, dyy = finish(arrays, (dx, dxx))
+    from_low_x = lax.ppermute(to_high_x, "gx", [(i, (i + 1) % gx) for i in range(gx)])
+    from_y_first = lax.ppermute(to_y_first, ("gx", "gy"), first)
+    from_high_x = lax.ppermute(to_low_x, "gx", [(i, (i - 1) % gx) for i in range(gx)])
+    from_y_second = lax.ppermute(to_y_second, ("gx", "gy"), second)
+    strips_x, dx, dxx, strips_y, solved_y = interior(u_near, inverses, dx, *early, *between)
+    table_x, table_y = tables
+    done_y = sides((from_y_first, from_y_second, near_low, near_high, table_y), strips_y)
+    dx, dxx, dy, dyy = finish((from_low_x, from_high_x, u_near, table_x, strips_x, done_y, solved_y), (dx, dxx))
     return tuple(o[None] for o in (dx, dy, dxx, dyy))
 
 

time: 11 us -> 11 us (level)
  the two profiles are of different devices: /device:TPU:0 before, /device:TPU:17 now
where the time goes in v5:
time: 11 us; the launch traced here: 10.9 us
  starting transfers between devices  4.78 us (43%)
  Pallas kernels  4.19 us (38%)
  waiting for transfers between devices  1.23 us (11%)
  between operations  0.69 us (6%)
    ppermute x1, starting transfers between devices, local(): lax.ppermute(to_low_x, 'gx', [(i, (i - 1) % gx) for i in range(gx)])  2.28 us
    pallas_call x1, Pallas kernels, interior(): pl.pallas_call(interior_kernel, name='interior', out_shape=(strips_x,) +...  1.55 us
    ppermute x1, starting transfers between devices, local(): lax.ppermute(to_high_x, 'gx', [(i, (i + 1) % gx) for i in range(gx)])  1.26 us
    ppermute x1, waiting for transfers between devices, local(): from_y_second = lax.ppermute(to_y_second, ('gx', 'gy'), second)  1.22 us
    pallas_call x1, Pallas kernels, pack(): pl.pallas_call(pack_kernel, name='pack', out_shape=(on_chip(MESSAGE, colu...  1.21 us
    pallas_call x1, Pallas kernels, finish(): pl.pallas_call(finish_kernel, name='finish', out_shape=(pltpu.HBM(parts[0...  1.12 us
    ppermute x1, starting transfers between devices, local(): from_y_first = lax.ppermute(to_y_first, ('gx', 'gy'), first)  0.96 us
    ppermute x1, starting transfers between devices, local(): from_y_second = lax.ppermute(to_y_second, ('gx', 'gy'), second)  0.28 us
  transfers between devices with their start and end apart: 4, of which 1 were waited for; matrix products, arithmetic and copies ran while one was open for 0% of the time, Pallas kernels for 17%

profile of v5, /device:TPU:17, one launch (start us, length us, event | category | flops | bytes accessed | tf_op | source)
XLA Modules:
  0.0 10.9 jit_solution(11100885054042127134)
XLA Ops:
  0.6 1.2 %pack.1 = (f32[4,512]{1,0:T(4,128)S(1)}, f32[4,512]{1,0:T(4,128)S(1)}, f32[4,512]{1,0:T(4,128)S(1)}, f32[4,512]{1,0:T(4,128)S(1)}, f32[256,512]{1,0:T(8,128)S(1)...) custom-call(f32[256,512]{1,0:T(8,128)} %bitcast.6), custom_call_target="tpu_custom_call" | custom-call | tf_op jit(solution)/shard_map/pack/pallas_call | solution.py:401
  1.9 1.3 %collective-permute-start = (f32[4,512]{1,0:T(4,128)S(1)}, f32[4,512]{1,0:T(4,128)S(1)}, u32[]{:S(2)}, u32[]{:S(2)}) collective-permute-start(f32[4,512]{1,0:T(4,128)S(1)} %get-tuple-element.36), channel_id=1, source_target_pairs={{0,4},{4,8},{8,12},{12,16},{16,20},{20,24},{24,28},{28,0},{1,5},{5... | collective-permute-start | bytes 24584 | tf_op jit(solution)/shard_map/ppermute | solution.py:499
  3.2 1.0 %collective-permute-start.2 = (f32[4,512]{1,0:T(4,128)S(1)}, f32[4,512]{1,0:T(4,128)S(1)}, u32[]{:S(2)}, u32[]{:S(2)}) collective-permute-start(f32[4,512]{1,0:T(4,128)S(1)} %get-tuple-element.47), channel_id=1, source_target_pairs={{0,3},{1,2},{2,1},{3,0},{4,7},{5,6},{6,5},{7,4},{8,11},{9,10},{10,... | collective-permute-start | bytes 24584 | tf_op jit(solution)/shard_map/ppermute | solution.py:500
  4.1 2.3 %collective-permute-start.1 = (f32[4,512]{1,0:T(4,128)S(1)}, f32[4,512]{1,0:T(4,128)S(1)}, u32[]{:S(2)}, u32[]{:S(2)}) collective-permute-start(f32[4,512]{1,0:T(4,128)S(1)} %get-tuple-element.40), channel_id=1, source_target_pairs={{0,28},{4,0},{8,4},{12,8},{16,12},{20,16},{24,20},{28,24},{1,29},{... | collective-permute-start | bytes 24584 | tf_op jit(solution)/shard_map/ppermute | solution.py:501
  6.4 0.3 %collective-permute-start.3 = (f32[4,512]{1,0:T(4,128)S(1)}, f32[4,512]{1,0:T(4,128)S(1)}, u32[]{:S(2)}, u32[]{:S(2)}) collective-permute-start(f32[4,512]{1,0:T(4,128)S(1)} %get-tuple-element.48), channel_id=1, source_target_pairs={{0,1},{1,0},{2,3},{3,2},{4,5},{5,4},{6,7},{7,6},{8,9},{9,8},{10,11... | collective-permute-start | bytes 24584 | tf_op jit(solution)/shard_map/ppermute | solution.py:502
  6.7 1.6 %interior.1 = (f32[2,2,24,512]{3,2,1,0:T(8,128)S(1)}, f32[256,512]{1,0:T(8,128)}, f32[256,512]{1,0:T(8,128)}, f32[2,2,256,128]{3,2,1,0:T(8,128)S(1)}, f32[2,256,256]{2,1,0:T(8,128)S(1)}) custom-call(f32[256,512]{1,0:T(8,128)S(1)} %get-tuple-element.32.u_ref.u_near, ...), custom_call_target="tpu_custom_call", output_to_operand_aliasing={{1}: (2, {})} | custom-call | flops 536870912 | bytes 2621440 | tf_op jit(solution)/shard_map/interior/pallas_call | solution.py:442
  8.2 0.0 collective-permute-done.2.from_y_first
  8.2 1.2 %collective-permute-done.3.from_y_second = f32[4,512]{1,0:T(4,128)S(1)} collective-permute-done((f32[4,512]{1,0:T(4,128)S(1)}, f32[4,512]{1,0:T(4,128)S(1)}, u32[]{:S(2)}, u32[]{:S(2)}) %collective-permute-start.3) | collective-permute-done | bytes 8224 | tf_op jit(solution)/shard_map/ppermute | solution.py:502
  9.5 0.3 %sides.1.done_y = f32[2,2,256,128]{3,2,1,0:T(8,128)S(1)} custom-call(f32[4,512]{1,0:T(4,128)S(1)} %collective-permute-done.2.from_y_first, f32[4,512]{1,0:T(4,128)S(1)} %collective-permute-done.3.from_y_second, f32[8,256]{1,0:T(8,128)S(1)} %get-tuple-element.49.near_low, f32[8,256]{1,0:T(8,128)S(1)} %get-tuple-element.50.near_high, ...), custom_call_target="tpu_custom_call" | custom-call | tf_op jit(solution)/shard_map/sides/pallas_call | solution.py:458
  9.7 0.0 collective-permute-done.from_low_x
  9.8 0.0 collective-permute-done.1.from_high_x
  9.8 1.1 %finish.1 = (f32[256,512]{1,0:T(8,128)}, f32[256,512]{1,0:T(8,128)}, f32[256,512]{1,0:T(8,128)}, f32[256,512]{1,0:T(8,128)}) custom-call(f32[4,512]{1,0:T(4,128)S(1)} %collective-permute-done.from_low_x, f32[4,512]{1,0:T(4,128)S(1)} %collective-permute-done.1.from_high_x, ...), custom_call_target="tpu_custom_call", output_to_operand_aliasing={{0}: (7, {}), {1}: (8, {})} | custom-call | tf_op jit(solution)/shard_map/finish/pallas_call | solution.py:470
  (2 shorter events, 0.0 us)
Async XLA Ops:
  1.9 7.9 %collective-permute-start = (f32[4,512]{1,0:T(4,128)S(1)}, f32[4,512]{1,0:T(4,128)S(1)}, u32[]{:S(2)}, u32[]{:S(2)}) collective-permute-start(f32[4,512]{1,0:T(4,128)S(1)} %get-tuple-element.36), channel_id=1, source_target_pairs={{0,4},{4,8},{8,12},{12,16},{16,20},{20,24},{24,28},{28,0},{1,5},{5... | collective-permute-start | bytes 24584 | tf_op jit(solution)/shard_map/ppermute | solution.py:499
  3.2 5.1 %collective-permute-start.2 = (f32[4,512]{1,0:T(4,128)S(1)}, f32[4,512]{1,0:T(4,128)S(1)}, u32[]{:S(2)}, u32[]{:S(2)}) collective-permute-start(f32[4,512]{1,0:T(4,128)S(1)} %get-tuple-element.47), channel_id=1, source_target_pairs={{0,3},{1,2},{2,1},{3,0},{4,7},{5,6},{6,5},{7,4},{8,11},{9,10},{10,... | collective-permute-start | bytes 24584 | tf_op jit(solution)/shard_map/ppermute | solution.py:500
  4.1 5.7 %collective-permute-start.1 = (f32[4,512]{1,0:T(4,128)S(1)}, f32[4,512]{1,0:T(4,128)S(1)}, u32[]{:S(2)}, u32[]{:S(2)}) collective-permute-start(f32[4,512]{1,0:T(4,128)S(1)} %get-tuple-element.40), channel_id=1, source_target_pairs={{0,28},{4,0},{8,4},{12,8},{16,12},{20,16},{24,20},{28,24},{1,29},{... | collective-permute-start | bytes 24584 | tf_op jit(solution)/shard_map/ppermute | solution.py:501
  6.4 3.1 %collective-permute-start.3 = (f32[4,512]{1,0:T(4,128)S(1)}, f32[4,512]{1,0:T(4,128)S(1)}, u32[]{:S(2)}, u32[]{:S(2)}) collective-permute-start(f32[4,512]{1,0:T(4,128)S(1)} %get-tuple-element.48), channel_id=1, source_target_pairs={{0,1},{1,0},{2,3},{3,2},{4,5},{5,4},{6,7},{7,6},{8,9},{9,8},{10,11... | collective-permute-start | bytes 24584 | tf_op jit(solution)/shard_map/ppermute | solution.py:502

commit v6 on v5

--- a/solution.py
+++ b/solution.py
@@ -109,7 +109,7 @@
 
 
 def low_goes_first():
-    next_chip_first = 2 * lax.axis_index("gx") < lax.axis_size("gx")
+    next_chip_first = lax.axis_index("gx") == 0
     return next_chip_first == (lax.rem(lax.axis_index("gy"), 2) == 0)
 
 
@@ -119,7 +119,7 @@
     same_chip = [(y, y + 1 if y % 2 == 0 else y - 1) for y in range(gy)]
     first, second = [], []
     for x in range(gx):
-        orders = (next_chip, same_chip) if 2 * x < gx else (same_chip, next_chip)
+        orders = (next_chip, same_chip) if x == 0 else (same_chip, next_chip)
         for found, pairs in zip((first, second), orders):
             found += [(x * gy + source, x * gy + target) for source, target in pairs]
     return first, second

time: 11 us -> 10.9 us (level)
  the two profiles are of different devices: /device:TPU:17 before, /device:TPU:0 now
where the time goes in v6:
time: 10.9 us; the launch traced here: 10.7 us
  starting transfers between devices  5.09 us (47%)
  Pallas kernels  4.86 us (45%)
  between operations  0.69 us (6%)
    ppermute x1, starting transfers between devices, local(): lax.ppermute(to_low_x, 'gx', [(i, (i - 1) % gx) for i in range(gx)])  2.55 us
    ppermute x1, starting transfers between devices, local(): lax.ppermute(to_high_x, 'gx', [(i, (i + 1) % gx) for i in range(gx)])  1.72 us
    pallas_call x2, Pallas kernels, lead(): pl.pallas_call(kernel, name=name, out_shape=tuple((on_chip(*a.shape) for...  1.3 us
    pallas_call x1, Pallas kernels, pack(): pl.pallas_call(pack_kernel, name='pack', out_shape=(on_chip(MESSAGE, colu...  1.21 us
    pallas_call x1, Pallas kernels, finish(): pl.pallas_call(finish_kernel, name='finish', out_shape=(pltpu.HBM(parts[0...  1.12 us
    pallas_call x1, Pallas kernels, interior(): pl.pallas_call(interior_kernel, name='interior', out_shape=(strips_x,) +...  0.95 us
    ppermute x1, starting transfers between devices, local(): from_y_first = lax.ppermute(to_y_first, ('gx', 'gy'), first)  0.68 us
    pallas_call x1, Pallas kernels, sides(): pl.pallas_call(sides_kernel, name='sides', out_shape=on_chip(*strips_y.sh...  0.27 us
  transfers between devices with their start and end apart: 4, of which 1 were waited for; matrix products, arithmetic and copies ran while one was open for 0% of the time, Pallas kernels for 12%

profile of v6, /device:TPU:0, one launch (start us, length us, event | category | flops | bytes accessed | tf_op | source)
XLA Modules:
  0.0 10.7 jit_solution(7091439508141979965)
XLA Ops:
  0.6 1.2 %pack.1 = (f32[4,512]{1,0:T(4,128)S(1)}, f32[4,512]{1,0:T(4,128)S(1)}, f32[4,512]{1,0:T(4,128)S(1)}, f32[4,512]{1,0:T(4,128)S(1)}, f32[256,512]{1,0:T(8,128)S(1)...) custom-call(f32[256,512]{1,0:T(8,128)} %bitcast.6), custom_call_target="tpu_custom_call" | custom-call | tf_op jit(solution)/shard_map/pack/pallas_call | solution.py:401
  1.9 1.3 %solve_first.1 = (f32[4,512]{1,0:T(4,128)S(1)}, f32[4,512]{1,0:T(4,128)S(1)}, f32[256,512]{1,0:T(8,128)}, f32[2,2,24,512]{3,2,1,0:T(8,128)S(1)}, f32[2,256,512]{2,1,0:T(8,128)S(1)}) custom-call(f32[256,512]{1,0:T(8,128)S(1)} %get-tuple-element.32.u_ref.u_near, bf16[4,256,256]{2,1,0:T(8,128)(2,1)S(1)} %get-tuple-element.33.k_ref, ...), custom_call_target="tpu_custom_call" | custom-call | tf_op jit(solution)/shard_map/solve_first/pallas_call | solution.py:428
  3.2 1.7 %collective-permute-start = (f32[4,512]{1,0:T(4,128)S(1)}, f32[4,512]{1,0:T(4,128)S(1)}, u32[]{:S(2)}, u32[]{:S(2)}) collective-permute-start(f32[4,512]{1,0:T(4,128)S(1)} %get-tuple-element.36), channel_id=1, source_target_pairs={{0,4},{4,8},{8,12},{12,16},{16,20},{20,24},{24,28},{28,0},{1,5},{5... | collective-permute-start | bytes 24584 | tf_op jit(solution)/shard_map/ppermute | solution.py:499
  4.9 0.7 %collective-permute-start.2 = (f32[4,512]{1,0:T(4,128)S(1)}, f32[4,512]{1,0:T(4,128)S(1)}, u32[]{:S(2)}, u32[]{:S(2)}) collective-permute-start(f32[4,512]{1,0:T(4,128)S(1)} %get-tuple-element.47), channel_id=1, source_target_pairs={{0,3},{1,2},{2,1},{3,0},{4,5},{5,4},{6,7},{7,6},{8,9},{9,8},{10,11... | collective-permute-start | bytes 24584 | tf_op jit(solution)/shard_map/ppermute | solution.py:500
  5.6 2.5 %collective-permute-start.1 = (f32[4,512]{1,0:T(4,128)S(1)}, f32[4,512]{1,0:T(4,128)S(1)}, u32[]{:S(2)}, u32[]{:S(2)}) collective-permute-start(f32[4,512]{1,0:T(4,128)S(1)} %get-tuple-element.40), channel_id=1, source_target_pairs={{0,28},{4,0},{8,4},{12,8},{16,12},{20,16},{24,20},{28,24},{1,29},{... | collective-permute-start | bytes 24584 | tf_op jit(solution)/shard_map/ppermute | solution.py:501
  8.1 0.1 %collective-permute-start.3 = (f32[4,512]{1,0:T(4,128)S(1)}, f32[4,512]{1,0:T(4,128)S(1)}, u32[]{:S(2)}, u32[]{:S(2)}) collective-permute-start(f32[4,512]{1,0:T(4,128)S(1)} %get-tuple-element.48), channel_id=1, source_target_pairs={{0,1},{1,0},{2,3},{3,2},{4,7},{5,6},{6,5},{7,4},{8,11},{9,10},{10,... | collective-permute-start | bytes 24584 | tf_op jit(solution)/shard_map/ppermute | solution.py:502
  8.3 1.0 %interior.1 = (f32[2,2,24,512]{3,2,1,0:T(8,128)S(1)}, f32[256,512]{1,0:T(8,128)}, f32[256,512]{1,0:T(8,128)}, f32[2,2,256,128]{3,2,1,0:T(8,128)S(1)}, f32[2,256,256]{2,1,0:T(8,128)S(1)}) custom-call(f32[256,512]{1,0:T(8,128)S(1)} %get-tuple-element.32.u_ref.u_near, ...), custom_call_target="tpu_custom_call", output_to_operand_aliasing={{1}: (2, {})} | custom-call | flops 536870912 | bytes 2621440 | tf_op jit(solution)/shard_map/interior/pallas_call | solution.py:442
  9.2 0.0 collective-permute-done.2.from_y_first
  9.2 0.1 collective-permute-done.3.from_y_second
  9.3 0.3 %sides.1.done_y = f32[2,2,256,128]{3,2,1,0:T(8,128)S(1)} custom-call(f32[4,512]{1,0:T(4,128)S(1)} %collective-permute-done.2.from_y_first, f32[4,512]{1,0:T(4,128)S(1)} %collective-permute-done.3.from_y_second, f32[8,256]{1,0:T(8,128)S(1)} %get-tuple-element.49.near_low, f32[8,256]{1,0:T(8,128)S(1)} %get-tuple-element.50.near_high, ...), custom_call_target="tpu_custom_call" | custom-call | tf_op jit(solution)/shard_map/sides/pallas_call | solution.py:458
  9.6 0.0 collective-permute-done.from_low_x
  9.6 0.0 collective-permute-done.1.from_high_x
  9.6 1.1 %finish.1 = (f32[256,512]{1,0:T(8,128)}, f32[256,512]{1,0:T(8,128)}, f32[256,512]{1,0:T(8,128)}, f32[256,512]{1,0:T(8,128)}) custom-call(f32[4,512]{1,0:T(4,128)S(1)} %collective-permute-done.from_low_x, f32[4,512]{1,0:T(4,128)S(1)} %collective-permute-done.1.from_high_x, ...), custom_call_target="tpu_custom_call", output_to_operand_aliasing={{0}: (7, {}), {1}: (8, {})} | custom-call | tf_op jit(solution)/shard_map/finish/pallas_call | solution.py:470
  (1 shorter events, 0.0 us)
Async XLA Ops:
  3.2 6.4 %collective-permute-start = (f32[4,512]{1,0:T(4,128)S(1)}, f32[4,512]{1,0:T(4,128)S(1)}, u32[]{:S(2)}, u32[]{:S(2)}) collective-permute-start(f32[4,512]{1,0:T(4,128)S(1)} %get-tuple-element.36), channel_id=1, source_target_pairs={{0,4},{4,8},{8,12},{12,16},{16,20},{20,24},{24,28},{28,0},{1,5},{5... | collective-permute-start | bytes 24584 | tf_op jit(solution)/shard_map/ppermute | solution.py:499
  4.9 4.3 %collective-permute-start.2 = (f32[4,512]{1,0:T(4,128)S(1)}, f32[4,512]{1,0:T(4,128)S(1)}, u32[]{:S(2)}, u32[]{:S(2)}) collective-permute-start(f32[4,512]{1,0:T(4,128)S(1)} %get-tuple-element.47), channel_id=1, source_target_pairs={{0,3},{1,2},{2,1},{3,0},{4,5},{5,4},{6,7},{7,6},{8,9},{9,8},{10,11... | collective-permute-start | bytes 24584 | tf_op jit(solution)/shard_map/ppermute | solution.py:500
  5.6 4.0 %collective-permute-start.1 = (f32[4,512]{1,0:T(4,128)S(1)}, f32[4,512]{1,0:T(4,128)S(1)}, u32[]{:S(2)}, u32[]{:S(2)}) collective-permute-start(f32[4,512]{1,0:T(4,128)S(1)} %get-tuple-element.40), channel_id=1, source_target_pairs={{0,28},{4,0},{8,4},{12,8},{16,12},{20,16},{24,20},{28,24},{1,29},{... | collective-permute-start | bytes 24584 | tf_op jit(solution)/shard_map/ppermute | solution.py:501
  8.1 1.2 %collective-permute-start.3 = (f32[4,512]{1,0:T(4,128)S(1)}, f32[4,512]{1,0:T(4,128)S(1)}, u32[]{:S(2)}, u32[]{:S(2)}) collective-permute-start(f32[4,512]{1,0:T(4,128)S(1)} %get-tuple-element.48), channel_id=1, source_target_pairs={{0,1},{1,0},{2,3},{3,2},{4,7},{5,6},{6,5},{7,4},{8,11},{9,10},{10,... | collective-permute-start | bytes 24584 | tf_op jit(solution)/shard_map/ppermute | solution.py:502

commit v7 on v6

--- a/solution.py
+++ b/solution.py
@@ -148,6 +148,7 @@
     weights_low, weights_high = tail_weights(False), tail_weights(True)
     put_inverses(k_ref)
     put_side_tables(table_x, table_y)
+
     def put_x(lanes):
         to_low_x[:, lanes] = message(u_near[pl.ds(0, STRIP), lanes], False, weights_low)
         to_high_x[:, lanes] = message(u_near[pl.ds(rows - STRIP, STRIP), lanes], True, weights_high)
@@ -206,16 +207,16 @@
             solved_ref[s, :, lanes] = solved
             strips[s, 0, :, lanes] = solved[:EDGE]
             strips[s, 1, :, lanes] = solved[rows - EDGE :]
-        if s < len(copies):
+        if s in copies:
             copies[s].start()
 
 
-def inner_copies(solved_ref, outs, sems):
+def inner_copies(solved_ref, outs, sems, systems):
     rows = solved_ref.shape[1]
     if rows <= 2 * EDGE:
-        return []
+        return {}
     inner = pl.ds(EDGE, rows - 2 * EDGE)
-    return [pltpu.make_async_copy(solved_ref.at[s, inner], out.at[inner], sems.at[s]) for s, out in enumerate(outs)]
+    return {s: pltpu.make_async_copy(solved_ref.at[s, inner], outs[s].at[inner], sems.at[s]) for s in systems}
 
 
 def solve_y(u_ref, k_ref, strips, solved_ref):
@@ -263,9 +264,9 @@
 
     @pl.when(solves_x() == FIRST)
     def _():
-        copies = inner_copies(solved_x, (dx,), sems)
+        copies = inner_copies(solved_x, (dx,), sems, (0,))
         solve_x(u_ref, k_ref, strips_x, solved_x, copies)
-        for copy in copies:
+        for copy in copies.values():
             copy.wait()
 
 
@@ -276,7 +277,7 @@
 
     @pl.when(solves_x() == BETWEEN)
     def _():
-        solve_x(u_ref, k_ref, strips_x, solved_x, [])
+        solve_x(u_ref, k_ref, strips_x, solved_x, {})
 
 
 def interior_kernel(u_ref, k_ref, _, first_strips, first_solved, between_strips, between_solved, *refs):
@@ -289,17 +290,15 @@
 
         @pl.when(solves_x() == when)
         def _():
-            copies = inner_copies(solved, (dx, dxx), sems)
+            copies = inner_copies(solved, (dx, dxx), sems, (1,) if when == FIRST else (0, 1))
             if when == LAST:
                 solve_x(u_ref, k_ref, strips, solved, copies)
             else:
-                if when == FIRST:
-                    copies = copies[1:]
-                for copy in copies:
+                for copy in copies.values():
                     copy.start()
                 strips_x[...] = strips[...]
             solve_y(u_ref, k_ref, strips_y, solved_y)
-            for copy in copies:
+            for copy in copies.values():
                 copy.wait()
 
 
@@ -338,9 +337,14 @@
 
 
 def sides_kernel(
-    from_y_first, from_y_second, near_low, near_high, table_y, strips_y, done_y
+    from_y_first, from_y_second, near_low, near_high, table_y, strips_y, solved_y, *done_y
 ):
     rows = near_low.shape[1]
+    columns = done_y[0].shape[1]
+    lanes_of = pl.ds(0, TILE), pl.ds(columns - TILE, TILE)
+    if columns > 2 * TILE:
+        for s in range(2):
+            done_y[s][:, pl.ds(TILE, columns - 2 * TILE)] = solved_y[s]
     row = lax.broadcasted_iota(jnp.int32, (8, 1), 0)
     low_first = low_goes_first()
     for lines in tiles_of(rows):
@@ -358,10 +362,10 @@
         for s in range(2):
             for side in range(2):
                 block = 2 * s + side
-                done_y[s, side, lines] = strips_y[s, side, lines] + added[:, block * TILE : (block + 1) * TILE]
-
-
-def finish_kernel(from_low_x, from_high_x, u_near, table_x, strips_x, done_y, solved_y, *refs):
+                done_y[s][lines, lanes_of[side]] = strips_y[s, side, lines] + added[:, block * TILE : (block + 1) * TILE]
+
+
+def finish_kernel(from_low_x, from_high_x, u_near, table_x, strips_x, done_y, done_yy, *refs):
     dx, dxx, dy, dyy, done_x, sems = refs[2:]
     rows, columns = dx.shape
     started = []
@@ -371,18 +375,14 @@
         copy.start()
         started.append(copy)
 
-    for s, out in enumerate((dy, dyy)):
-        for side in range(2):
-            send(done_y.at[s, side], out.at[:, pl.ds(side * (columns - TILE), TILE)])
+    send(done_y, dy)
+    send(done_yy, dyy)
     for lanes in tiles_of(columns):
         add_side_x(low_terms(from_low_x[:, lanes], u_near[pl.ds(0, 8), lanes]), 0, lanes, table_x, strips_x, done_x.at[0])
         add_side_x(high_terms(from_high_x[:, lanes], u_near[pl.ds(rows - 8, 8), lanes]), 1, lanes, table_x, strips_x, done_x.at[1])
     for s, out in enumerate((dx, dxx)):
         for side in range(2):
             send(done_x.at[side, s], out.at[pl.ds(side * (rows - EDGE), EDGE)])
-    if columns > 2 * TILE:
-        for s, out in enumerate((dy, dyy)):
-            send(solved_y.at[s], out.at[:, pl.ds(TILE, columns - 2 * TILE)])
     for copy in started:
         copy.wait()
 
@@ -454,15 +454,15 @@
     )(near(u_near), near(inverses), dx, *(near(a) for a in early))
 
 
-def sides(arrays, strips_y):
+def sides(size, *arrays):
     return pl.pallas_call(
         sides_kernel,
         name="sides",
-        out_shape=on_chip(*strips_y.shape),
-        in_specs=[VMEM] * 6,
-        out_specs=VMEM,
+        out_shape=(on_chip(*size),) * 2,
+        in_specs=[VMEM] * 7,
+        out_specs=[VMEM] * 2,
         compiler_params=LIMIT,
-    )(*(near(a) for a in (*arrays, strips_y)))
+    )(*(near(a) for a in arrays))
 
 
 def finish(arrays, parts):
@@ -474,7 +474,7 @@
         in_specs=[VMEM] * 7 + [ANY] * 2,
         out_specs=[ANY] * 4,
         input_output_aliases={7: 0, 8: 1},
-        scratch_shapes=[on_chip(2, 2, EDGE, columns), pltpu.SemaphoreType.DMA((10,))],
+        scratch_shapes=[on_chip(2, 2, EDGE, columns), pltpu.SemaphoreType.DMA((6,))],
         compiler_params=LIMIT,
     )(*(near(a) for a in arrays), *parts)
 
@@ -502,8 +502,8 @@
     from_y_second = lax.ppermute(to_y_second, ("gx", "gy"), second)
     strips_x, dx, dxx, strips_y, solved_y = interior(u_near, inverses, dx, *early, *between)
     table_x, table_y = tables
-    done_y = sides((from_y_first, from_y_second, near_low, near_high, table_y), strips_y)
-    dx, dxx, dy, dyy = finish((from_low_x, from_high_x, u_near, table_x, strips_x, done_y, solved_y), (dx, dxx))
+    done = sides(size, from_y_first, from_y_second, near_low, near_high, table_y, strips_y, solved_y)
+    dx, dxx, dy, dyy = finish((from_low_x, from_high_x, u_near, table_x, strips_x, *done), (dx, dxx))
     return tuple(o[None] for o in (dx, dy, dxx, dyy))
 
 

time: 10.9 us -> 10.8 us (level)
  no operation moved by 1% of the time
where the time goes in v7:
time: 10.8 us; the launch traced here: 10.7 us
  starting transfers between devices  5.09 us (47%)
  Pallas kernels  4.82 us (45%)
  between operations  0.69 us (6%)
    ppermute x1, starting transfers between devices, local(): lax.ppermute(to_low_x, 'gx', [(i, (i - 1) % gx) for i in range(gx)])  2.55 us
    ppermute x1, starting transfers between devices, local(): lax.ppermute(to_high_x, 'gx', [(i, (i + 1) % gx) for i in range(gx)])  1.72 us
    pallas_call x2, Pallas kernels, lead(): pl.pallas_call(kernel, name=name, out_shape=tuple((on_chip(*a.shape) for...  1.3 us
    pallas_call x1, Pallas kernels, pack(): pl.pallas_call(pack_kernel, name='pack', out_shape=(on_chip(MESSAGE, colu...  1.21 us
    pallas_call x1, Pallas kernels, finish(): pl.pallas_call(finish_kernel, name='finish', out_shape=(pltpu.HBM(parts[0...  1.07 us
    pallas_call x1, Pallas kernels, interior(): pl.pallas_call(interior_kernel, name='interior', out_shape=(strips_x,) +...  0.95 us
    ppermute x1, starting transfers between devices, local(): from_y_first = lax.ppermute(to_y_first, ('gx', 'gy'), first)  0.68 us
    pallas_call x1, Pallas kernels, sides(): pl.pallas_call(sides_kernel, name='sides', out_shape=(on_chip(*size),) *...  0.28 us
  transfers between devices with their start and end apart: 4, of which 1 were waited for; matrix products, arithmetic and copies ran while one was open for 0% of the time, Pallas kernels for 12%

profile of v7, /device:TPU:0, one launch (start us, length us, event | category | flops | bytes accessed | tf_op | source)
XLA Modules:
  0.0 10.7 jit_solution(5870082672756152336)
XLA Ops:
  0.6 1.2 %pack.1 = (f32[4,512]{1,0:T(4,128)S(1)}, f32[4,512]{1,0:T(4,128)S(1)}, f32[4,512]{1,0:T(4,128)S(1)}, f32[4,512]{1,0:T(4,128)S(1)}, f32[256,512]{1,0:T(8,128)S(1)...) custom-call(f32[256,512]{1,0:T(8,128)} %bitcast.6), custom_call_target="tpu_custom_call" | custom-call | tf_op jit(solution)/shard_map/pack/pallas_call | solution.py:401
  1.9 1.3 %solve_first.1 = (f32[4,512]{1,0:T(4,128)S(1)}, f32[4,512]{1,0:T(4,128)S(1)}, f32[256,512]{1,0:T(8,128)}, f32[2,2,24,512]{3,2,1,0:T(8,128)S(1)}, f32[2,256,512]{2,1,0:T(8,128)S(1)}) custom-call(f32[256,512]{1,0:T(8,128)S(1)} %get-tuple-element.34.u_ref.u_near, bf16[4,256,256]{2,1,0:T(8,128)(2,1)S(1)} %get-tuple-element.35.k_ref, ...), custom_call_target="tpu_custom_call" | custom-call | tf_op jit(solution)/shard_map/solve_first/pallas_call | solution.py:428
  3.2 1.7 %collective-permute-start = (f32[4,512]{1,0:T(4,128)S(1)}, f32[4,512]{1,0:T(4,128)S(1)}, u32[]{:S(2)}, u32[]{:S(2)}) collective-permute-start(f32[4,512]{1,0:T(4,128)S(1)} %get-tuple-element.38), channel_id=1, source_target_pairs={{0,4},{4,8},{8,12},{12,16},{16,20},{20,24},{24,28},{28,0},{1,5},{5... | collective-permute-start | bytes 24584 | tf_op jit(solution)/shard_map/ppermute | solution.py:499
  4.9 0.7 %collective-permute-start.2 = (f32[4,512]{1,0:T(4,128)S(1)}, f32[4,512]{1,0:T(4,128)S(1)}, u32[]{:S(2)}, u32[]{:S(2)}) collective-permute-start(f32[4,512]{1,0:T(4,128)S(1)} %get-tuple-element.49), channel_id=1, source_target_pairs={{0,3},{1,2},{2,1},{3,0},{4,5},{5,4},{6,7},{7,6},{8,9},{9,8},{10,11... | collective-permute-start | bytes 24584 | tf_op jit(solution)/shard_map/ppermute | solution.py:500
  5.6 2.5 %collective-permute-start.1 = (f32[4,512]{1,0:T(4,128)S(1)}, f32[4,512]{1,0:T(4,128)S(1)}, u32[]{:S(2)}, u32[]{:S(2)}) collective-permute-start(f32[4,512]{1,0:T(4,128)S(1)} %get-tuple-element.42), channel_id=1, source_target_pairs={{0,28},{4,0},{8,4},{12,8},{16,12},{20,16},{24,20},{28,24},{1,29},{... | collective-permute-start | bytes 24584 | tf_op jit(solution)/shard_map/ppermute | solution.py:501
  8.1 0.1 %collective-permute-start.3 = (f32[4,512]{1,0:T(4,128)S(1)}, f32[4,512]{1,0:T(4,128)S(1)}, u32[]{:S(2)}, u32[]{:S(2)}) collective-permute-start(f32[4,512]{1,0:T(4,128)S(1)} %get-tuple-element.50), channel_id=1, source_target_pairs={{0,1},{1,0},{2,3},{3,2},{4,7},{5,6},{6,5},{7,4},{8,11},{9,10},{10,... | collective-permute-start | bytes 24584 | tf_op jit(solution)/shard_map/ppermute | solution.py:502
  8.3 1.0 %interior.1 = (f32[2,2,24,512]{3,2,1,0:T(8,128)S(1)}, f32[256,512]{1,0:T(8,128)}, f32[256,512]{1,0:T(8,128)}, f32[2,2,256,128]{3,2,1,0:T(8,128)S(1)}, f32[2,256,256]{2,1,0:T(8,128)S(1)}) custom-call(f32[256,512]{1,0:T(8,128)S(1)} %get-tuple-element.34.u_ref.u_near, ...), custom_call_target="tpu_custom_call", output_to_operand_aliasing={{1}: (2, {})} | custom-call | flops 536870912 | bytes 2621440 | tf_op jit(solution)/shard_map/interior/pallas_call | solution.py:442
  9.2 0.0 collective-permute-done.2.from_y_first
  9.2 0.1 collective-permute-done.3.from_y_second
  9.3 0.3 %sides.1 = (f32[256,512]{1,0:T(8,128)S(1)}, f32[256,512]{1,0:T(8,128)S(1)}) custom-call(f32[4,512]{1,0:T(4,128)S(1)} %collective-permute-done.2.from_y_first, f32[4,512]{1,0:T(4,128)S(1)} %collective-permute-done.3.from_y_second, f32[8,256]{1,0:T(8,128)S(1)} %get-tuple-element.51.near_low, f32[8,256]{1,0:T(8,128)S(1)} %get-tuple-element.52.near_high, ...), custom_call_target="tpu_custom_call" | custom-call | tf_op jit(solution)/shard_map/sides/pallas_call | solution.py:458
  9.6 0.0 collective-permute-done.from_low_x
  9.6 0.0 collective-permute-done.1.from_high_x
  9.6 1.1 %finish.1 = (f32[256,512]{1,0:T(8,128)}, f32[256,512]{1,0:T(8,128)}, f32[256,512]{1,0:T(8,128)}, f32[256,512]{1,0:T(8,128)}) custom-call(f32[4,512]{1,0:T(4,128)S(1)} %collective-permute-done.from_low_x, f32[4,512]{1,0:T(4,128)S(1)} %collective-permute-done.1.from_high_x, ...), custom_call_target="tpu_custom_call", output_to_operand_aliasing={{0}: (7, {}), {1}: (8, {})} | custom-call | tf_op jit(solution)/shard_map/finish/pallas_call | solution.py:470
  (1 shorter events, 0.0 us)
Async XLA Ops:
  3.2 6.4 %collective-permute-start = (f32[4,512]{1,0:T(4,128)S(1)}, f32[4,512]{1,0:T(4,128)S(1)}, u32[]{:S(2)}, u32[]{:S(2)}) collective-permute-start(f32[4,512]{1,0:T(4,128)S(1)} %get-tuple-element.38), channel_id=1, source_target_pairs={{0,4},{4,8},{8,12},{12,16},{16,20},{20,24},{24,28},{28,0},{1,5},{5... | collective-permute-start | bytes 24584 | tf_op jit(solution)/shard_map/ppermute | solution.py:499
  4.9 4.3 %collective-permute-start.2 = (f32[4,512]{1,0:T(4,128)S(1)}, f32[4,512]{1,0:T(4,128)S(1)}, u32[]{:S(2)}, u32[]{:S(2)}) collective-permute-start(f32[4,512]{1,0:T(4,128)S(1)} %get-tuple-element.49), channel_id=1, source_target_pairs={{0,3},{1,2},{2,1},{3,0},{4,5},{5,4},{6,7},{7,6},{8,9},{9,8},{10,11... | collective-permute-start | bytes 24584 | tf_op jit(solution)/shard_map/ppermute | solution.py:500
  5.6 4.0 %collective-permute-start.1 = (f32[4,512]{1,0:T(4,128)S(1)}, f32[4,512]{1,0:T(4,128)S(1)}, u32[]{:S(2)}, u32[]{:S(2)}) collective-permute-start(f32[4,512]{1,0:T(4,128)S(1)} %get-tuple-element.42), channel_id=1, source_target_pairs={{0,28},{4,0},{8,4},{12,8},{16,12},{20,16},{24,20},{28,24},{1,29},{... | collective-permute-start | bytes 24584 | tf_op jit(solution)/shard_map/ppermute | solution.py:501
  8.1 1.2 %collective-permute-start.3 = (f32[4,512]{1,0:T(4,128)S(1)}, f32[4,512]{1,0:T(4,128)S(1)}, u32[]{:S(2)}, u32[]{:S(2)}) collective-permute-start(f32[4,512]{1,0:T(4,128)S(1)} %get-tuple-element.50), channel_id=1, source_target_pairs={{0,1},{1,0},{2,3},{3,2},{4,7},{5,6},{6,5},{7,4},{8,11},{9,10},{10,... | collective-permute-start | bytes 24584 | tf_op jit(solution)/shard_map/ppermute | solution.py:502

commit v8 on v7

--- a/solution.py
+++ b/solution.py
@@ -258,9 +258,7 @@
 
 
 def first_kernel(u_ref, k_ref, *refs):
-    messages, passed, (dx, strips_x, solved_x, sems) = refs[:2], refs[2:4], refs[4:]
-    for message_ref, passed_ref in zip(messages, passed):
-        passed_ref[...] = message_ref[...]
+    dx, strips_x, solved_x, sems = refs[4:]
 
     @pl.when(solves_x() == FIRST)
     def _():
@@ -271,9 +269,7 @@
 
 
 def between_kernel(u_ref, k_ref, *refs):
-    messages, passed, (strips_x, solved_x) = refs[:2], refs[3:5], refs[5:]
-    for message_ref, passed_ref in zip(messages, passed):
-        passed_ref[...] = message_ref[...]
+    strips_x, solved_x = refs[5:]
 
     @pl.when(solves_x() == BETWEEN)
     def _():
@@ -429,8 +425,9 @@
         kernel,
         name=name,
         out_shape=tuple(on_chip(*a.shape) for a in messages[:2]) + outs,
-        in_specs=[VMEM] * (2 + len(messages)),
-        out_specs=[VMEM] * 2 + [ANY] * (len(outs) - 2) + [VMEM] * 2,
+        in_specs=[VMEM] * 2 + [ANY] * len(messages),
+        out_specs=[ANY] * 2 + [ANY] * (len(outs) - 2) + [VMEM] * 2,
+        input_output_aliases={2: 0, 3: 1},
         scratch_shapes=scratch,
         compiler_params=LIMIT,
     )(*(near(a) for a in (u_near, inverses, *messages)))

time: 10.8 us -> 10.8 us (level)
  no operation moved by 1% of the time
where the time goes in v8:
time: 10.8 us; the launch traced here: 10.7 us
  starting transfers between devices  5.09 us (47%)
  Pallas kernels  4.82 us (45%)
  between operations  0.69 us (6%)
    ppermute x1, starting transfers between devices, local(): lax.ppermute(to_low_x, 'gx', [(i, (i - 1) % gx) for i in range(gx)])  2.55 us
    ppermute x1, starting transfers between devices, local(): lax.ppermute(to_high_x, 'gx', [(i, (i + 1) % gx) for i in range(gx)])  1.72 us
    pallas_call x2, Pallas kernels, lead(): pl.pallas_call(kernel, name=name, out_shape=tuple((on_chip(*a.shape) for...  1.3 us
    pallas_call x1, Pallas kernels, pack(): pl.pallas_call(pack_kernel, name='pack', out_shape=(on_chip(MESSAGE, colu...  1.21 us
    pallas_call x1, Pallas kernels, finish(): pl.pallas_call(finish_kernel, name='finish', out_shape=(pltpu.HBM(parts[0...  1.07 us
    pallas_call x1, Pallas kernels, interior(): pl.pallas_call(interior_kernel, name='interior', out_shape=(strips_x,) +...  0.95 us
    ppermute x1, starting transfers between devices, local(): from_y_first = lax.ppermute(to_y_first, ('gx', 'gy'), first)  0.68 us
    pallas_call x1, Pallas kernels, sides(): pl.pallas_call(sides_kernel, name='sides', out_shape=(on_chip(*size),) *...  0.28 us
  transfers between devices with their start and end apart: 4, of which 1 were waited for; matrix products, arithmetic and copies ran while one was open for 0% of the time, Pallas kernels for 12%

profile of v8, /device:TPU:0, one launch (start us, length us, event | category | flops | bytes accessed | tf_op | source)
XLA Modules:
  0.0 10.7 jit_solution(15292450016848124265)
XLA Ops:
  0.6 1.2 %pack.1 = (f32[4,512]{1,0:T(4,128)S(1)}, f32[4,512]{1,0:T(4,128)S(1)}, f32[4,512]{1,0:T(4,128)S(1)}, f32[4,512]{1,0:T(4,128)S(1)}, f32[256,512]{1,0:T(8,128)S(1)...) custom-call(f32[256,512]{1,0:T(8,128)} %bitcast.6), custom_call_target="tpu_custom_call" | custom-call | tf_op jit(solution)/shard_map/pack/pallas_call | solution.py:397
  1.9 1.3 %solve_first.1 = (f32[4,512]{1,0:T(4,128)S(1)}, f32[4,512]{1,0:T(4,128)S(1)}, f32[256,512]{1,0:T(8,128)}, f32[2,2,24,512]{3,2,1,0:T(8,128)S(1)}, f32[2,256,512]{2,1,0:T(8,128)S(1)}) custom-call(f32[256,512]{1,0:T(8,128)S(1)} %get-tuple-element.34.u_ref.u_near, ...), custom_call_target="tpu_custom_call", output_to_operand_aliasing={{0}: (2, {}), {1}: (3, {})} | custom-call | tf_op jit(solution)/shard_map/solve_first/pallas_call | solution.py:424
  3.2 1.7 %collective-permute-start = (f32[4,512]{1,0:T(4,128)S(1)}, f32[4,512]{1,0:T(4,128)S(1)}, u32[]{:S(2)}, u32[]{:S(2)}) collective-permute-start(f32[4,512]{1,0:T(4,128)S(1)} %get-tuple-element.38), channel_id=1, source_target_pairs={{0,4},{4,8},{8,12},{12,16},{16,20},{20,24},{24,28},{28,0},{1,5},{5... | collective-permute-start | bytes 24584 | tf_op jit(solution)/shard_map/ppermute | solution.py:496
  4.9 0.7 %collective-permute-start.2 = (f32[4,512]{1,0:T(4,128)S(1)}, f32[4,512]{1,0:T(4,128)S(1)}, u32[]{:S(2)}, u32[]{:S(2)}) collective-permute-start(f32[4,512]{1,0:T(4,128)S(1)} %get-tuple-element.49), channel_id=1, source_target_pairs={{0,3},{1,2},{2,1},{3,0},{4,5},{5,4},{6,7},{7,6},{8,9},{9,8},{10,11... | collective-permute-start | bytes 24584 | tf_op jit(solution)/shard_map/ppermute | solution.py:497
  5.6 2.5 %collective-permute-start.1 = (f32[4,512]{1,0:T(4,128)S(1)}, f32[4,512]{1,0:T(4,128)S(1)}, u32[]{:S(2)}, u32[]{:S(2)}) collective-permute-start(f32[4,512]{1,0:T(4,128)S(1)} %get-tuple-element.42), channel_id=1, source_target_pairs={{0,28},{4,0},{8,4},{12,8},{16,12},{20,16},{24,20},{28,24},{1,29},{... | collective-permute-start | bytes 24584 | tf_op jit(solution)/shard_map/ppermute | solution.py:498
  8.1 0.1 %collective-permute-start.3 = (f32[4,512]{1,0:T(4,128)S(1)}, f32[4,512]{1,0:T(4,128)S(1)}, u32[]{:S(2)}, u32[]{:S(2)}) collective-permute-start(f32[4,512]{1,0:T(4,128)S(1)} %get-tuple-element.50), channel_id=1, source_target_pairs={{0,1},{1,0},{2,3},{3,2},{4,7},{5,6},{6,5},{7,4},{8,11},{9,10},{10,... | collective-permute-start | bytes 24584 | tf_op jit(solution)/shard_map/ppermute | solution.py:499
  8.3 1.0 %interior.1 = (f32[2,2,24,512]{3,2,1,0:T(8,128)S(1)}, f32[256,512]{1,0:T(8,128)}, f32[256,512]{1,0:T(8,128)}, f32[2,2,256,128]{3,2,1,0:T(8,128)S(1)}, f32[2,256,256]{2,1,0:T(8,128)S(1)}) custom-call(f32[256,512]{1,0:T(8,128)S(1)} %get-tuple-element.34.u_ref.u_near, ...), custom_call_target="tpu_custom_call", output_to_operand_aliasing={{1}: (2, {})} | custom-call | flops 536870912 | bytes 2621440 | tf_op jit(solution)/shard_map/interior/pallas_call | solution.py:439
  9.2 0.0 collective-permute-done.2.from_y_first
  9.2 0.1 collective-permute-done.3.from_y_second
  9.3 0.3 %sides.1 = (f32[256,512]{1,0:T(8,128)S(1)}, f32[256,512]{1,0:T(8,128)S(1)}) custom-call(f32[4,512]{1,0:T(4,128)S(1)} %collective-permute-done.2.from_y_first, f32[4,512]{1,0:T(4,128)S(1)} %collective-permute-done.3.from_y_second, f32[8,256]{1,0:T(8,128)S(1)} %get-tuple-element.51.near_low, f32[8,256]{1,0:T(8,128)S(1)} %get-tuple-element.52.near_high, ...), custom_call_target="tpu_custom_call" | custom-call | tf_op jit(solution)/shard_map/sides/pallas_call | solution.py:455
  9.6 0.0 collective-permute-done.from_low_x
  9.6 0.0 collective-permute-done.1.from_high_x
  9.6 1.1 %finish.1 = (f32[256,512]{1,0:T(8,128)}, f32[256,512]{1,0:T(8,128)}, f32[256,512]{1,0:T(8,128)}, f32[256,512]{1,0:T(8,128)}) custom-call(f32[4,512]{1,0:T(4,128)S(1)} %collective-permute-done.from_low_x, f32[4,512]{1,0:T(4,128)S(1)} %collective-permute-done.1.from_high_x, ...), custom_call_target="tpu_custom_call", output_to_operand_aliasing={{0}: (7, {}), {1}: (8, {})} | custom-call | tf_op jit(solution)/shard_map/finish/pallas_call | solution.py:467
  (1 shorter events, 0.0 us)
Async XLA Ops:
  3.2 6.4 %collective-permute-start = (f32[4,512]{1,0:T(4,128)S(1)}, f32[4,512]{1,0:T(4,128)S(1)}, u32[]{:S(2)}, u32[]{:S(2)}) collective-permute-start(f32[4,512]{1,0:T(4,128)S(1)} %get-tuple-element.38), channel_id=1, source_target_pairs={{0,4},{4,8},{8,12},{12,16},{16,20},{20,24},{24,28},{28,0},{1,5},{5... | collective-permute-start | bytes 24584 | tf_op jit(solution)/shard_map/ppermute | solution.py:496
  4.9 4.3 %collective-permute-start.2 = (f32[4,512]{1,0:T(4,128)S(1)}, f32[4,512]{1,0:T(4,128)S(1)}, u32[]{:S(2)}, u32[]{:S(2)}) collective-permute-start(f32[4,512]{1,0:T(4,128)S(1)} %get-tuple-element.49), channel_id=1, source_target_pairs={{0,3},{1,2},{2,1},{3,0},{4,5},{5,4},{6,7},{7,6},{8,9},{9,8},{10,11... | collective-permute-start | bytes 24584 | tf_op jit(solution)/shard_map/ppermute | solution.py:497
  5.6 4.0 %collective-permute-start.1 = (f32[4,512]{1,0:T(4,128)S(1)}, f32[4,512]{1,0:T(4,128)S(1)}, u32[]{:S(2)}, u32[]{:S(2)}) collective-permute-start(f32[4,512]{1,0:T(4,128)S(1)} %get-tuple-element.42), channel_id=1, source_target_pairs={{0,28},{4,0},{8,4},{12,8},{16,12},{20,16},{24,20},{28,24},{1,29},{... | collective-permute-start | bytes 24584 | tf_op jit(solution)/shard_map/ppermute | solution.py:498
  8.1 1.2 %collective-permute-start.3 = (f32[4,512]{1,0:T(4,128)S(1)}, f32[4,512]{1,0:T(4,128)S(1)}, u32[]{:S(2)}, u32[]{:S(2)}) collective-permute-start(f32[4,512]{1,0:T(4,128)S(1)} %get-tuple-element.50), channel_id=1, source_target_pairs={{0,1},{1,0},{2,3},{3,2},{4,7},{5,6},{6,5},{7,4},{8,11},{9,10},{10,... | collective-permute-start | bytes 24584 | tf_op jit(solution)/shard_map/ppermute | solution.py:499

commit v9 on v8

--- a/solution.py
+++ b/solution.py
@@ -131,7 +131,7 @@
     rows, columns = u_ref.shape
     across = [pl.ds(0, TILE), pl.ds(columns - TILE, TILE)]
     pieces = [(pl.ds(0, rows), lanes) for lanes in across]
-    order = (2, 3, 0, 1, 4)
+    order = (0, 2, 1, 3, 4)
     if columns > 2 * TILE:
         middle = pl.ds(TILE, columns - 2 * TILE)
         pieces += [(pl.ds(0, STRIP), middle), (pl.ds(rows - STRIP, STRIP), middle)]
@@ -153,10 +153,6 @@
         to_low_x[:, lanes] = message(u_near[pl.ds(0, STRIP), lanes], False, weights_low)
         to_high_x[:, lanes] = message(u_near[pl.ds(rows - STRIP, STRIP), lanes], True, weights_high)
 
-    for copy in copies[2:4]:
-        copy.wait()
-    for lanes in tiles_of(columns)[1:-1]:
-        put_x(lanes)
     low, high = [], []
     for k in range(2):
         copies[k].wait()
@@ -170,6 +166,10 @@
     for lanes, to_low, to_high in zip(tiles_of(rows), low, high):
         to_y_first[:, lanes] = jnp.where(low_first, to_low, to_high)
         to_y_second[:, lanes] = jnp.where(low_first, to_high, to_low)
+    for copy in copies[2:4]:
+        copy.wait()
+    for lanes in tiles_of(columns)[1:-1]:
+        put_x(lanes)
     for copy in copies[4:]:
         copy.wait()
 

time: 10.8 us -> 10.8 us (level)
  no operation moved by 1% of the time
where the time goes in v9:
time: 10.8 us; the launch traced here: 10.7 us
  starting transfers between devices  5.09 us (47%)
  Pallas kernels  4.82 us (45%)
  between operations  0.69 us (6%)
    ppermute x1, starting transfers between devices, local(): lax.ppermute(to_low_x, 'gx', [(i, (i - 1) % gx) for i in range(gx)])  2.55 us
    ppermute x1, starting transfers between devices, local(): lax.ppermute(to_high_x, 'gx', [(i, (i + 1) % gx) for i in range(gx)])  1.72 us
    pallas_call x2, Pallas kernels, lead(): pl.pallas_call(kernel, name=name, out_shape=tuple((on_chip(*a.shape) for...  1.3 us
    pallas_call x1, Pallas kernels, pack(): pl.pallas_call(pack_kernel, name='pack', out_shape=(on_chip(MESSAGE, colu...  1.21 us
    pallas_call x1, Pallas kernels, finish(): pl.pallas_call(finish_kernel, name='finish', out_shape=(pltpu.HBM(parts[0...  1.07 us
    pallas_call x1, Pallas kernels, interior(): pl.pallas_call(interior_kernel, name='interior', out_shape=(strips_x,) +...  0.95 us
    ppermute x1, starting transfers between devices, local(): from_y_first = lax.ppermute(to_y_first, ('gx', 'gy'), first)  0.68 us
    pallas_call x1, Pallas kernels, sides(): pl.pallas_call(sides_kernel, name='sides', out_shape=(on_chip(*size),) *...  0.28 us
  transfers between devices with their start and end apart: 4, of which 1 were waited for; matrix products, arithmetic and copies ran while one was open for 0% of the time, Pallas kernels for 12%

profile of v9, /device:TPU:0, one launch (start us, length us, event | category | flops | bytes accessed | tf_op | source)
XLA Modules:
  0.0 10.7 jit_solution(10878797053961293691)
XLA Ops:
  0.6 1.2 %pack.1 = (f32[4,512]{1,0:T(4,128)S(1)}, f32[4,512]{1,0:T(4,128)S(1)}, f32[4,512]{1,0:T(4,128)S(1)}, f32[4,512]{1,0:T(4,128)S(1)}, f32[256,512]{1,0:T(8,128)S(1)...) custom-call(f32[256,512]{1,0:T(8,128)} %bitcast.6), custom_call_target="tpu_custom_call" | custom-call | tf_op jit(solution)/shard_map/pack/pallas_call | solution.py:397
  1.9 1.3 %solve_first.1 = (f32[4,512]{1,0:T(4,128)S(1)}, f32[4,512]{1,0:T(4,128)S(1)}, f32[256,512]{1,0:T(8,128)}, f32[2,2,24,512]{3,2,1,0:T(8,128)S(1)}, f32[2,256,512]{2,1,0:T(8,128)S(1)}) custom-call(f32[256,512]{1,0:T(8,128)S(1)} %get-tuple-element.34.u_ref.u_near, ...), custom_call_target="tpu_custom_call", output_to_operand_aliasing={{0}: (2, {}), {1}: (3, {})} | custom-call | tf_op jit(solution)/shard_map/solve_first/pallas_call | solution.py:424
  3.2 1.7 %collective-permute-start = (f32[4,512]{1,0:T(4,128)S(1)}, f32[4,512]{1,0:T(4,128)S(1)}, u32[]{:S(2)}, u32[]{:S(2)}) collective-permute-start(f32[4,512]{1,0:T(4,128)S(1)} %get-tuple-element.38), channel_id=1, source_target_pairs={{0,4},{4,8},{8,12},{12,16},{16,20},{20,24},{24,28},{28,0},{1,5},{5... | collective-permute-start | bytes 24584 | tf_op jit(solution)/shard_map/ppermute | solution.py:496
  4.9 0.7 %collective-permute-start.2 = (f32[4,512]{1,0:T(4,128)S(1)}, f32[4,512]{1,0:T(4,128)S(1)}, u32[]{:S(2)}, u32[]{:S(2)}) collective-permute-start(f32[4,512]{1,0:T(4,128)S(1)} %get-tuple-element.49), channel_id=1, source_target_pairs={{0,3},{1,2},{2,1},{3,0},{4,5},{5,4},{6,7},{7,6},{8,9},{9,8},{10,11... | collective-permute-start | bytes 24584 | tf_op jit(solution)/shard_map/ppermute | solution.py:497
  5.6 2.5 %collective-permute-start.1 = (f32[4,512]{1,0:T(4,128)S(1)}, f32[4,512]{1,0:T(4,128)S(1)}, u32[]{:S(2)}, u32[]{:S(2)}) collective-permute-start(f32[4,512]{1,0:T(4,128)S(1)} %get-tuple-element.42), channel_id=1, source_target_pairs={{0,28},{4,0},{8,4},{12,8},{16,12},{20,16},{24,20},{28,24},{1,29},{... | collective-permute-start | bytes 24584 | tf_op jit(solution)/shard_map/ppermute | solution.py:498
  8.1 0.1 %collective-permute-start.3 = (f32[4,512]{1,0:T(4,128)S(1)}, f32[4,512]{1,0:T(4,128)S(1)}, u32[]{:S(2)}, u32[]{:S(2)}) collective-permute-start(f32[4,512]{1,0:T(4,128)S(1)} %get-tuple-element.50), channel_id=1, source_target_pairs={{0,1},{1,0},{2,3},{3,2},{4,7},{5,6},{6,5},{7,4},{8,11},{9,10},{10,... | collective-permute-start | bytes 24584 | tf_op jit(solution)/shard_map/ppermute | solution.py:499
  8.3 1.0 %interior.1 = (f32[2,2,24,512]{3,2,1,0:T(8,128)S(1)}, f32[256,512]{1,0:T(8,128)}, f32[256,512]{1,0:T(8,128)}, f32[2,2,256,128]{3,2,1,0:T(8,128)S(1)}, f32[2,256,256]{2,1,0:T(8,128)S(1)}) custom-call(f32[256,512]{1,0:T(8,128)S(1)} %get-tuple-element.34.u_ref.u_near, ...), custom_call_target="tpu_custom_call", output_to_operand_aliasing={{1}: (2, {})} | custom-call | flops 536870912 | bytes 2621440 | tf_op jit(solution)/shard_map/interior/pallas_call | solution.py:439
  9.2 0.0 collective-permute-done.2.from_y_first
  9.2 0.1 collective-permute-done.3.from_y_second
  9.3 0.3 %sides.1 = (f32[256,512]{1,0:T(8,128)S(1)}, f32[256,512]{1,0:T(8,128)S(1)}) custom-call(f32[4,512]{1,0:T(4,128)S(1)} %collective-permute-done.2.from_y_first, f32[4,512]{1,0:T(4,128)S(1)} %collective-permute-done.3.from_y_second, f32[8,256]{1,0:T(8,128)S(1)} %get-tuple-element.51.near_low, f32[8,256]{1,0:T(8,128)S(1)} %get-tuple-element.52.near_high, ...), custom_call_target="tpu_custom_call" | custom-call | tf_op jit(solution)/shard_map/sides/pallas_call | solution.py:455
  9.6 0.0 collective-permute-done.from_low_x
  9.6 0.0 collective-permute-done.1.from_high_x
  9.6 1.1 %finish.1 = (f32[256,512]{1,0:T(8,128)}, f32[256,512]{1,0:T(8,128)}, f32[256,512]{1,0:T(8,128)}, f32[256,512]{1,0:T(8,128)}) custom-call(f32[4,512]{1,0:T(4,128)S(1)} %collective-permute-done.from_low_x, f32[4,512]{1,0:T(4,128)S(1)} %collective-permute-done.1.from_high_x, ...), custom_call_target="tpu_custom_call", output_to_operand_aliasing={{0}: (7, {}), {1}: (8, {})} | custom-call | tf_op jit(solution)/shard_map/finish/pallas_call | solution.py:467
  (1 shorter events, 0.0 us)
Async XLA Ops:
  3.2 6.4 %collective-permute-start = (f32[4,512]{1,0:T(4,128)S(1)}, f32[4,512]{1,0:T(4,128)S(1)}, u32[]{:S(2)}, u32[]{:S(2)}) collective-permute-start(f32[4,512]{1,0:T(4,128)S(1)} %get-tuple-element.38), channel_id=1, source_target_pairs={{0,4},{4,8},{8,12},{12,16},{16,20},{20,24},{24,28},{28,0},{1,5},{5... | collective-permute-start | bytes 24584 | tf_op jit(solution)/shard_map/ppermute | solution.py:496
  4.9 4.3 %collective-permute-start.2 = (f32[4,512]{1,0:T(4,128)S(1)}, f32[4,512]{1,0:T(4,128)S(1)}, u32[]{:S(2)}, u32[]{:S(2)}) collective-permute-start(f32[4,512]{1,0:T(4,128)S(1)} %get-tuple-element.49), channel_id=1, source_target_pairs={{0,3},{1,2},{2,1},{3,0},{4,5},{5,4},{6,7},{7,6},{8,9},{9,8},{10,11... | collective-permute-start | bytes 24584 | tf_op jit(solution)/shard_map/ppermute | solution.py:497
  5.6 4.0 %collective-permute-start.1 = (f32[4,512]{1,0:T(4,128)S(1)}, f32[4,512]{1,0:T(4,128)S(1)}, u32[]{:S(2)}, u32[]{:S(2)}) collective-permute-start(f32[4,512]{1,0:T(4,128)S(1)} %get-tuple-element.42), channel_id=1, source_target_pairs={{0,28},{4,0},{8,4},{12,8},{16,12},{20,16},{24,20},{28,24},{1,29},{... | collective-permute-start | bytes 24584 | tf_op jit(solution)/shard_map/ppermute | solution.py:498
  8.1 1.2 %collective-permute-start.3 = (f32[4,512]{1,0:T(4,128)S(1)}, f32[4,512]{1,0:T(4,128)S(1)}, u32[]{:S(2)}, u32[]{:S(2)}) collective-permute-start(f32[4,512]{1,0:T(4,128)S(1)} %get-tuple-element.50), channel_id=1, source_target_pairs={{0,1},{1,0},{2,3},{3,2},{4,7},{5,6},{6,5},{7,4},{8,11},{9,10},{10,... | collective-permute-start | bytes 24584 | tf_op jit(solution)/shard_map/ppermute | solution.py:499

commit v10 on v9

--- a/solution.py
+++ b/solution.py
@@ -21,7 +21,7 @@
 
 WINDOW = 256
 TILE = 128
-STRIP = 32
+STRIP = 24
 EDGE = 24
 REACH = 64
 MESSAGE = 4

time: 10.8 us -> 10.8 us (level)
  no operation moved by 1% of the time
where the time goes in v10:
time: 10.8 us; the launch traced here: 10.6 us
  starting transfers between devices  5.1 us (47%)
  Pallas kernels  4.8 us (44%)
  between operations  0.69 us (6%)
    ppermute x1, starting transfers between devices, local(): lax.ppermute(to_low_x, 'gx', [(i, (i - 1) % gx) for i in range(gx)])  2.55 us
    ppermute x1, starting transfers between devices, local(): lax.ppermute(to_high_x, 'gx', [(i, (i + 1) % gx) for i in range(gx)])  1.72 us
    pallas_call x2, Pallas kernels, lead(): pl.pallas_call(kernel, name=name, out_shape=tuple((on_chip(*a.shape) for...  1.3 us
    pallas_call x1, Pallas kernels, pack(): pl.pallas_call(pack_kernel, name='pack', out_shape=(on_chip(MESSAGE, colu...  1.2 us
    pallas_call x1, Pallas kernels, finish(): pl.pallas_call(finish_kernel, name='finish', out_shape=(pltpu.HBM(parts[0...  1.07 us
    pallas_call x1, Pallas kernels, interior(): pl.pallas_call(interior_kernel, name='interior', out_shape=(strips_x,) +...  0.95 us
    ppermute x1, starting transfers between devices, local(): from_y_first = lax.ppermute(to_y_first, ('gx', 'gy'), first)  0.68 us
    pallas_call x1, Pallas kernels, sides(): pl.pallas_call(sides_kernel, name='sides', out_shape=(on_chip(*size),) *...  0.28 us
  transfers between devices with their start and end apart: 4, of which 1 were waited for; matrix products, arithmetic and copies ran while one was open for 0% of the time, Pallas kernels for 12%

profile of v10, /device:TPU:0, one launch (start us, length us, event | category | flops | bytes accessed | tf_op | source)
XLA Modules:
  0.0 10.6 jit_solution(9916276768396908854)
XLA Ops:
  0.6 1.2 %pack.1 = (f32[4,512]{1,0:T(4,128)S(1)}, f32[4,512]{1,0:T(4,128)S(1)}, f32[4,512]{1,0:T(4,128)S(1)}, f32[4,512]{1,0:T(4,128)S(1)}, f32[256,512]{1,0:T(8,128)S(1)...) custom-call(f32[256,512]{1,0:T(8,128)} %bitcast.6), custom_call_target="tpu_custom_call" | custom-call | tf_op jit(solution)/shard_map/pack/pallas_call | solution.py:397
  1.8 1.3 %solve_first.1 = (f32[4,512]{1,0:T(4,128)S(1)}, f32[4,512]{1,0:T(4,128)S(1)}, f32[256,512]{1,0:T(8,128)}, f32[2,2,24,512]{3,2,1,0:T(8,128)S(1)}, f32[2,256,512]{2,1,0:T(8,128)S(1)}) custom-call(f32[256,512]{1,0:T(8,128)S(1)} %get-tuple-element.34.u_ref.u_near, ...), custom_call_target="tpu_custom_call", output_to_operand_aliasing={{0}: (2, {}), {1}: (3, {})} | custom-call | tf_op jit(solution)/shard_map/solve_first/pallas_call | solution.py:424
  3.1 1.7 %collective-permute-start = (f32[4,512]{1,0:T(4,128)S(1)}, f32[4,512]{1,0:T(4,128)S(1)}, u32[]{:S(2)}, u32[]{:S(2)}) collective-permute-start(f32[4,512]{1,0:T(4,128)S(1)} %get-tuple-element.38), channel_id=1, source_target_pairs={{0,4},{4,8},{8,12},{12,16},{16,20},{20,24},{24,28},{28,0},{1,5},{5... | collective-permute-start | bytes 24584 | tf_op jit(solution)/shard_map/ppermute | solution.py:496
  4.9 0.7 %collective-permute-start.2 = (f32[4,512]{1,0:T(4,128)S(1)}, f32[4,512]{1,0:T(4,128)S(1)}, u32[]{:S(2)}, u32[]{:S(2)}) collective-permute-start(f32[4,512]{1,0:T(4,128)S(1)} %get-tuple-element.49), channel_id=1, source_target_pairs={{0,3},{1,2},{2,1},{3,0},{4,5},{5,4},{6,7},{7,6},{8,9},{9,8},{10,11... | collective-permute-start | bytes 24584 | tf_op jit(solution)/shard_map/ppermute | solution.py:497
  5.5 2.5 %collective-permute-start.1 = (f32[4,512]{1,0:T(4,128)S(1)}, f32[4,512]{1,0:T(4,128)S(1)}, u32[]{:S(2)}, u32[]{:S(2)}) collective-permute-start(f32[4,512]{1,0:T(4,128)S(1)} %get-tuple-element.42), channel_id=1, source_target_pairs={{0,28},{4,0},{8,4},{12,8},{16,12},{20,16},{24,20},{28,24},{1,29},{... | collective-permute-start | bytes 24584 | tf_op jit(solution)/shard_map/ppermute | solution.py:498
  8.1 0.1 %collective-permute-start.3 = (f32[4,512]{1,0:T(4,128)S(1)}, f32[4,512]{1,0:T(4,128)S(1)}, u32[]{:S(2)}, u32[]{:S(2)}) collective-permute-start(f32[4,512]{1,0:T(4,128)S(1)} %get-tuple-element.50), channel_id=1, source_target_pairs={{0,1},{1,0},{2,3},{3,2},{4,7},{5,6},{6,5},{7,4},{8,11},{9,10},{10,... | collective-permute-start | bytes 24584 | tf_op jit(solution)/shard_map/ppermute | solution.py:499
  8.2 1.0 %interior.1 = (f32[2,2,24,512]{3,2,1,0:T(8,128)S(1)}, f32[256,512]{1,0:T(8,128)}, f32[256,512]{1,0:T(8,128)}, f32[2,2,256,128]{3,2,1,0:T(8,128)S(1)}, f32[2,256,256]{2,1,0:T(8,128)S(1)}) custom-call(f32[256,512]{1,0:T(8,128)S(1)} %get-tuple-element.34.u_ref.u_near, ...), custom_call_target="tpu_custom_call", output_to_operand_aliasing={{1}: (2, {})} | custom-call | flops 536870912 | bytes 2621440 | tf_op jit(solution)/shard_map/interior/pallas_call | solution.py:439
  9.2 0.0 collective-permute-done.2.from_y_first
  9.2 0.1 collective-permute-done.3.from_y_second
  9.3 0.3 %sides.1 = (f32[256,512]{1,0:T(8,128)S(1)}, f32[256,512]{1,0:T(8,128)S(1)}) custom-call(f32[4,512]{1,0:T(4,128)S(1)} %collective-permute-done.2.from_y_first, f32[4,512]{1,0:T(4,128)S(1)} %collective-permute-done.3.from_y_second, f32[8,256]{1,0:T(8,128)S(1)} %get-tuple-element.51.near_low, f32[8,256]{1,0:T(8,128)S(1)} %get-tuple-element.52.near_high, ...), custom_call_target="tpu_custom_call" | custom-call | tf_op jit(solution)/shard_map/sides/pallas_call | solution.py:455
  9.6 0.0 collective-permute-done.from_low_x
  9.6 0.0 collective-permute-done.1.from_high_x
  9.6 1.1 %finish.1 = (f32[256,512]{1,0:T(8,128)}, f32[256,512]{1,0:T(8,128)}, f32[256,512]{1,0:T(8,128)}, f32[256,512]{1,0:T(8,128)}) custom-call(f32[4,512]{1,0:T(4,128)S(1)} %collective-permute-done.from_low_x, f32[4,512]{1,0:T(4,128)S(1)} %collective-permute-done.1.from_high_x, ...), custom_call_target="tpu_custom_call", output_to_operand_aliasing={{0}: (7, {}), {1}: (8, {})} | custom-call | tf_op jit(solution)/shard_map/finish/pallas_call | solution.py:467
  (1 shorter events, 0.0 us)
Async XLA Ops:
  3.1 6.4 %collective-permute-start = (f32[4,512]{1,0:T(4,128)S(1)}, f32[4,512]{1,0:T(4,128)S(1)}, u32[]{:S(2)}, u32[]{:S(2)}) collective-permute-start(f32[4,512]{1,0:T(4,128)S(1)} %get-tuple-element.38), channel_id=1, source_target_pairs={{0,4},{4,8},{8,12},{12,16},{16,20},{20,24},{24,28},{28,0},{1,5},{5... | collective-permute-start | bytes 24584 | tf_op jit(solution)/shard_map/ppermute | solution.py:496
  4.9 4.3 %collective-permute-start.2 = (f32[4,512]{1,0:T(4,128)S(1)}, f32[4,512]{1,0:T(4,128)S(1)}, u32[]{:S(2)}, u32[]{:S(2)}) collective-permute-start(f32[4,512]{1,0:T(4,128)S(1)} %get-tuple-element.49), channel_id=1, source_target_pairs={{0,3},{1,2},{2,1},{3,0},{4,5},{5,4},{6,7},{7,6},{8,9},{9,8},{10,11... | collective-permute-start | bytes 24584 | tf_op jit(solution)/shard_map/ppermute | solution.py:497
  5.5 4.0 %collective-permute-start.1 = (f32[4,512]{1,0:T(4,128)S(1)}, f32[4,512]{1,0:T(4,128)S(1)}, u32[]{:S(2)}, u32[]{:S(2)}) collective-permute-start(f32[4,512]{1,0:T(4,128)S(1)} %get-tuple-element.42), channel_id=1, source_target_pairs={{0,28},{4,0},{8,4},{12,8},{16,12},{20,16},{24,20},{28,24},{1,29},{... | collective-permute-start | bytes 24584 | tf_op jit(solution)/shard_map/ppermute | solution.py:498
  8.1 1.2 %collective-permute-start.3 = (f32[4,512]{1,0:T(4,128)S(1)}, f32[4,512]{1,0:T(4,128)S(1)}, u32[]{:S(2)}, u32[]{:S(2)}) collective-permute-start(f32[4,512]{1,0:T(4,128)S(1)} %get-tuple-element.50), channel_id=1, source_target_pairs={{0,1},{1,0},{2,3},{3,2},{4,7},{5,6},{6,5},{7,4},{8,11},{9,10},{10,... | collective-permute-start | bytes 24584 | tf_op jit(solution)/shard_map/ppermute | solution.py:499
